TPU v7x, 512 devices: a whole 4x8x8 slice. The times are simulated.
512 devices in a mesh: dp: 64 (over y, z), mp: 8 (over x, core).
Axes of the slice: x: 4, y: 8, z: 8, core: 2. Of those that a mesh axis runs over, the one named last changes fastest.
Arguments:
- hidden: bfloat16 [32768, 8192], P('dp', 'mp'), may hold values from -6 to 6
- queries: bfloat16 [32768, 4096], P('dp', 'mp'), may hold values from -6 to 6
- keys: bfloat16 [32768, 512], P('dp'), may hold values from -6 to 6
- upstream: bfloat16 [32768, 4096], P('dp', 'mp'), may hold values from -6 to 6
- value_matrix: bfloat16 [8192, 512], P(('mp', 'dp')), may hold values from -0.0625 to 0.0625
- lengths: int32 [64, 64], replicated, may hold values from 1 to 8, 256 in all within a row
- plan: int32 [64, 64], replicated, may hold values from 0 to 63, each once within a row
- correct: int32 [64, 64], P('dp'), may hold values 0 or 1
- problem: int32 [64, 64], P('dp'), may hold values from 0 to 63, as said below
Outputs:
- context: bfloat16 [16384, 4096], P('dp', 'mp')
- grad_weight: float32 [8192, 512], P(('mp', 'dp'))
Inputs may be any that keep to these rules, and one draw needn't show every extreme that they name: `lengths`: each row b sums to 256; some entry equals 8. `plan`: each row is a permutation: every slot of a rollout device goes to exactly one bin. Every problem id occurs exactly 64 times.
All inputs are finite; a program needn't handle non-finite values. No bound on the sum of `correct` on one device may be relied on, other than what follows from the above.
Results may differ from a plain program's by a relative error of at most 0.02.
Values may be sent and summed in bfloat16 or wider, within the bound.
No kernel may reach another device: no remote copies, remote signals or barrier semaphores. Data moves between devices by JAX's collectives and lax.ppermute only.
A program may use at most 64 MiB of HBM per device.

v0:
```python
import math

import jax
import jax.numpy as jnp
from jax import lax
from jax.sharding import PartitionSpec as P

LOCAL_QUERY_HEADS = 32
LOCAL_KEY_HEADS = 4
HEAD_WIDTH = 128
LMAX = 8
GROUP = 64
KPASS = 8


def pass_rate(total, hits):
    missed = jnp.ones_like(hits)
    for step in range(KPASS):
        missed = missed * jnp.maximum(total - hits - step, 0.0) / (total - step)
    return 1.0 - missed


def advantages(all_ok, all_ids):
    flat_ok = all_ok.reshape(-1).astype(jnp.float32)
    flat_id = all_ids.reshape(-1)
    problems = flat_id.shape[0] // GROUP
    member = (flat_id[None, :] == jnp.arange(problems, dtype=jnp.int32)[:, None]).astype(
        jnp.float32
    )
    counts = jnp.dot(member, flat_ok, precision=lax.Precision.HIGHEST)
    own = jnp.dot(counts, member, precision=lax.Precision.HIGHEST)
    gain = pass_rate(float(GROUP), own) - pass_rate(float(GROUP - 1), own - flat_ok)
    return gain.reshape(all_ok.shape)


def bin_layout(lengths, me, rows_bin):
    own = lax.dynamic_index_in_dim(lengths, me, 0, keepdims=False)
    ends = jnp.cumsum(own)
    starts = ends - own
    token_rows = jnp.arange(rows_bin, dtype=jnp.int32)
    slot = jnp.sum((token_rows[:, None] >= ends[None, :]).astype(jnp.int32), axis=1)
    match = slot[:, None] == jnp.arange(own.shape[0], dtype=jnp.int32)[None, :]
    place = token_rows - jnp.sum(jnp.where(match, starts[None, :], 0), axis=1)
    return (own, starts, slot, place, match)


def outgoing(array, plan_row):
    blocks = array.reshape(plan_row.shape[0], LMAX, array.shape[1])
    return jnp.take(blocks, plan_row, axis=0)


def packed(received, recv_index):
    return jnp.take(received.reshape(-1, received.shape[2]), recv_index, axis=0)


def project(token_rows, value_matrix):
    partial_sum = jnp.dot(
        token_rows,
        lax.all_gather(value_matrix, "dp", axis=0, tiled=True),
        preferred_element_type=jnp.float32,
    )
    return lax.psum(partial_sum.astype(jnp.bfloat16), "mp")


def attend(query_bin, full_key_rows, full_value_rows, grad_bin, slot, place, row_gain, part):
    token_rows = query_bin.shape[0]
    heads_dev = query_bin.shape[1] // HEAD_WIDTH
    head_groups = LOCAL_QUERY_HEADS // LOCAL_KEY_HEADS
    first = part * heads_dev
    chosen_rows = (first + jnp.arange(heads_dev, dtype=jnp.int32)) // head_groups
    selection_matrix = chosen_rows[:, None] == jnp.arange(LOCAL_KEY_HEADS, dtype=jnp.int32)[None, :]
    key_heads = jnp.einsum(
        "rkd,hk->rhd",
        full_key_rows.reshape(token_rows, LOCAL_KEY_HEADS, HEAD_WIDTH),
        selection_matrix.astype(jnp.bfloat16),
        preferred_element_type=jnp.float32,
    ).astype(jnp.bfloat16)
    value_heads = jnp.einsum(
        "rkd,hk->rhd",
        full_value_rows.reshape(token_rows, LOCAL_KEY_HEADS, HEAD_WIDTH),
        selection_matrix.astype(jnp.bfloat16),
        preferred_element_type=jnp.float32,
    ).astype(jnp.bfloat16)
    query_heads = query_bin.reshape(token_rows, heads_dev, HEAD_WIDTH)
    scores = jnp.einsum(
        "qhd,khd->hqk", query_heads, key_heads, preferred_element_type=jnp.float32
    ) * (1.0 / math.sqrt(HEAD_WIDTH))
    allowed = (slot[:, None] == slot[None, :]) & (place[None, :] <= place[:, None])
    scores = jnp.where(allowed[None], scores, -jnp.inf)
    top = jnp.max(scores, axis=2, keepdims=True)
    expo = jnp.exp(scores - top)
    probs = (expo / jnp.sum(expo, axis=2, keepdims=True)).astype(jnp.bfloat16)
    context = jnp.einsum(
        "hqk,khd->qhd", probs, value_heads, preferred_element_type=jnp.float32
    ).astype(jnp.bfloat16)
    grad_ctx = (
        (row_gain[:, None] * grad_bin.astype(jnp.float32))
        .astype(jnp.bfloat16)
        .reshape(token_rows, heads_dev, HEAD_WIDTH)
    )
    head_gradient = jnp.einsum("hqk,qhd->khd", probs, grad_ctx, preferred_element_type=jnp.float32)
    group_gradient = jnp.einsum("khd,hg->kgd", head_gradient, selection_matrix.astype(jnp.float32))
    value_gradient = lax.psum(
        group_gradient.reshape(token_rows, LOCAL_KEY_HEADS * HEAD_WIDTH).astype(jnp.bfloat16), "mp"
    )
    return (context.reshape(token_rows, heads_dev * HEAD_WIDTH), value_gradient)


def per_device(hidden, queries, keys, upstream, value_matrix, lengths, plan, correct, problem):
    me = lax.axis_index("dp")
    part = lax.axis_index("mp")
    slots = lengths.shape[0]
    samples = correct.shape[1]
    rows_bin = slots * LMAX // 2
    all_ok, all_ids = (
        lax.all_gather(correct, "dp", axis=0, tiled=True),
        lax.all_gather(problem, "dp", axis=0, tiled=True),
    )
    gain_table = advantages(all_ok, all_ids)
    plan_row = lax.dynamic_index_in_dim(plan, me, 0, keepdims=False)
    arriving = lax.dynamic_index_in_dim(plan, me, 1, keepdims=False)
    pick_sample = arriving[:, None] == jnp.arange(samples, dtype=jnp.int32)[None, :]
    slot_gain = jnp.sum(jnp.where(pick_sample, gain_table, 0.0), axis=1)
    own, starts, slot, place, match = bin_layout(lengths, me, rows_bin)
    row_gain = jnp.sum(jnp.where(match, slot_gain[None, :], 0.0), axis=1)
    recv_index = slot * LMAX + place
    x_in, query_in, key_in, grad_in = (
        lax.all_to_all(outgoing(hidden, plan_row), "dp", split_axis=0, concat_axis=0, tiled=True),
        lax.all_to_all(outgoing(queries, plan_row), "dp", split_axis=0, concat_axis=0, tiled=True),
        lax.all_to_all(outgoing(keys, plan_row), "dp", split_axis=0, concat_axis=0, tiled=True),
        lax.all_to_all(outgoing(upstream, plan_row), "dp", split_axis=0, concat_axis=0, tiled=True),
    )
    x_bin = packed(x_in, recv_index)
    query_bin = packed(query_in, recv_index)
    grad_bin = packed(grad_in, recv_index)
    full_key_rows = packed(key_in, recv_index)
    full_value_rows = project(x_bin, value_matrix)
    context, value_gradient = attend(
        query_bin, full_key_rows, full_value_rows, grad_bin, slot, place, row_gain, part
    )
    grad_weight = lax.psum_scatter(
        lax.dot_general(
            x_bin, value_gradient, (((0,), (0,)), ((), ())), preferred_element_type=jnp.float32
        ),
        "dp",
        scatter_dimension=0,
        tiled=True,
    )
    return (context, grad_weight)


def solution(mesh):
    in_specs = (
        P("dp", "mp"),
        P("dp", "mp"),
        P("dp", None),
        P("dp", "mp"),
        P(("mp", "dp"), None),
        P(),
        P(),
        P("dp", None),
        P("dp", None),
    )
    out_specs = (P("dp", "mp"), P(("mp", "dp"), None))
    return jax.shard_map(
        per_device, mesh=mesh, in_specs=in_specs, out_specs=out_specs, check_vma=False
    )
```

profile of v0, /device:TPU:2, one launch (start us, length us, event | category | flops | bytes accessed | tf_op | source)
XLA Modules:
  0.0 528.1 jit_solution(7163441437614584850)
XLA Ops:
  7.2 0.8 compare_and_fusion.1
  8.0 1.6 gather_fusion.4
  9.7 1.6 gather_fusion.6
  11.3 0.6 gather_fusion.2
  12.0 1.4 broadcast_select_fusion.2
  13.4 16.6 %all-to-all-start.3 = ((bf16[64,8,512]{2,1,0:T(8,128)(2,1)}), bf16[64,8,512]{2,1,0:T(8,128)(2,1)S(1)}, u32[]{:S(2)}, u32[]{:S(2)}) async-start(bf16[64,8,512]{2,1,0:T(8,128)(2,1)} %get-tuple-element.21), calls=%async_computation.3 | async-start | bytes 1048576 | tf_op jit(solution)/shard_map/all_to_all | solution.py:131
  30.0 0.0 all-gather.4.cloned.1.call-start
  30.0 0.7 all-gather.4.cloned.1.call-update
  30.7 0.7 fusion.27
  31.4 0.1 copy.30
  31.5 0.1 reduce-window.4
  31.6 0.1 reduce
  31.7 50.7 %all-gather.1 = s32[64,1,64]{2,1,0:T(1,128)S(1)} all-gather(s32[1,1,64]{2,1,0:T(1,128)S(1)} %bitcast.99), channel_id=1, replica_groups=mesh['dp'=64,'mp'=8] {'dp'}, dimensions={0}, use_global_device_ids=true | all-gather | bytes 16640 | tf_op jit(solution)/shard_map/all_gather | solution.py:116
  82.4 0.1 convert_reduce_fusion.1
  82.5 0.7 fusion.20
  83.2 6.4 %all-to-all-start.2 = ((bf16[64,8,512]{2,1,0:T(8,128)(2,1)}), bf16[64,8,512]{2,1,0:T(8,128)(2,1)S(1)}, u32[]{:S(2)}, u32[]{:S(2)}) async-start(bf16[64,8,512]{2,1,0:T(8,128)(2,1)} %get-tuple-element.20), calls=%async_computation.2 | async-start | bytes 1048576 | tf_op jit(solution)/shard_map/all_to_all | solution.py:130
  89.6 0.1 reshape.338
  89.7 48.1 %all-gather = s32[64,1,64]{2,1,0:T(1,128)S(1)} all-gather(s32[1,1,64]{2,1,0:T(1,128)S(1)} %bitcast.100), channel_id=1, replica_groups=mesh['dp'=64,'mp'=8] {'dp'}, dimensions={0}, use_global_device_ids=true | all-gather | bytes 16640 | tf_op jit(solution)/shard_map/all_gather | solution.py:117
  137.8 0.5 broadcast.288
  138.3 0.7 reduce.13
  139.0 0.1 eq.86
  139.1 0.1 convert_element_type.62
  139.2 1.6 gather_fusion
  140.8 0.1 convert_reduce_fusion
  140.9 0.1 select_reduce_fusion.1
  141.1 10.6 %all-to-all-start.1 = ((bf16[64,8,512]{2,1,0:T(8,128)(2,1)}), bf16[64,8,512]{2,1,0:T(8,128)(2,1)S(1)}, u32[]{:S(2)}, u32[]{:S(2)}) async-start(bf16[64,8,512]{2,1,0:T(8,128)(2,1)} %get-tuple-element.22), calls=%async_computation.1 | async-start | bytes 1048576 | tf_op jit(solution)/shard_map/all_to_all | solution.py:129
  151.7 0.6 convolution_bitcast_fusion.1
  152.3 0.4 fusion.6
  152.8 2.4 broadcast_select_fusion
  155.2 15.6 %all-to-all-done.1 = bf16[64,8,512]{2,1,0:T(8,128)(2,1)S(1)} async-done(((bf16[64,8,512]{2,1,0:T(8,128)(2,1)}), bf16[64,8,512]{2,1,0:T(8,128)(2,1)S(1)}, u32[]{:S(2)}, u32[]{:S(2)}) %all-to-all-start.1) | async-done | bytes 524320 | tf_op jit(solution)/shard_map/all_to_all | solution.py:129
  170.9 0.8 copy-done.1
  171.7 11.3 %all-to-all-start = ((bf16[64,8,1024]{2,1,0:T(8,128)(2,1)}), bf16[64,8,1024]{2,1,0:T(8,128)(2,1)S(1)}, u32[]{:S(2)}, u32[]{:S(2)}) async-start(bf16[64,8,1024]{2,1,0:T(8,128)(2,1)} %broadcast_select_fusion), calls=%async_computation | async-start | bytes 2097152 | tf_op jit(solution)/shard_map/all_to_all | solution.py:128
  183.0 0.0 all-reduce.3.cloned.1.call-start
  183.1 0.1 reshape.243
  183.1 0.2 dynamic-slice_reduce_fusion
  183.3 0.2 select_reduce_fusion.2
  183.5 0.1 select_reduce_fusion
  183.6 0.1 compare_and_fusion
  183.7 1.2 gather_fusion.7
  184.9 0.8 multiply_convert_fusion
  185.8 1.8 copy.47
  187.5 1.2 gather_fusion.5
  188.7 1.2 gather_fusion.3
  189.9 0.1 broadcast_select_fusion.5
  190.0 0.1 reshape.241
  190.1 0.3 fusion.5
  190.4 0.5 fusion.50
  190.9 1.7 convolution_bitcast_fusion
  192.6 0.2 copy.39
  192.8 0.3 convolution_convert_fusion
  193.1 0.7 copy.87
  193.8 9.0 %all-to-all-done = bf16[64,8,1024]{2,1,0:T(8,128)(2,1)S(1)} async-done(((bf16[64,8,1024]{2,1,0:T(8,128)(2,1)}), bf16[64,8,1024]{2,1,0:T(8,128)(2,1)S(1)}, u32[]{:S(2)}, u32[]{:S(2)}) %all-to-all-start) | async-done | bytes 1048608 | tf_op jit(solution)/shard_map/all_to_all | solution.py:128
  202.8 1.2 gather_fusion.1
  204.0 0.0 all-gather.4.cloned.1.call-done
  204.0 1.7 convolution_convert_fusion.2
  205.7 0.8 reshape.235
  206.5 0.0 all-reduce.3.cloned.1.call-update
  206.5 0.0 reduce-scatter.2.cloned.1.call-start
  206.6 63.9 %all-reduce.3.cloned.1.call-done = (bf16[256,4,128]{2,1,0:T(4,128)(2,1)}, bf16[256,512]{1,0:T(8,128)(2,1)}) async-done(((bf16[256,4,128]{2,1,0:T(4,128)(2,1)}, bf16[256,512]{1,0:T(8,128)(2,1)}), (bf16[256,4,128]{2,1,0:T(4,128)(2,1)}, bf16[256,512]{1,0:T(8,128)(2,1)})) %all-reduce.3.cloned.1.call-update) | async-done | bytes 524304 | tf_op jit(solution)/shard_map/psum | solution.py:62
  270.4 2.9 fusion.13
  273.4 0.3 fusion.4
  273.7 0.7 convolution_convert_fusion.1
  274.5 0.8 copy.40
  275.3 246.3 %reduce-scatter.2.cloned.1.call-done = f32[16,512]{1,0:T(8,128)} async-done(((f32[1024,512]{1,0:T(8,128)}), f32[16,512]{1,0:T(8,128)}) %reduce-scatter.2.cloned.1.call-update) | async-done | bytes 32784 | tf_op jit(solution)/shard_map/reduce_scatter | solution.py:141
  (36 shorter events, 0.2 us)
Async XLA Ops:
  7.2 132.0 %copy-start = (bf16[512,1024]{1,0:T(8,128)(2,1)S(1)}, bf16[512,1024]{1,0:T(8,128)(2,1)}, u32[]{:S(2)}) copy-start(bf16[512,1024]{1,0:T(8,128)(2,1)} %param.13) | copy-start | bytes 3145732
  7.2 4.1 copy-start.3
  11.9 19.8 %copy-start.9 = (s32[1,64]{1,0:T(1,128)S(1)}, s32[1,64]{1,0:T(1,128)}, u32[]{:S(2)}) copy-start(s32[1,64]{1,0:T(1,128)} %param.20) | copy-start | bytes 772
  11.9 70.4 %copy-start.8 = (s32[64,64]{1,0:T(8,128)S(1)}, s32[64,64]{1,0:T(8,128)}, u32[]{:S(2)}) copy-start(s32[64,64]{1,0:T(8,128)} %param.19) | copy-start | bytes 49156
  11.9 77.7 %copy-start.10 = (s32[1,64]{1,0:T(1,128)S(1)}, s32[1,64]{1,0:T(1,128)}, u32[]{:S(2)}) copy-start(s32[1,64]{1,0:T(1,128)} %param.21) | copy-start | bytes 772
  13.4 69.8 %all-to-all-start.3 = ((bf16[64,8,512]{2,1,0:T(8,128)(2,1)}), bf16[64,8,512]{2,1,0:T(8,128)(2,1)S(1)}, u32[]{:S(2)}, u32[]{:S(2)}) async-start(bf16[64,8,512]{2,1,0:T(8,128)(2,1)} %get-tuple-element.21), calls=%async_computation.3 | async-start | bytes 1048576 | tf_op jit(solution)/shard_map/all_to_all | solution.py:131
  30.0 174.1 %all-gather.4.cloned.1.call-start = ((), (), s32[]{:S(2)}) async-start(), calls=%async_computation.5 | async-start | bytes 1064960 | tf_op jit(solution)/shard_map/all_gather | solution.py:59
  83.2 57.9 %all-to-all-start.2 = ((bf16[64,8,512]{2,1,0:T(8,128)(2,1)}), bf16[64,8,512]{2,1,0:T(8,128)(2,1)S(1)}, u32[]{:S(2)}, u32[]{:S(2)}) async-start(bf16[64,8,512]{2,1,0:T(8,128)(2,1)} %get-tuple-element.20), calls=%async_computation.2 | async-start | bytes 1048576 | tf_op jit(solution)/shard_map/all_to_all | solution.py:130
  141.1 29.8 %all-to-all-start.1 = ((bf16[64,8,512]{2,1,0:T(8,128)(2,1)}), bf16[64,8,512]{2,1,0:T(8,128)(2,1)S(1)}, u32[]{:S(2)}, u32[]{:S(2)}) async-start(bf16[64,8,512]{2,1,0:T(8,128)(2,1)} %get-tuple-element.22), calls=%async_computation.1 | async-start | bytes 1048576 | tf_op jit(solution)/shard_map/all_to_all | solution.py:129
  170.9 0.8 copy-start.1
  171.7 31.2 %all-to-all-start = ((bf16[64,8,1024]{2,1,0:T(8,128)(2,1)}), bf16[64,8,1024]{2,1,0:T(8,128)(2,1)S(1)}, u32[]{:S(2)}, u32[]{:S(2)}) async-start(bf16[64,8,1024]{2,1,0:T(8,128)(2,1)} %broadcast_select_fusion), calls=%async_computation | async-start | bytes 2097152 | tf_op jit(solution)/shard_map/all_to_all | solution.py:128
  183.0 87.4 %all-reduce.3.cloned.1.call-start = ((), (), s32[]{:S(2)}) async-start(), calls=%async_computation.7 | async-start | bytes 1048576 | tf_op jit(solution)/shard_map/psum | solution.py:62
  184.9 3.8 copy-start.2
  189.9 1.1 copy-start.5
  190.0 0.9 copy-start.6
  206.5 315.1 %reduce-scatter.2.cloned.1.call-start = ((), (), s32[]{:S(2)}) async-start(), calls=%async_computation.6 | async-start | bytes 2129920 | tf_op jit(solution)/shard_map/reduce_scatter | solution.py:141
  270.4 2.9 copy-start.4
  270.4 3.3 copy-start.7
Sparse Core Ops, SparseCore 0:
  33.8 84.6 all-gather.3
  206.6 63.7 all-reduce.2
  275.6 245.9 reduce-scatter.1
where the time goes:
time: 529 us; the launch traced here: 528 us
  waiting for transfers between devices  336 us (64%)
  blocking collectives  98.8 us (19%)
  starting transfers between devices  45 us (9%)
  local copies, waits for them, and re-layouts  17.2 us (3%)
  between operations  14.1 us (3%)
  matrix products  9.46 us (2%)
  other arithmetic  8.06 us (2%)
    reduce_scatter x1, waiting for transfers between devices, per_device(): lax.psum_scatter(lax.dot_general(x_bin, value_gradient, (((0,), (0,)), ((...  246 us
    psum x1, waiting for transfers between devices, project(): return lax.psum(partial_sum.astype(jnp.bfloat16), 'mp')  63.9 us
    all_gather x1, blocking collectives, per_device(): lax.all_gather(correct, 'dp', axis=0, tiled=True)  50.7 us
    all_gather x1, blocking collectives, per_device(): lax.all_gather(problem, 'dp', axis=0, tiled=True)  48.1 us
    all_to_all x1, starting transfers between devices, per_device(): lax.all_to_all(outgoing(upstream, plan_row), 'dp', split_axis=0, concat_a...  16.6 us
    all_to_all x1, waiting for transfers between devices, per_device(): lax.all_to_all(outgoing(queries, plan_row), 'dp', split_axis=0, concat_ax...  15.6 us
    all_to_all x1, starting transfers between devices, per_device(): lax.all_to_all(outgoing(hidden, plan_row), 'dp', split_axis=0, concat_axi...  11.3 us
    all_to_all x1, starting transfers between devices, per_device(): lax.all_to_all(outgoing(queries, plan_row), 'dp', split_axis=0, concat_ax...  10.6 us
  transfers between devices with their start and end apart: 7, of which 4 were waited for; matrix products, arithmetic and copies ran while one was open for 4% of the time, Pallas kernels for 0%

commit v1 on v0

v1 whole, which is shorter than its diff:
```python
import math

import jax
import jax.numpy as jnp
from jax import lax
from jax.experimental import pallas as pl
from jax.experimental.pallas import tpu as pltpu
from jax.sharding import PartitionSpec as P

KEY_HEADS = 4
HEAD = 128
HEADS_DEV = 4
LMAX = 8
GROUP = 64
KPASS = 8
BINS = 64
ROWS = 512
PACKED = 256
FEATS = 1024
WROWS = 16
BLOCK = KEY_HEADS * WROWS
EXTRA = 8
TILE = 128

f32 = jnp.float32
bf16 = jnp.bfloat16
VM = pl.BlockSpec(memory_space=pltpu.VMEM)
SM = pl.BlockSpec(memory_space=pltpu.SMEM)
PARAMS = pltpu.CompilerParams(vmem_limit_bytes=40 * 1024 * 1024)


def iota(shape, dim):
    return lax.broadcasted_iota(jnp.int32, shape, dim)


def dot(a, b, dims=((1,), (0,))):
    return lax.dot_general(a, b, (dims, ((), ())), preferred_element_type=f32)


def call(body, out_shape, args, specs, flops=0, moved=0):
    return pl.pallas_call(
        body,
        out_shape=out_shape,
        in_specs=specs,
        out_specs=jax.tree.map(lambda _: VM, out_shape),
        compiler_params=PARAMS,
        cost_estimate=pl.CostEstimate(flops=flops, bytes_accessed=moved, transcendentals=0),
    )(*args)


def weight_block(wm_ref, ok_ref, id_ref, out_ref):
    member = (id_ref[...] == iota((128, BINS), 0) % BINS).astype(f32).astype(bf16)
    ok = jnp.broadcast_to(ok_ref[...], (EXTRA, BINS)).astype(f32).astype(bf16)
    hits = dot(ok, member, ((1,), (1,))).astype(bf16)
    for m in range(KEY_HEADS):
        out_ref[:, m * WROWS : (m + 1) * WROWS, :] = jnp.broadcast_to(
            wm_ref[:, m * HEAD : (m + 1) * HEAD][None], (BINS, WROWS, HEAD)
        )
    out_ref[:, BLOCK:, :] = jnp.broadcast_to(hits[None], (BINS, EXTRA, HEAD))


def attend(
    where_ref, x_ref, q_ref, k_ref, g_ref, len_ref, plan_ref, ok_ref, id_ref,
    xb_ref, xt_ref, dv_ref, pr_ref, pick_ref,
):
    me, xpos = where_ref[0], where_ref[1]
    sample = (iota((ROWS, BINS), 0) // LMAX == iota((ROWS, BINS), 1)).astype(f32).astype(bf16)
    mine = iota((ROWS, BINS), 1) == me
    lens = dot(sample, len_ref[...].astype(f32).astype(bf16))
    lens = jnp.sum(jnp.where(mine, lens, 0.0), axis=1, keepdims=True)
    slot = dot(sample, plan_ref[...].astype(f32).astype(bf16), ((1,), (1,)))
    slot = jnp.sum(jnp.where(mine, slot, 0.0), axis=1, keepdims=True)
    slot = slot.astype(jnp.int32)
    source = slot == iota((ROWS, BINS), 1)
    prob_id = jnp.sum(jnp.where(source, id_ref[...], 0).astype(f32), axis=1, keepdims=True)
    good = jnp.sum(jnp.where(source, ok_ref[...], 0).astype(f32), axis=1, keepdims=True)
    lane = (prob_id + BINS * good).astype(jnp.int32)
    pick_ref[...] = (lane == iota((ROWS, 128), 1)).astype(f32)
    row_source = slot * LMAX + iota((ROWS, 1), 0) % LMAX
    order = (row_source == iota((ROWS, ROWS), 1)).astype(f32).astype(bf16)
    valid = (iota((ROWS, 1), 0) % LMAX).astype(f32) < lens
    queries = dot(order, q_ref[...]).astype(bf16)
    cotangents = dot(order, g_ref[...]).astype(bf16)
    keys = dot(order, k_ref[:, pl.ds(pl.multiple_of(xpos * HEAD, HEAD), HEAD)]).astype(bf16)
    r, c = iota((TILE, TILE), 0), iota((TILE, TILE), 1)
    allowed = (r // LMAX == c // LMAX) & (c <= r)
    allowed = jnp.concatenate([allowed] * HEADS_DEV, axis=0)
    for tile in range(ROWS // TILE):
        rows = slice(tile * TILE, (tile + 1) * TILE)
        stack = lambda a: jnp.concatenate(
            [a[rows, h * HEAD : (h + 1) * HEAD] for h in range(HEADS_DEV)], axis=0
        )
        scores = dot(stack(queries), keys[rows], ((1,), (1,))) * (1.0 / math.sqrt(HEAD))
        scores = jnp.where(allowed, scores, -jnp.inf)
        expo = jnp.exp(scores - jnp.max(scores, axis=1, keepdims=True))
        probs = expo / jnp.sum(expo, axis=1, keepdims=True)
        alive = jnp.concatenate([valid[rows]] * HEADS_DEV, axis=0)
        probs = jnp.where(alive, probs, 0.0).astype(bf16)
        dv_ref[rows, :] = dot(probs, stack(cotangents), ((0,), (0,))).astype(bf16)
        short = jnp.zeros((TILE, HEAD), f32)
        for h in range(HEADS_DEV):
            to = (c == h * LMAX + r % LMAX).astype(f32).astype(bf16)
            short += dot(probs[h * TILE : (h + 1) * TILE], to)
        pr_ref[rows, :] = short.astype(bf16)
    x_bins = dot(order, x_ref[...]).astype(bf16)
    xb_ref[...] = x_bins
    xt_ref[...] = x_bins.T


def pass_rate(total, hits):
    missed = jnp.ones_like(hits)
    for step in range(KPASS):
        missed = missed * jnp.maximum(total - hits - step, 0.0) / (total - step)
    return 1.0 - missed


def weight_gradient(where_ref, w_ref, xt_ref, d0_ref, d1_ref, d2_ref, d3_ref, pick_ref, pr_ref, out_ref):
    xpos = where_ref[1]
    hits = jnp.sum(w_ref[:, BLOCK:, :].astype(f32), axis=0)[:1]
    good = (iota((1, 128), 1) // BINS).astype(f32)
    table = pass_rate(float(GROUP), hits) - pass_rate(float(GROUP - 1), hits - good)
    gain = jnp.sum(pick_ref[...] * table, axis=1, keepdims=True)
    dv = jnp.concatenate(
        [(gain * d[...].astype(f32)).astype(bf16) for d in (d0_ref, d1_ref, d2_ref, d3_ref)], axis=1
    )
    grad = dot(xt_ref[...], dv).astype(bf16)
    for i in range(KEY_HEADS):
        m = lax.rem(xpos + KEY_HEADS - i, KEY_HEADS)
        out_ref[:, pl.ds(pl.multiple_of(m * WROWS, WROWS), WROWS), :] = grad[
            :, i * HEAD : (i + 1) * HEAD
        ].reshape(BINS, WROWS, HEAD)
    out_ref[:, BLOCK:, :] = pr_ref[...].reshape(BINS, LMAX, HEAD)


def project(where_ref, w_ref, xb_ref, out_ref):
    xpos = where_ref[1]
    for i in range(KEY_HEADS):
        m = lax.rem(xpos + i, KEY_HEADS)
        w = w_ref[:, pl.ds(pl.multiple_of(m * WROWS, WROWS), WROWS), :].reshape(FEATS, HEAD)
        out_ref[i] = dot(xb_ref[...], w).astype(bf16)


def collect(where_ref, got_ref, len_ref, grad_ref, mix_ref):
    me = where_ref[0]
    total = jnp.sum(got_ref[:, :BLOCK, :].astype(f32), axis=0)
    for m in range(KEY_HEADS):
        grad_ref[:, m * HEAD : (m + 1) * HEAD] = total[m * WROWS : (m + 1) * WROWS]
    probs = got_ref[:, BLOCK:, :].reshape(ROWS, HEAD)
    own = jnp.where(iota((BINS, BINS), 0) == me, len_ref[...], 0).astype(f32)
    own = jnp.broadcast_to(jnp.sum(own, axis=0, keepdims=True), (8, BINS)).astype(bf16)
    s, lane = iota((BINS, ROWS), 0), iota((BINS, ROWS), 1)
    start = dot(own, (s < lane // LMAX).astype(f32).astype(bf16))[:1].astype(jnp.int32)
    size = dot(own, (s == lane // LMAX).astype(f32).astype(bf16))[:1].astype(jnp.int32)
    i, lane = iota((PACKED, ROWS), 0), iota((PACKED, ROWS), 1)
    same = (i >= start) & (i < start + size)
    take = same & (i == start + lane % LMAX)
    packed = dot(take.astype(f32).astype(bf16), probs).astype(bf16)
    a, b = iota((HEAD, ROWS), 0), iota((HEAD, ROWS), 1)
    for h in range(HEADS_DEV):
        spread = dot(packed, (a == h * LMAX + b % LMAX).astype(f32).astype(bf16))
        mix_ref[h * PACKED : (h + 1) * PACKED, :] = jnp.where(same, spread, 0.0).astype(bf16)


def mix(mix_ref, v_ref, out_ref):
    context = dot(mix_ref[...], v_ref[...]).astype(bf16)
    for h in range(HEADS_DEV):
        out_ref[:, h * HEAD : (h + 1) * HEAD] = context[h * PACKED : (h + 1) * PACKED]


def swap_cores(a):
    return lax.ppermute(a, "mp", [(p, p ^ 1) for p in range(8)])


def shift_x(a, step):
    return lax.ppermute(a, "mp", [(p, (p + 2 * step) % 8) for p in range(8)])


def all_to_all(a):
    return lax.all_to_all(a, "dp", split_axis=0, concat_axis=0, tiled=True)


def per_device(hidden, queries, keys, upstream, value_matrix, lengths, plan, correct, problem):
    where = jnp.stack([lax.axis_index("dp"), lax.axis_index("mp") // 2]).astype(jnp.int32)
    struct = jax.ShapeDtypeStruct
    block = struct((BINS, BLOCK + EXTRA, HEAD), bf16)
    sent = call(weight_block, block, (value_matrix, correct, problem), [VM] * 3, 10**6, 10**6)
    weights = all_to_all(sent)
    x_bins, x_turned, dv, probs, pick = call(
        attend,
        (
            struct((ROWS, FEATS), bf16),
            struct((FEATS, ROWS), bf16),
            struct((ROWS, HEAD), bf16),
            struct((ROWS, HEAD), bf16),
            struct((ROWS, 128), f32),
        ),
        (where, hidden, queries, keys, upstream, lengths, plan, correct, problem),
        [SM] + [VM] * 8,
        2 * 10**9,
        5 * 10**6,
    )
    dv = (dv.astype(f32) + swap_cores(dv).astype(f32)).astype(bf16)
    others = [shift_x(dv, step) for step in (1, 2, 3)]
    grads = call(
        weight_gradient,
        block,
        (where, weights, x_turned, dv, *others, pick, probs),
        [SM] + [VM] * 8,
        6 * 10**8,
        4 * 10**6,
    )
    got = all_to_all(grads)
    part = call(
        project,
        struct((KEY_HEADS, ROWS, HEAD), bf16),
        (where, weights, x_bins),
        [SM] + [VM] * 2,
        6 * 10**8,
        3 * 10**6,
    )
    both = part.astype(f32) + swap_cores(part).astype(f32)
    value = both[0]
    for step in (1, 2, 3):
        value = value + shift_x(both[step].astype(bf16), step).astype(f32)
    arrived = all_to_all(value.astype(bf16).reshape(BINS, LMAX, HEAD))
    grad_weight, matrix = call(
        collect,
        (struct((WROWS, KEY_HEADS * HEAD), f32), struct((HEADS_DEV * PACKED, ROWS), bf16)),
        (where, got, lengths),
        [SM] + [VM] * 2,
        6 * 10**8,
        3 * 10**6,
    )
    context = call(
        mix,
        struct((PACKED, HEADS_DEV * HEAD), bf16),
        (matrix, arrived.reshape(ROWS, HEAD)),
        [VM] * 2,
        3 * 10**8,
        2 * 10**6,
    )
    return context, grad_weight


def solution(mesh):
    in_specs = (
        P("dp", "mp"),
        P("dp", "mp"),
        P("dp", None),
        P("dp", "mp"),
        P(("mp", "dp"), None),
        P(),
        P(),
        P("dp", None),
        P("dp", None),
    )
    out_specs = (P("dp", "mp"), P(("mp", "dp"), None))
    return jax.shard_map(
        per_device, mesh=mesh, in_specs=in_specs, out_specs=out_specs, check_vma=False
    )
```

time: 529 us -> 121 us (0.23)
  waiting for transfers between devices: 336 us -> 36.5 us
  blocking collectives: 98.8 us -> 0 us
  between operations: 14.1 us -> 0.86 us
  Pallas kernels: 0 us -> 13.2 us
  starting transfers between devices: 45 us -> 56.2 us
  matrix products: 9.46 us -> 0 us
  other arithmetic: 8.06 us -> 0.97 us
    reduce_scatter x1 -> x0, waiting for transfers between devices: 246 us -> none  [per_device(): lax.psum_scatter(lax.dot_general(x_bin, value_gradient, (((0,), (0,)), ((...]
    all_gather x2 -> x0, blocking collectives: 98.8 us -> none  [the longest x1 50.7 us: per_device(): lax.all_gather(correct, 'dp', axis=0, tiled=True)]
    psum x1 -> x0, waiting for transfers between devices: 63.9 us -> none  [project(): return lax.psum(partial_sum.astype(jnp.bfloat16), 'mp')]
    ppermute x0 -> x8, starting transfers between devices: none -> 24.7 us  [the longest x6 20.9 us: shift_x(): return lax.ppermute(a, 'mp', [(p, (p + 2 * step) % 8) for p in range(8)])]
    all_to_all x4 -> x3, starting transfers between devices: 44.9 us -> 31.5 us  [all_to_all(): return lax.all_to_all(a, 'dp', split_axis=0, concat_axis=0, tiled=True)]
    pallas_call x0 -> x6, Pallas kernels: none -> 13.2 us  [call(): pl.pallas_call(body, out_shape=out_shape, in_specs=specs, out_specs=jax.t...]
    gather x8 -> x0, local copies, waits for them, and re-layouts: 10.1 us -> none  [the longest x4 5.52 us: outgoing(): return jnp.take(blocks, plan_row, axis=0)]
    ppermute x0 -> x8, waiting for transfers between devices: none -> 9.75 us  [the longest x6 6.56 us: shift_x(): return lax.ppermute(a, 'mp', [(p, (p + 2 * step) % 8) for p in range(8)])]
  transfers between devices with their start and end apart: 7 -> 11, of which waited for: 4 -> 9; matrix products, arithmetic and copies ran while one was open for 4% -> 1% of each run, Pallas kernels for 0% -> 7%
where the time goes in v1:
time: 121 us; the launch traced here: 120 us
  starting transfers between devices  56.2 us (46%)
  waiting for transfers between devices  36.5 us (30%)
  Pallas kernels  13.2 us (11%)
  local copies, waits for them, and re-layouts  12 us (10%)
    all_to_all x3, starting transfers between devices, all_to_all(): return lax.all_to_all(a, 'dp', split_axis=0, concat_axis=0, tiled=True)  31.5 us
    all_to_all x3, waiting for transfers between devices, all_to_all(): return lax.all_to_all(a, 'dp', split_axis=0, concat_axis=0, tiled=True)  26.7 us
    ppermute x6, starting transfers between devices, shift_x(): return lax.ppermute(a, 'mp', [(p, (p + 2 * step) % 8) for p in range(8)])  20.9 us
    pallas_call x6, Pallas kernels, call(): pl.pallas_call(body, out_shape=out_shape, in_specs=specs, out_specs=jax.t...  13.2 us
    unnamed x40, local copies, waits for them, and re-layouts  12 us
    ppermute x6, waiting for transfers between devices, shift_x(): return lax.ppermute(a, 'mp', [(p, (p + 2 * step) % 8) for p in range(8)])  6.56 us
    ppermute x2, starting transfers between devices, swap_cores(): return lax.ppermute(a, 'mp', [(p, p ^ 1) for p in range(8)])  3.84 us
    ppermute x2, waiting for transfers between devices, swap_cores(): return lax.ppermute(a, 'mp', [(p, p ^ 1) for p in range(8)])  3.19 us
  transfers between devices with their start and end apart: 11, of which 9 were waited for; matrix products, arithmetic and copies ran while one was open for 1% of the time, Pallas kernels for 7%

profile of v1, /device:TPU:2, one launch (start us, length us, event | category | flops | bytes accessed | tf_op | source)
XLA Modules:
  0.0 119.7 jit_solution(17077301930720313420)
XLA Ops:
  0.6 0.0 copy-start.8
  0.6 0.7 copy-done.8
  1.3 0.0 copy-start.9
  1.4 0.7 copy-done.9
  2.0 0.0 copy-start.11
  2.0 0.7 copy-done.11
  2.7 1.2 %shard_map.104 = bf16[64,72,128]{2,1,0:T(8,128)(2,1)} custom-call(bf16[16,512]{1,0:T(8,128)(2,1)S(1)} %copy-done.8, s32[1,64]{1,0:T(1,128)S(1)} %copy-done.9, s32[1,64]{1,0:T(1,128)S(1)} %copy-done.11), custom_call_target="tpu_custom_call" | custom-call | flops 1000000 | bytes 1000000 | tf_op jit(solution)/shard_map/pallas_call | solution.py:41
  3.9 0.0 copy-start.10
  3.9 0.0 copy-start.12
  3.9 0.0 copy-start.17
  3.9 0.0 copy-start.18
  3.9 16.7 %all-to-all-start = ((bf16[64,72,128]{2,1,0:T(8,128)(2,1)}), bf16[64,72,128]{2,1,0:T(8,128)(2,1)S(1)}, u32[]{:S(2)}, u32[]{:S(2)}) async-start(bf16[64,72,128]{2,1,0:T(8,128)(2,1)} %shard_map.104), calls=%async_computation | async-start | bytes 2359296 | tf_op jit(solution)/shard_map/all_to_all | solution.py:179
  20.6 0.1 pad_add_fusion.where_ref
  20.7 0.0 copy-done.10
  20.7 0.0 copy-done.12
  20.7 0.0 copy-done.17
  20.7 0.0 copy-done.18
  20.7 0.0 copy-start.13
  20.7 1.2 %copy-done.13 = bf16[512,1024]{1,0:T(8,128)(2,1)S(1)} copy-done((bf16[512,1024]{1,0:T(8,128)(2,1)S(1)}, bf16[512,1024]{1,0:T(8,128)(2,1)}, u32[]{:S(2)}) %copy-start.13) | copy-done | bytes 1048600
  21.9 0.0 copy-start.14
  22.0 1.0 copy-done.14
  23.0 0.0 copy-start.15
  23.0 1.0 copy-done.15
  24.0 1.0 copy-done.16
  25.1 4.5 %shard_map.105 = (bf16[512,1024]{1,0:T(8,128)(2,1)S(1)}, bf16[1024,512]{1,0:T(8,128)(2,1)S(1)}, bf16[512,128]{1,0:T(8,128)(2,1)S(1)}, bf16[512,128]{1,0:T(8,128)(2,1)S(1)}, f32[512,128]{1,0:T(8,128)S(1)}) custom-call(s32[2]{0:T(128)S(1)} %pad_add_fusion.where_ref, bf16[512,1024]{1,0:T(8,128)(2,1)S(1)} %copy-done.13, bf16[512,512]{1,0:T(8,128)(2,1)S(1)} %copy-done.14, ...), custom_call_target="tpu_custom_call" | custom-call | flops 2000000000 | bytes 5000000 | tf_op jit(solution)/shard_map/pallas_call | solution.py:41
  29.6 0.0 copy-start
  29.6 1.9 %collective-permute-start = (bf16[512,128]{1,0:T(8,128)(2,1)S(1)}, bf16[512,128]{1,0:T(8,128)(2,1)S(1)}, u32[]{:S(2)}, u32[]{:S(2)}) collective-permute-start(bf16[512,128]{1,0:T(8,128)(2,1)S(1)} %get-tuple-element.10), channel_id=1, source_target_pairs={{0,1},{1,0},{2,3},{3,2},{4,5},{5,4},{6,7},{7,6},{8,9},{9,8},{10,11... | collective-permute-start | bytes 393224 | tf_op jit(solution)/shard_map/ppermute | solution.py:171
  31.5 1.3 %collective-permute-done = bf16[512,128]{1,0:T(8,128)(2,1)S(1)} collective-permute-done((bf16[512,128]{1,0:T(8,128)(2,1)S(1)}, bf16[512,128]{1,0:T(8,128)(2,1)S(1)}, u32[]{:S(2)}, u32[]{:S(2)}) %collective-permute-start) | collective-permute-done | bytes 131104 | tf_op jit(solution)/shard_map/ppermute | solution.py:171
  32.9 3.4 %collective-permute-start.1 = (bf16[512,128]{1,0:T(8,128)(2,1)S(1)}, bf16[512,128]{1,0:T(8,128)(2,1)S(1)}, u32[]{:S(2)}, u32[]{:S(2)}) collective-permute-start(bf16[512,128]{1,0:T(8,128)(2,1)S(1)} %add_convert_fusion.d0_ref), channel_id=1, source_target_pairs={{0,2},{1,3},{2,4},{3,5},{4,6},{5,7},{6,0},{7,1},{8,10},{9,11},{10,... | collective-permute-start | bytes 393224 | tf_op jit(solution)/shard_map/ppermute | solution.py:175
  36.3 3.0 %collective-permute-start.2 = (bf16[512,128]{1,0:T(8,128)(2,1)S(1)}, bf16[512,128]{1,0:T(8,128)(2,1)S(1)}, u32[]{:S(2)}, u32[]{:S(2)}) collective-permute-start(bf16[512,128]{1,0:T(8,128)(2,1)S(1)} %add_convert_fusion.d0_ref), channel_id=1, source_target_pairs={{0,4},{1,5},{2,6},{3,7},{4,0},{5,1},{6,2},{7,3},{8,12},{9,13},{10,... | collective-permute-start | bytes 393224 | tf_op jit(solution)/shard_map/ppermute | solution.py:175
  39.3 4.1 %collective-permute-start.3 = (bf16[512,128]{1,0:T(8,128)(2,1)S(1)}, bf16[512,128]{1,0:T(8,128)(2,1)S(1)}, u32[]{:S(2)}, u32[]{:S(2)}) collective-permute-start(bf16[512,128]{1,0:T(8,128)(2,1)S(1)} %add_convert_fusion.d0_ref), channel_id=1, source_target_pairs={{0,6},{1,7},{2,0},{3,1},{4,2},{5,3},{6,4},{7,5},{8,14},{9,15},{10,... | collective-permute-start | bytes 393224 | tf_op jit(solution)/shard_map/ppermute | solution.py:175
  43.4 0.0 collective-permute-done.1.d1_ref
  43.4 0.0 copy-start.2
  43.4 0.6 copy-done.2
  44.0 1.8 %collective-permute-done.2.d2_ref = bf16[512,128]{1,0:T(8,128)(2,1)S(1)} collective-permute-done((bf16[512,128]{1,0:T(8,128)(2,1)S(1)}, bf16[512,128]{1,0:T(8,128)(2,1)S(1)}, u32[]{:S(2)}, u32[]{:S(2)}) %collective-permute-start.2) | collective-permute-done | bytes 131104 | tf_op jit(solution)/shard_map/ppermute | solution.py:175
  45.9 0.0 copy-done
  45.9 0.7 copy-done.4
  46.5 1.2 %collective-permute-done.3.d3_ref = bf16[512,128]{1,0:T(8,128)(2,1)S(1)} collective-permute-done((bf16[512,128]{1,0:T(8,128)(2,1)S(1)}, bf16[512,128]{1,0:T(8,128)(2,1)S(1)}, u32[]{:S(2)}, u32[]{:S(2)}) %collective-permute-start.3) | collective-permute-done | bytes 131104 | tf_op jit(solution)/shard_map/ppermute | solution.py:175
  47.8 0.7 copy-done.6
  48.4 4.4 %all-to-all-done.w_ref = bf16[64,72,128]{2,1,0:T(8,128)(2,1)S(1)} async-done(((bf16[64,72,128]{2,1,0:T(8,128)(2,1)}), bf16[64,72,128]{2,1,0:T(8,128)(2,1)S(1)}, u32[]{:S(2)}, u32[]{:S(2)}) %all-to-all-start) | async-done | bytes 1179680 | tf_op jit(solution)/shard_map/all_to_all | solution.py:179
  52.9 0.9 copy-done.1
  53.8 0.9 copy-done.3
  54.7 0.9 copy-done.5
  55.6 0.9 copy-done.7
  56.5 2.5 %shard_map.106 = bf16[64,72,128]{2,1,0:T(8,128)(2,1)} custom-call(s32[2]{0:T(128)S(1)} %pad_add_fusion.where_ref, bf16[64,72,128]{2,1,0:T(8,128)(2,1)S(1)} %all-to-all-done.w_ref, bf16[1024,512]{1,0:T(8,128)(2,1)S(1)} %get-tuple-element.9.xt_ref, bf16[512,128]{1,0:T(8,128)(2,1)S(1)} %add_convert_fusion.d0_ref, bf16[512,128]{1,0:T(8,128)(2,1)S(1)} %copy-done.3, ...), custom_call_target="tpu_custom_call" | custom-call | flops 600000000 | bytes 4000000 | tf_op jit(solution)/shard_map/pallas_call | solution.py:41
  59.0 8.3 %all-to-all-start.1 = ((bf16[64,72,128]{2,1,0:T(8,128)(2,1)}), bf16[64,72,128]{2,1,0:T(8,128)(2,1)S(1)}, u32[]{:S(2)}, u32[]{:S(2)}) async-start(bf16[64,72,128]{2,1,0:T(8,128)(2,1)} %shard_map.106), calls=%async_computation.1 | async-start | bytes 2359296 | tf_op jit(solution)/shard_map/all_to_all | solution.py:179
  67.3 1.8 %shard_map.108 = bf16[4,512,128]{2,1,0:T(8,128)(2,1)S(1)} custom-call(s32[2]{0:T(128)S(1)} %pad_add_fusion.where_ref, bf16[64,72,128]{2,1,0:T(8,128)(2,1)S(1)} %all-to-all-done.w_ref, bf16[512,1024]{1,0:T(8,128)(2,1)S(1)} %get-tuple-element.14.xb_ref), custom_call_target="tpu_custom_call" | custom-call | flops 600000000 | bytes 3000000 | tf_op jit(solution)/shard_map/pallas_call | solution.py:41
  69.1 1.9 %collective-permute-start.4 = (bf16[4,512,128]{2,1,0:T(8,128)(2,1)S(1)}, bf16[4,512,128]{2,1,0:T(8,128)(2,1)S(1)}, u32[]{:S(2)}, u32[]{:S(2)}) collective-permute-start(bf16[4,512,128]{2,1,0:T(8,128)(2,1)S(1)} %shard_map.108), channel_id=1, source_target_pairs={{0,1},{1,0},{2,3},{3,2},{4,5},{5,4},{6,7},{7,6},{8,9},{9,8},{10,11... | collective-permute-start | bytes 1572872 | tf_op jit(solution)/shard_map/ppermute | solution.py:171
  71.0 1.9 %collective-permute-done.4 = bf16[4,512,128]{2,1,0:T(8,128)(2,1)S(1)} collective-permute-done((bf16[4,512,128]{2,1,0:T(8,128)(2,1)S(1)}, bf16[4,512,128]{2,1,0:T(8,128)(2,1)S(1)}, u32[]{:S(2)}, u32[]{:S(2)}) %collective-permute-start.4) | collective-permute-done | bytes 524320 | tf_op jit(solution)/shard_map/ppermute | solution.py:171
  72.9 0.1 convert_add_fusion
  73.0 0.0 copy-start.19
  73.1 2.5 %collective-permute-start.5 = (bf16[512,128]{1,0:T(8,128)(2,1)S(1)}, bf16[512,128]{1,0:T(8,128)(2,1)S(1)}, u32[]{:S(2)}, u32[]{:S(2)}) collective-permute-start(bf16[512,128]{1,0:T(8,128)(2,1)S(1)} %get-tuple-element.18), channel_id=1, source_target_pairs={{0,2},{1,3},{2,4},{3,5},{4,6},{5,7},{6,0},{7,1},{8,10},{9,11},{10,... | collective-permute-start | bytes 393224 | tf_op jit(solution)/shard_map/ppermute | solution.py:175
  75.6 4.0 %collective-permute-start.6 = (bf16[512,128]{1,0:T(8,128)(2,1)S(1)}, bf16[512,128]{1,0:T(8,128)(2,1)S(1)}, u32[]{:S(2)}, u32[]{:S(2)}) collective-permute-start(bf16[512,128]{1,0:T(8,128)(2,1)S(1)} %get-tuple-element.20), channel_id=1, source_target_pairs={{0,4},{1,5},{2,6},{3,7},{4,0},{5,1},{6,2},{7,3},{8,12},{9,13},{10,... | collective-permute-start | bytes 393224 | tf_op jit(solution)/shard_map/ppermute | solution.py:175
  79.6 3.9 %collective-permute-start.7 = (bf16[512,128]{1,0:T(8,128)(2,1)S(1)}, bf16[512,128]{1,0:T(8,128)(2,1)S(1)}, u32[]{:S(2)}, u32[]{:S(2)}) collective-permute-start(bf16[512,128]{1,0:T(8,128)(2,1)S(1)} %get-tuple-element.19), channel_id=1, source_target_pairs={{0,6},{1,7},{2,0},{3,1},{4,2},{5,3},{6,4},{7,5},{8,14},{9,15},{10,... | collective-permute-start | bytes 393224 | tf_op jit(solution)/shard_map/ppermute | solution.py:175
  83.5 0.0 collective-permute-done.5
  83.5 0.9 collective-permute-done.6
  84.5 2.5 %collective-permute-done.7 = bf16[512,128]{1,0:T(8,128)(2,1)S(1)} collective-permute-done((bf16[512,128]{1,0:T(8,128)(2,1)S(1)}, bf16[512,128]{1,0:T(8,128)(2,1)S(1)}, u32[]{:S(2)}, u32[]{:S(2)}) %collective-permute-start.7) | collective-permute-done | bytes 131104 | tf_op jit(solution)/shard_map/ppermute | solution.py:175
  87.0 0.7 fusion.4
  87.8 11.8 %all-to-all-done.1.got_ref = bf16[64,72,128]{2,1,0:T(8,128)(2,1)S(1)} async-done(((bf16[64,72,128]{2,1,0:T(8,128)(2,1)}), bf16[64,72,128]{2,1,0:T(8,128)(2,1)S(1)}, u32[]{:S(2)}, u32[]{:S(2)}) %all-to-all-start.1) | async-done | bytes 1179680 | tf_op jit(solution)/shard_map/all_to_all | solution.py:179
  99.5 6.5 %all-to-all-start.2 = ((bf16[64,8,128]{2,1,0:T(8,128)(2,1)}), bf16[64,8,128]{2,1,0:T(8,128)(2,1)S(1)}, u32[]{:S(2)}, u32[]{:S(2)}) async-start(bf16[64,8,128]{2,1,0:T(8,128)(2,1)} %fusion.4), calls=%async_computation.2 | async-start | bytes 262144 | tf_op jit(solution)/shard_map/all_to_all | solution.py:179
  106.0 0.0 copy-done.19
  106.0 2.1 %shard_map.107 = (f32[16,512]{1,0:T(8,128)}, bf16[1024,512]{1,0:T(8,128)(2,1)S(1)}) custom-call(s32[2]{0:T(128)S(1)} %pad_add_fusion.where_ref, bf16[64,72,128]{2,1,0:T(8,128)(2,1)S(1)} %all-to-all-done.1.got_ref, s32[64,64]{1,0:T(8,128)S(1)} %copy-done.19), custom_call_target="tpu_custom_call" | custom-call | flops 600000000 | bytes 3000000 | tf_op jit(solution)/shard_map/pallas_call | solution.py:41
  108.1 10.5 %all-to-all-done.2 = bf16[64,8,128]{2,1,0:T(8,128)(2,1)S(1)} async-done(((bf16[64,8,128]{2,1,0:T(8,128)(2,1)}), bf16[64,8,128]{2,1,0:T(8,128)(2,1)S(1)}, u32[]{:S(2)}, u32[]{:S(2)}) %all-to-all-start.2) | async-done | bytes 131104 | tf_op jit(solution)/shard_map/all_to_all | solution.py:179
  118.6 1.1 shard_map.109
  (9 shorter events, 0.1 us)
Async XLA Ops:
  0.6 0.7 copy-start.8
  1.3 0.7 copy-start.9
  2.0 0.7 copy-start.11
  3.9 16.8 %copy-start.10 = (s32[1,64]{1,0:T(1,128)S(1)}, s32[1,64]{1,0:T(1,128)}, u32[]{:S(2)}) copy-start(s32[1,64]{1,0:T(1,128)} %ok_ref.3) | copy-start | bytes 772
  3.9 16.8 %copy-start.12 = (s32[1,64]{1,0:T(1,128)S(1)}, s32[1,64]{1,0:T(1,128)}, u32[]{:S(2)}) copy-start(s32[1,64]{1,0:T(1,128)} %id_ref.3) | copy-start | bytes 772
  3.9 16.8 %copy-start.17 = (s32[64,64]{1,0:T(8,128)S(1)}, s32[64,64]{1,0:T(8,128)}, u32[]{:S(2)}) copy-start(s32[64,64]{1,0:T(8,128)} %plan_ref.1) | copy-start | bytes 49156
  3.9 16.8 %copy-start.18 = (s32[64,64]{1,0:T(8,128)S(1)}, s32[64,64]{1,0:T(8,128)}, u32[]{:S(2)}) copy-start(s32[64,64]{1,0:T(8,128)} %len_ref.3) | copy-start | bytes 49156
  3.9 49.0 %all-to-all-start = ((bf16[64,72,128]{2,1,0:T(8,128)(2,1)}), bf16[64,72,128]{2,1,0:T(8,128)(2,1)S(1)}, u32[]{:S(2)}, u32[]{:S(2)}) async-start(bf16[64,72,128]{2,1,0:T(8,128)(2,1)} %shard_map.104), calls=%async_computation | async-start | bytes 2359296 | tf_op jit(solution)/shard_map/all_to_all | solution.py:179
  20.7 1.2 %copy-start.13 = (bf16[512,1024]{1,0:T(8,128)(2,1)S(1)}, bf16[512,1024]{1,0:T(8,128)(2,1)}, u32[]{:S(2)}) copy-start(bf16[512,1024]{1,0:T(8,128)(2,1)} %x_ref.1) | copy-start | bytes 3145732
  21.9 1.0 copy-start.14
  23.0 1.0 copy-start.15
  24.0 1.0 copy-start.16
  29.6 16.3 %copy-start = (f32[512,128]{1,0:T(8,128)}, f32[512,128]{1,0:T(8,128)S(1)}, u32[]{:S(2)}) copy-start(f32[512,128]{1,0:T(8,128)S(1)} %get-tuple-element.11.pick_ref) | copy-start | bytes 786436
  29.6 3.2 %collective-permute-start = (bf16[512,128]{1,0:T(8,128)(2,1)S(1)}, bf16[512,128]{1,0:T(8,128)(2,1)S(1)}, u32[]{:S(2)}, u32[]{:S(2)}) collective-permute-start(bf16[512,128]{1,0:T(8,128)(2,1)S(1)} %get-tuple-element.10), channel_id=1, source_target_pairs={{0,1},{1,0},{2,3},{3,2},{4,5},{5,4},{6,7},{7,6},{8,9},{9,8},{10,11... | collective-permute-start | bytes 393224 | tf_op jit(solution)/shard_map/ppermute | solution.py:171
  32.9 10.5 %collective-permute-start.1 = (bf16[512,128]{1,0:T(8,128)(2,1)S(1)}, bf16[512,128]{1,0:T(8,128)(2,1)S(1)}, u32[]{:S(2)}, u32[]{:S(2)}) collective-permute-start(bf16[512,128]{1,0:T(8,128)(2,1)S(1)} %add_convert_fusion.d0_ref), channel_id=1, source_target_pairs={{0,2},{1,3},{2,4},{3,5},{4,6},{5,7},{6,0},{7,1},{8,10},{9,11},{10,... | collective-permute-start | bytes 393224 | tf_op jit(solution)/shard_map/ppermute | solution.py:175
  36.3 9.6 %collective-permute-start.2 = (bf16[512,128]{1,0:T(8,128)(2,1)S(1)}, bf16[512,128]{1,0:T(8,128)(2,1)S(1)}, u32[]{:S(2)}, u32[]{:S(2)}) collective-permute-start(bf16[512,128]{1,0:T(8,128)(2,1)S(1)} %add_convert_fusion.d0_ref), channel_id=1, source_target_pairs={{0,4},{1,5},{2,6},{3,7},{4,0},{5,1},{6,2},{7,3},{8,12},{9,13},{10,... | collective-permute-start | bytes 393224 | tf_op jit(solution)/shard_map/ppermute | solution.py:175
  39.3 8.5 %collective-permute-start.3 = (bf16[512,128]{1,0:T(8,128)(2,1)S(1)}, bf16[512,128]{1,0:T(8,128)(2,1)S(1)}, u32[]{:S(2)}, u32[]{:S(2)}) collective-permute-start(bf16[512,128]{1,0:T(8,128)(2,1)S(1)} %add_convert_fusion.d0_ref), channel_id=1, source_target_pairs={{0,6},{1,7},{2,0},{3,1},{4,2},{5,3},{6,4},{7,5},{8,14},{9,15},{10,... | collective-permute-start | bytes 393224 | tf_op jit(solution)/shard_map/ppermute | solution.py:175
  43.4 0.6 copy-start.2
  45.9 0.7 copy-start.4
  47.8 0.7 copy-start.6
  52.8 1.0 copy-start.1
  53.8 0.9 copy-start.3
  54.7 0.9 copy-start.5
  55.6 0.9 copy-start.7
  59.0 40.5 %all-to-all-start.1 = ((bf16[64,72,128]{2,1,0:T(8,128)(2,1)}), bf16[64,72,128]{2,1,0:T(8,128)(2,1)S(1)}, u32[]{:S(2)}, u32[]{:S(2)}) async-start(bf16[64,72,128]{2,1,0:T(8,128)(2,1)} %shard_map.106), calls=%async_computation.1 | async-start | bytes 2359296 | tf_op jit(solution)/shard_map/all_to_all | solution.py:179
  69.1 3.8 %collective-permute-start.4 = (bf16[4,512,128]{2,1,0:T(8,128)(2,1)S(1)}, bf16[4,512,128]{2,1,0:T(8,128)(2,1)S(1)}, u32[]{:S(2)}, u32[]{:S(2)}) collective-permute-start(bf16[4,512,128]{2,1,0:T(8,128)(2,1)S(1)} %shard_map.108), channel_id=1, source_target_pairs={{0,1},{1,0},{2,3},{3,2},{4,5},{5,4},{6,7},{7,6},{8,9},{9,8},{10,11... | collective-permute-start | bytes 1572872 | tf_op jit(solution)/shard_map/ppermute | solution.py:171
  73.0 33.0 %copy-start.19 = (s32[64,64]{1,0:T(8,128)S(1)}, s32[64,64]{1,0:T(8,128)}, u32[]{:S(2)}) copy-start(s32[64,64]{1,0:T(8,128)} %len_ref.3) | copy-start | bytes 49156
  73.1 10.4 %collective-permute-start.5 = (bf16[512,128]{1,0:T(8,128)(2,1)S(1)}, bf16[512,128]{1,0:T(8,128)(2,1)S(1)}, u32[]{:S(2)}, u32[]{:S(2)}) collective-permute-start(bf16[512,128]{1,0:T(8,128)(2,1)S(1)} %get-tuple-element.18), channel_id=1, source_target_pairs={{0,2},{1,3},{2,4},{3,5},{4,6},{5,7},{6,0},{7,1},{8,10},{9,11},{10,... | collective-permute-start | bytes 393224 | tf_op jit(solution)/shard_map/ppermute | solution.py:175
  75.6 8.9 %collective-permute-start.6 = (bf16[512,128]{1,0:T(8,128)(2,1)S(1)}, bf16[512,128]{1,0:T(8,128)(2,1)S(1)}, u32[]{:S(2)}, u32[]{:S(2)}) collective-permute-start(bf16[512,128]{1,0:T(8,128)(2,1)S(1)} %get-tuple-element.20), channel_id=1, source_target_pairs={{0,4},{1,5},{2,6},{3,7},{4,0},{5,1},{6,2},{7,3},{8,12},{9,13},{10,... | collective-permute-start | bytes 393224 | tf_op jit(solution)/shard_map/ppermute | solution.py:175
  79.6 7.4 %collective-permute-start.7 = (bf16[512,128]{1,0:T(8,128)(2,1)S(1)}, bf16[512,128]{1,0:T(8,128)(2,1)S(1)}, u32[]{:S(2)}, u32[]{:S(2)}) collective-permute-start(bf16[512,128]{1,0:T(8,128)(2,1)S(1)} %get-tuple-element.19), channel_id=1, source_target_pairs={{0,6},{1,7},{2,0},{3,1},{4,2},{5,3},{6,4},{7,5},{8,14},{9,15},{10,... | collective-permute-start | bytes 393224 | tf_op jit(solution)/shard_map/ppermute | solution.py:175
  99.5 19.1 %all-to-all-start.2 = ((bf16[64,8,128]{2,1,0:T(8,128)(2,1)}), bf16[64,8,128]{2,1,0:T(8,128)(2,1)S(1)}, u32[]{:S(2)}, u32[]{:S(2)}) async-start(bf16[64,8,128]{2,1,0:T(8,128)(2,1)} %fusion.4), calls=%async_computation.2 | async-start | bytes 262144 | tf_op jit(solution)/shard_map/all_to_all | solution.py:179

commit v2 on v1

v2 whole, which is shorter than its diff:
```python
import math

import jax
import jax.numpy as jnp
from jax import lax
from jax.experimental import pallas as pl
from jax.experimental.pallas import tpu as pltpu
from jax.sharding import PartitionSpec as P

KEY_HEADS = 4
HEAD = 128
HEADS_DEV = 4
LMAX = 8
GROUP = 64
KPASS = 8
BINS = 64
ROWS = 512
PACKED = 256
FEATS = 1024
WROWS = 16
BLOCK = KEY_HEADS * WROWS
EXTRA = 8
TILE = 128

f32 = jnp.float32
bf16 = jnp.bfloat16
VM = pl.BlockSpec(memory_space=pltpu.VMEM)
SM = pl.BlockSpec(memory_space=pltpu.SMEM)
HB = pl.BlockSpec(memory_space=pltpu.HBM)
MIB = 1024 * 1024
ATTEND_MIB = 60


def iota(shape, dim):
    return lax.broadcasted_iota(jnp.int32, shape, dim)


def dot(a, b, dims=((1,), (0,))):
    return lax.dot_general(a, b, (dims, ((), ())), preferred_element_type=f32)


def call(body, out_shape, args, specs, flops=0, moved=0, vmem=16, scratch=()):
    return pl.pallas_call(
        body,
        out_shape=out_shape,
        in_specs=specs,
        out_specs=jax.tree.map(lambda _: VM, out_shape),
        scratch_shapes=scratch,
        compiler_params=pltpu.CompilerParams(vmem_limit_bytes=vmem * MIB),
        cost_estimate=pl.CostEstimate(flops=flops, bytes_accessed=moved, transcendentals=0),
    )(*args)


def fetch(sources, targets, sems):
    copies = [pltpu.make_async_copy(s, t, sems.at[i]) for i, (s, t) in enumerate(zip(sources, targets))]
    for copy in copies:
        copy.start()
    return copies


def weight_block(wm_hbm, ok_hbm, id_hbm, out_ref, wm_ref, ok_ref, id_ref, sems):
    for copy in fetch((wm_hbm, ok_hbm, id_hbm), (wm_ref, ok_ref, id_ref), sems):
        copy.wait()
    member = (id_ref[...] == iota((128, BINS), 0) % BINS).astype(f32).astype(bf16)
    ok = jnp.broadcast_to(ok_ref[...], (EXTRA, BINS)).astype(f32).astype(bf16)
    hits = dot(ok, member, ((1,), (1,))).astype(bf16)
    for m in range(KEY_HEADS):
        out_ref[:, m * WROWS : (m + 1) * WROWS, :] = jnp.broadcast_to(
            wm_ref[:, m * HEAD : (m + 1) * HEAD][None], (BINS, WROWS, HEAD)
        )
    out_ref[:, BLOCK:, :] = jnp.broadcast_to(hits[None], (BINS, EXTRA, HEAD))


def slots(me, plan_ref):
    sample = (iota((ROWS, BINS), 0) // LMAX == iota((ROWS, BINS), 1)).astype(f32).astype(bf16)
    slot = dot(sample, plan_ref[...].astype(f32).astype(bf16), ((1,), (1,)))
    slot = jnp.sum(jnp.where(iota((ROWS, BINS), 1) == me, slot, 0.0), axis=1, keepdims=True)
    return sample, slot.astype(jnp.int32)


def reorder(slot):
    source = slot * LMAX + iota((ROWS, 1), 0) % LMAX
    return (source == iota((ROWS, ROWS), 1)).astype(f32).astype(bf16)


def attend(where_ref, q_hbm, k_hbm, g_hbm, len_ref, plan_ref, dv_ref, pr_ref, q_ref, k_ref, g_ref, sems):
    me, xpos = where_ref[0], where_ref[1]
    key_columns = k_hbm.at[:, pl.ds(pl.multiple_of(xpos * HEAD, HEAD), HEAD)]
    got_q, got_k, got_g = fetch((q_hbm, key_columns, g_hbm), (q_ref, k_ref, g_ref), sems)
    sample, slot = slots(me, plan_ref)
    lens = dot(sample, len_ref[...].astype(f32).astype(bf16))
    lens = jnp.sum(jnp.where(iota((ROWS, BINS), 1) == me, lens, 0.0), axis=1, keepdims=True)
    valid = (iota((ROWS, 1), 0) % LMAX).astype(f32) < lens
    order = reorder(slot)
    got_q.wait()
    queries = dot(order, q_ref[...]).astype(bf16)
    got_k.wait()
    keys = dot(order, k_ref[...]).astype(bf16)
    got_g.wait()
    cotangents = dot(order, g_ref[...]).astype(bf16)
    r, c = iota((TILE, TILE), 0), iota((TILE, TILE), 1)
    allowed = (r // LMAX == c // LMAX) & (c <= r)
    allowed = jnp.concatenate([allowed] * HEADS_DEV, axis=0)
    for tile in range(ROWS // TILE):
        rows = slice(tile * TILE, (tile + 1) * TILE)
        stack = lambda a: jnp.concatenate(
            [a[rows, h * HEAD : (h + 1) * HEAD] for h in range(HEADS_DEV)], axis=0
        )
        scores = dot(stack(queries), keys[rows], ((1,), (1,))) * (1.0 / math.sqrt(HEAD))
        scores = jnp.where(allowed, scores, -jnp.inf)
        expo = jnp.exp(scores - jnp.max(scores, axis=1, keepdims=True))
        probs = expo / jnp.sum(expo, axis=1, keepdims=True)
        alive = jnp.concatenate([valid[rows]] * HEADS_DEV, axis=0)
        probs = jnp.where(alive, probs, 0.0).astype(bf16)
        dv_ref[rows, :] = dot(probs, stack(cotangents), ((0,), (0,))).astype(bf16)
        short = jnp.zeros((TILE, HEAD), f32)
        for h in range(HEADS_DEV):
            to = (c == h * LMAX + r % LMAX).astype(f32).astype(bf16)
            short += dot(probs[h * TILE : (h + 1) * TILE], to)
        pr_ref[rows, :] = short.astype(bf16)


def put_in_order(where_ref, x_ref, plan_ref, ok_ref, id_ref, dv_ref, xb_ref, out_ref):
    _, slot = slots(where_ref[0], plan_ref)
    xb_ref[...] = dot(reorder(slot), x_ref[...]).astype(bf16)
    source = slot == iota((ROWS, BINS), 1)
    lane = jnp.where(source, id_ref[...] + BINS * ok_ref[...], 0).astype(f32)
    lane = jnp.sum(lane, axis=1, keepdims=True).astype(jnp.int32)
    for m in range(KEY_HEADS):
        out_ref[:, m * HEAD : (m + 1) * HEAD] = dv_ref[m]
    out_ref[:, KEY_HEADS * HEAD :] = (lane == iota((ROWS, HEAD), 1)).astype(f32).astype(bf16)


def pass_rate(total, hits):
    missed = jnp.ones_like(hits)
    for step in range(KPASS):
        missed = missed * jnp.maximum(total - hits - step, 0.0) / (total - step)
    return 1.0 - missed


def multiply(where_ref, w_ref, xb_ref, dv_ref, part_ref, grad_ref):
    xpos = where_ref[1]
    for i in range(KEY_HEADS):
        m = lax.rem(xpos + i, KEY_HEADS)
        w = w_ref[:, pl.ds(pl.multiple_of(m * WROWS, WROWS), WROWS), :].reshape(FEATS, HEAD)
        part_ref[i] = dot(xb_ref[...], w).astype(bf16)
    hits = jnp.sum(w_ref[:, BLOCK:, :].astype(f32), axis=0)[:1]
    good = (iota((1, 128), 1) // BINS).astype(f32)
    table = pass_rate(float(GROUP), hits) - pass_rate(float(GROUP - 1), hits - good)
    pick = dv_ref[:, KEY_HEADS * HEAD :].astype(f32)
    gain = jnp.sum(pick * table, axis=1, keepdims=True)
    dv = (gain * dv_ref[:, : KEY_HEADS * HEAD].astype(f32)).astype(bf16)
    grad = dot(xb_ref[...].T, dv).astype(bf16)
    for m in range(KEY_HEADS):
        grad_ref[m] = grad[:, m * HEAD : (m + 1) * HEAD]


def add_cores(where_ref, mine_ref, other_ref, own_ref, next_ref, far_ref):
    core = where_ref[2]
    half = pl.ds(pl.multiple_of(core * (ROWS // 2), ROWS // 2), ROWS // 2)
    own_ref[...] = mine_ref[0].astype(f32) + other_ref[0].astype(f32)
    to = 1 + 2 * core
    next_ref[...] = (mine_ref[to].astype(f32) + other_ref[to].astype(f32)).astype(bf16)
    far_ref[...] = (mine_ref[2, half].astype(f32) + other_ref[2, half].astype(f32)).astype(bf16)


def add_arrived(where_ref, next_ref, far_ref, out_ref):
    half = pl.ds(pl.multiple_of(where_ref[2] * (ROWS // 2), ROWS // 2), ROWS // 2)
    out_ref[...] = next_ref[...]
    out_ref[half] = (next_ref[half].astype(f32) + far_ref[...].astype(f32)).astype(bf16)


def assemble(own_ref, r1_ref, r2_ref, near_ref, pr_ref, out_ref):
    grad = jnp.sum(near_ref[...].astype(f32), axis=0).astype(bf16)
    out_ref[:, :WROWS, :] = grad.reshape(BINS, WROWS, HEAD)
    value = own_ref[...] + r1_ref[...].astype(f32) + r2_ref[...].astype(f32)
    out_ref[:, WROWS : WROWS + LMAX, :] = value.astype(bf16).reshape(BINS, LMAX, HEAD)
    out_ref[:, WROWS + LMAX :, :] = pr_ref[...].reshape(BINS, LMAX, HEAD)


def finish(where_ref, got_ref, len_ref, grad_ref, out_ref):
    me = where_ref[0]
    probs = got_ref[:, WROWS + LMAX :, :].reshape(ROWS, HEAD)
    values = got_ref[:, WROWS : WROWS + LMAX, :].reshape(ROWS, HEAD)
    own = jnp.where(iota((BINS, BINS), 0) == me, len_ref[...], 0).astype(f32)
    own = jnp.broadcast_to(jnp.sum(own, axis=0, keepdims=True), (8, BINS)).astype(bf16)
    s, lane = iota((BINS, ROWS), 0), iota((BINS, ROWS), 1)
    start = dot(own, (s < lane // LMAX).astype(f32).astype(bf16))[:1].astype(jnp.int32)
    size = dot(own, (s == lane // LMAX).astype(f32).astype(bf16))[:1].astype(jnp.int32)
    i, lane = iota((PACKED, ROWS), 0), iota((PACKED, ROWS), 1)
    same = (i >= start) & (i < start + size)
    take = same & (i == start + lane % LMAX)
    packed = dot(take.astype(f32).astype(bf16), probs).astype(bf16)
    a, b = iota((HEAD, ROWS), 0), iota((HEAD, ROWS), 1)
    for h in range(HEADS_DEV):
        spread = dot(packed, (a == h * LMAX + b % LMAX).astype(f32).astype(bf16))
        spread = jnp.where(same, spread, 0.0).astype(bf16)
        out_ref[:, h * HEAD : (h + 1) * HEAD] = dot(spread, values).astype(bf16)
    for m in range(KEY_HEADS):
        total = jnp.zeros((WROWS, HEAD), f32)
        for source in range(BINS):
            if square_place(source) == m:
                total += got_ref[source, :WROWS, :].astype(f32)
        grad_ref[:, m * HEAD : (m + 1) * HEAD] = total


def square_place(source):
    return source // 8 % 2 * 2 + source % 2


SQUARES = [
    [(y + i) * 8 + z + j for i in range(2) for j in range(2)]
    for y in range(0, 8, 2)
    for z in range(0, 8, 2)
]


def swap_cores(a):
    return lax.ppermute(a, "mp", [(p, p ^ 1) for p in range(8)])


def to_next_chips(a):
    return lax.ppermute(a, "mp", [(p, (p + (2, -2)[p % 2]) % 8) for p in range(8)])


def to_far_chip(a):
    return lax.ppermute(a, "mp", [(p, (p + 4) % 8) for p in range(8)])


def all_to_all(a, groups=None):
    return lax.all_to_all(
        a, "dp", split_axis=0, concat_axis=0, tiled=True, axis_index_groups=groups
    )


def per_device(hidden, queries, keys, upstream, value_matrix, lengths, plan, correct, problem):
    part_of_mp = lax.axis_index("mp")
    where = jnp.stack([lax.axis_index("dp"), part_of_mp // 2, part_of_mp % 2]).astype(jnp.int32)
    struct = jax.ShapeDtypeStruct
    rows = struct((ROWS, HEAD), bf16)
    sent = call(
        weight_block,
        struct((BINS, BLOCK + EXTRA, HEAD), bf16),
        (value_matrix, correct, problem),
        [HB] * 3,
        10**6,
        10**6,
        scratch=[
            pltpu.VMEM((WROWS, KEY_HEADS * HEAD), bf16),
            pltpu.VMEM((1, BINS), jnp.int32),
            pltpu.VMEM((1, BINS), jnp.int32),
            pltpu.SemaphoreType.DMA((3,)),
        ],
        vmem=60,
    )
    weights = all_to_all(sent)
    dv, probs = call(
        attend,
        (rows, rows),
        (where, queries, keys, upstream, lengths, plan),
        [SM] + [HB] * 3 + [VM] * 2,
        2 * 10**9,
        2 * 10**6,
        scratch=[
            pltpu.VMEM((ROWS, HEADS_DEV * HEAD), bf16),
            pltpu.VMEM((ROWS, HEAD), bf16),
            pltpu.VMEM((ROWS, HEADS_DEV * HEAD), bf16),
            pltpu.SemaphoreType.DMA((3,)),
        ],
        vmem=ATTEND_MIB,
    )
    dv = (dv.astype(f32) + swap_cores(dv).astype(f32)).astype(bf16)
    dv = lax.all_gather(dv, "mp", axis_index_groups=[[0, 2, 4, 6], [1, 3, 5, 7]])
    x_bins, packed = call(
        put_in_order,
        (struct((ROWS, FEATS), bf16), struct((ROWS, (KEY_HEADS + 1) * HEAD), bf16)),
        (where, hidden, plan, correct, problem, dv),
        [SM] + [VM] * 5,
        6 * 10**8,
        4 * 10**6,
    )
    part, grads = call(
        multiply,
        (struct((KEY_HEADS, ROWS, HEAD), bf16), struct((KEY_HEADS, FEATS, HEAD), bf16)),
        (where, weights, x_bins, packed),
        [SM] + [VM] * 3,
        10**9,
        6 * 10**6,
    )
    other_part = swap_cores(part)
    near = all_to_all(grads, SQUARES)
    own, following, far = call(
        add_cores,
        (struct((ROWS, HEAD), f32), rows, struct((ROWS // 2, HEAD), bf16)),
        (where, part, other_part),
        [SM] + [VM] * 2,
        10**6,
        2 * 10**6,
    )
    arrived = call(
        add_arrived,
        rows,
        (where, to_next_chips(following), to_far_chip(far)),
        [SM] + [VM] * 2,
        10**6,
        10**6,
    )
    block = call(
        assemble,
        struct((BINS, WROWS + 2 * LMAX, HEAD), bf16),
        (own, arrived, swap_cores(arrived), near, probs),
        [VM] * 5,
        10**6,
        3 * 10**6,
    )
    grad_weight, context = call(
        finish,
        (struct((WROWS, KEY_HEADS * HEAD), f32), struct((PACKED, HEADS_DEV * HEAD), bf16)),
        (where, all_to_all(block), lengths),
        [SM] + [VM] * 2,
        6 * 10**8,
        10**6,
    )
    return context, grad_weight


def solution(mesh):
    in_specs = (
        P("dp", "mp"),
        P("dp", "mp"),
        P("dp", None),
        P("dp", "mp"),
        P(("mp", "dp"), None),
        P(),
        P(),
        P("dp", None),
        P("dp", None),
    )
    out_specs = (P("dp", "mp"), P(("mp", "dp"), None))
    return jax.shard_map(
        per_device, mesh=mesh, in_specs=in_specs, out_specs=out_specs, check_vma=False
    )
```

time: 121 us -> 112 us (0.926)
  the two profiles are of different devices: /device:TPU:2 before, /device:TPU:16 now
where the time goes in v2:
time: 112 us; the launch traced here: 111 us
  blocking collectives  40.3 us (36%)
  starting transfers between devices  34 us (30%)
  Pallas kernels  16.6 us (15%)
  waiting for transfers between devices  13.7 us (12%)
  local copies, waits for them, and re-layouts  4.15 us (4%)
  other arithmetic  1.6 us (1%)
    all_to_all x1, blocking collectives, all_to_all(): lax.all_to_all(a, 'dp', split_axis=0, concat_axis=0, tiled=True, axis_ind...  27.2 us
    all_to_all x2, starting transfers between devices, all_to_all(): lax.all_to_all(a, 'dp', split_axis=0, concat_axis=0, tiled=True, axis_ind...  20 us
    pallas_call x8, Pallas kernels, call(): pl.pallas_call(body, out_shape=out_shape, in_specs=specs, out_specs=jax.t...  16.6 us
    all_gather x1, blocking collectives, per_device(): lax.all_gather(dv, 'mp', axis_index_groups=[[0, 2, 4, 6], [1, 3, 5, 7]])  13.1 us
    ppermute x3, starting transfers between devices, swap_cores(): return lax.ppermute(a, 'mp', [(p, p ^ 1) for p in range(8)])  6 us
    all_to_all x2, waiting for transfers between devices, all_to_all(): lax.all_to_all(a, 'dp', split_axis=0, concat_axis=0, tiled=True, axis_ind...  5.48 us
    ppermute x1, starting transfers between devices, to_far_chip(): return lax.ppermute(a, 'mp', [(p, (p + 4) % 8) for p in range(8)])  4.64 us
    ppermute x3, waiting for transfers between devices, swap_cores(): return lax.ppermute(a, 'mp', [(p, p ^ 1) for p in range(8)])  4.61 us
  transfers between devices with their start and end apart: 7, of which 5 were waited for; matrix products, arithmetic and copies ran while one was open for 1% of the time, Pallas kernels for 8%

profile of v2, /device:TPU:16, one launch (start us, length us, event | category | flops | bytes accessed | tf_op | source)
XLA Modules:
  0.0 111.2 jit_solution(26029728615920953)
XLA Ops:
  0.6 1.9 %shard_map.104 = bf16[64,72,128]{2,1,0:T(8,128)(2,1)} custom-call(bf16[16,512]{1,0:T(8,128)(2,1)} %wm_hbm.1, s32[1,64]{1,0:T(1,128)} %ok_ref.1, s32[1,64]{1,0:T(1,128)} %id_ref.1), custom_call_target="tpu_custom_call" | custom-call | flops 1000000 | bytes 1000000 | tf_op jit(solution)/shard_map/pallas_call | solution.py:43
  2.6 16.5 %all-to-all-start = ((bf16[64,72,128]{2,1,0:T(8,128)(2,1)}), bf16[64,72,128]{2,1,0:T(8,128)(2,1)S(1)}, u32[]{:S(2)}, u32[]{:S(2)}) async-start(bf16[64,72,128]{2,1,0:T(8,128)(2,1)} %shard_map.104), calls=%async_computation | async-start | bytes 2359296 | tf_op jit(solution)/shard_map/all_to_all | solution.py:231
  19.1 0.7 pad_add_fusion.where_ref
  19.8 0.0 copy-start.1
  19.8 0.0 copy-start.2
  19.8 0.0 copy-start.3
  19.8 0.0 copy-start.4
  19.8 0.0 copy-start.5
  19.8 5.9 %shard_map.105 = (bf16[512,128]{1,0:T(8,128)(2,1)}, bf16[512,128]{1,0:T(8,128)(2,1)}) custom-call(s32[3]{0:T(128)} %pad_add_fusion.where_ref, bf16[512,512]{1,0:T(8,128)(2,1)} %q_hbm.1, bf16[512,512]{1,0:T(8,128)(2,1)} %k_hbm.1, bf16[512,512]{1,0:T(8,128)(2,1)} %g_hbm.1, s32[64,64]{1,0:T(8,128)} %len_ref.3, s32[64,64]{1,0:T(8,128)} %plan_ref.3), custom_call_target="tpu_custom_call" | custom-call | flops 2000000000 | bytes 2000000 | tf_op jit(solution)/shard_map/pallas_call | solution.py:43
  25.7 1.9 %collective-permute-start = (bf16[512,128]{1,0:T(8,128)(2,1)}, bf16[512,128]{1,0:T(8,128)(2,1)S(1)}, u32[]{:S(2)}, u32[]{:S(2)}) collective-permute-start(bf16[512,128]{1,0:T(8,128)(2,1)} %get-tuple-element.13), channel_id=1, source_target_pairs={{0,1},{1,0},{2,3},{3,2},{4,5},{5,4},{6,7},{7,6},{8,9},{9,8},{10,11... | collective-permute-start | bytes 393224 | tf_op jit(solution)/shard_map/ppermute | solution.py:219
  27.6 1.5 %collective-permute-done = bf16[512,128]{1,0:T(8,128)(2,1)S(1)} collective-permute-done((bf16[512,128]{1,0:T(8,128)(2,1)}, bf16[512,128]{1,0:T(8,128)(2,1)S(1)}, u32[]{:S(2)}, u32[]{:S(2)}) %collective-permute-start) | collective-permute-done | bytes 131104 | tf_op jit(solution)/shard_map/ppermute | solution.py:219
  29.2 0.9 add_convert_fusion
  30.1 13.1 %all-gather = bf16[2048,128]{1,0:T(8,128)(2,1)S(1)} all-gather(bf16[512,128]{1,0:T(8,128)(2,1)S(1)} %add_convert_fusion), channel_id=2, replica_groups={{0,2,4,6},{1,3,5,7},{8,10,12,14},{9,11,13,15},{16,18,20,22},{17,19,21,2..., dimensions={0}, use_global_device_ids=true | all-gather | bytes 655360 | tf_op jit(solution)/shard_map/all_gather | solution.py:273
  43.3 0.0 copy-done.1
  43.3 0.0 copy-done.2
  43.3 0.0 copy-done.3
  43.3 0.0 copy-done.4
  43.3 0.0 copy-done.5
  43.3 1.5 %shard_map.106 = (bf16[512,1024]{1,0:T(8,128)(2,1)S(1)}, bf16[512,640]{1,0:T(8,128)(2,1)S(1)}) custom-call(s32[3]{0:T(128)S(1)} %copy-done.1, bf16[512,1024]{1,0:T(8,128)(2,1)S(1)} %copy-done.4, s32[64,64]{1,0:T(8,128)S(1)} %copy-done.5, s32[1,64]{1,0:T(1,128)S(1)} %copy-done.2, s32[1,64]{1,0:T(1,128)S(1)} %copy-done.3, bf16[4,512,128]{2,1,0:T(8,128)(2,1)S(1)} %bitcast.4), custom_call_target="tpu_custom_call" | custom-call | flops 600000000 | bytes 4000000 | tf_op jit(solution)/shard_map/pallas_call | solution.py:43
  44.8 0.0 copy-start.7
  44.8 1.0 copy-done.7
  45.8 0.0 copy-start.9
  45.8 0.8 copy-done.9
  46.6 5.5 %all-to-all-done.w_ref = bf16[64,72,128]{2,1,0:T(8,128)(2,1)S(1)} async-done(((bf16[64,72,128]{2,1,0:T(8,128)(2,1)}), bf16[64,72,128]{2,1,0:T(8,128)(2,1)S(1)}, u32[]{:S(2)}, u32[]{:S(2)}) %all-to-all-start) | async-done | bytes 1179680 | tf_op jit(solution)/shard_map/all_to_all | solution.py:231
  52.1 0.0 copy-start.8
  52.1 1.2 %copy-done.8 = bf16[512,1024]{1,0:T(8,128)(2,1)S(1)} copy-done((bf16[512,1024]{1,0:T(8,128)(2,1)S(1)}, bf16[512,1024]{1,0:T(8,128)(2,1)}, u32[]{:S(2)}) %copy-start.8) | copy-done | bytes 1048600
  53.3 0.0 copy-start.10
  53.3 1.1 copy-done.10
  54.4 3.4 %shard_map.107 = (bf16[4,512,128]{2,1,0:T(8,128)(2,1)S(1)}, bf16[4,1024,128]{2,1,0:T(8,128)(2,1)}) custom-call(s32[3]{0:T(128)S(1)} %copy-done.1, bf16[64,72,128]{2,1,0:T(8,128)(2,1)S(1)} %all-to-all-done.w_ref, bf16[512,1024]{1,0:T(8,128)(2,1)S(1)} %copy-done.8, bf16[512,640]{1,0:T(8,128)(2,1)S(1)} %copy-done.10), custom_call_target="tpu_custom_call" | custom-call | flops 1000000000 | bytes 6000000 | tf_op jit(solution)/shard_map/pallas_call | solution.py:43
  57.8 3.5 %all-to-all-start.1 = ((bf16[4,1024,128]{2,1,0:T(8,128)(2,1)}), bf16[4,1024,128]{2,1,0:T(8,128)(2,1)S(1)}, u32[]{:S(2)}, u32[]{:S(2)}) async-start(bf16[4,1024,128]{2,1,0:T(8,128)(2,1)} %get-tuple-element.20), calls=%async_computation.1 | async-start | bytes 2097152 | tf_op jit(solution)/shard_map/all_to_all | solution.py:231
  61.3 0.0 copy-start
  61.3 2.1 %collective-permute-start.1 = (bf16[4,512,128]{2,1,0:T(8,128)(2,1)S(1)}, bf16[4,512,128]{2,1,0:T(8,128)(2,1)S(1)}, u32[]{:S(2)}, u32[]{:S(2)}) collective-permute-start(bf16[4,512,128]{2,1,0:T(8,128)(2,1)S(1)} %get-tuple-element.16.mine_ref), channel_id=1, source_target_pairs={{0,1},{1,0},{2,3},{3,2},{4,5},{5,4},{6,7},{7,6},{8,9},{9,8},{10,11... | collective-permute-start | bytes 1572872 | tf_op jit(solution)/shard_map/ppermute | solution.py:219
  63.3 1.9 %collective-permute-done.1.other_ref = bf16[4,512,128]{2,1,0:T(8,128)(2,1)S(1)} collective-permute-done((bf16[4,512,128]{2,1,0:T(8,128)(2,1)S(1)}, bf16[4,512,128]{2,1,0:T(8,128)(2,1)S(1)}, u32[]{:S(2)}, u32[]{:S(2)}) %collective-permute-start.1) | collective-permute-done | bytes 524320 | tf_op jit(solution)/shard_map/ppermute | solution.py:219
  65.2 0.6 shard_map.108
  65.8 3.4 %collective-permute-start.2 = (bf16[512,128]{1,0:T(8,128)(2,1)S(1)}, bf16[512,128]{1,0:T(8,128)(2,1)S(1)}, u32[]{:S(2)}, u32[]{:S(2)}) collective-permute-start(bf16[512,128]{1,0:T(8,128)(2,1)S(1)} %get-tuple-element.18), channel_id=1, source_target_pairs={{0,2},{1,7},{2,4},{3,1},{4,6},{5,3},{6,0},{7,5},{8,10},{9,15},{10,... | collective-permute-start | bytes 393224 | tf_op jit(solution)/shard_map/ppermute | solution.py:223
  69.2 4.6 %collective-permute-start.3 = (bf16[256,128]{1,0:T(8,128)(2,1)S(1)}, bf16[256,128]{1,0:T(8,128)(2,1)S(1)}, u32[]{:S(2)}, u32[]{:S(2)}) collective-permute-start(bf16[256,128]{1,0:T(8,128)(2,1)S(1)} %get-tuple-element.19), channel_id=1, source_target_pairs={{0,4},{1,5},{2,6},{3,7},{4,0},{5,1},{6,2},{7,3},{8,12},{9,13},{10,... | collective-permute-start | bytes 196616 | tf_op jit(solution)/shard_map/ppermute | solution.py:227
  73.9 3.6 %collective-permute-done.3.far_ref = bf16[256,128]{1,0:T(8,128)(2,1)S(1)} collective-permute-done((bf16[256,128]{1,0:T(8,128)(2,1)S(1)}, bf16[256,128]{1,0:T(8,128)(2,1)S(1)}, u32[]{:S(2)}, u32[]{:S(2)}) %collective-permute-start.3) | collective-permute-done | bytes 65568 | tf_op jit(solution)/shard_map/ppermute | solution.py:227
  77.5 0.0 collective-permute-done.2.next_ref
  77.5 0.6 shard_map.109.r1_ref
  78.0 2.0 %collective-permute-start.4 = (bf16[512,128]{1,0:T(8,128)(2,1)S(1)}, bf16[512,128]{1,0:T(8,128)(2,1)S(1)}, u32[]{:S(2)}, u32[]{:S(2)}) collective-permute-start(bf16[512,128]{1,0:T(8,128)(2,1)S(1)} %shard_map.109.r1_ref), channel_id=1, source_target_pairs={{0,1},{1,0},{2,3},{3,2},{4,5},{5,4},{6,7},{7,6},{8,9},{9,8},{10,11... | collective-permute-start | bytes 393224 | tf_op jit(solution)/shard_map/ppermute | solution.py:219
  80.1 1.2 %collective-permute-done.4.r2_ref = bf16[512,128]{1,0:T(8,128)(2,1)S(1)} collective-permute-done((bf16[512,128]{1,0:T(8,128)(2,1)S(1)}, bf16[512,128]{1,0:T(8,128)(2,1)S(1)}, u32[]{:S(2)}, u32[]{:S(2)}) %collective-permute-start.4) | collective-permute-done | bytes 131104 | tf_op jit(solution)/shard_map/ppermute | solution.py:219
  81.3 0.0 all-to-all-done.1.near_ref
  81.3 0.0 copy-done
  81.3 0.0 copy-start.6
  81.3 0.2 shard_map.110
  81.5 27.2 %all_to_all.15.got_ref = bf16[64,32,128]{2,1,0:T(8,128)(2,1)S(1)} all-to-all(bf16[64,32,128]{2,1,0:T(8,128)(2,1)S(1)} %shard_map.110), channel_id=1, replica_groups=mesh['dp'=64,'mp'=8] {'dp'}, dimensions={0} | all-to-all | bytes 1048576 | tf_op jit(solution)/shard_map/all_to_all | solution.py:231
  108.7 0.0 copy-done.6
  108.7 2.5 %shard_map.111 = (f32[16,512]{1,0:T(8,128)}, bf16[256,512]{1,0:T(8,128)(2,1)}) custom-call(s32[3]{0:T(128)S(1)} %copy-done.1, bf16[64,32,128]{2,1,0:T(8,128)(2,1)S(1)} %all_to_all.15.got_ref, s32[64,64]{1,0:T(8,128)S(1)} %copy-done.6), custom_call_target="tpu_custom_call" | custom-call | flops 600000000 | bytes 1000000 | tf_op jit(solution)/shard_map/pallas_call | solution.py:43
Async XLA Ops:
  2.6 49.5 %all-to-all-start = ((bf16[64,72,128]{2,1,0:T(8,128)(2,1)}), bf16[64,72,128]{2,1,0:T(8,128)(2,1)S(1)}, u32[]{:S(2)}, u32[]{:S(2)}) async-start(bf16[64,72,128]{2,1,0:T(8,128)(2,1)} %shard_map.104), calls=%async_computation | async-start | bytes 2359296 | tf_op jit(solution)/shard_map/all_to_all | solution.py:231
  19.8 23.5 %copy-start.1 = (s32[3]{0:T(128)S(1)}, s32[3]{0:T(128)}, u32[]{:S(2)}) copy-start(s32[3]{0:T(128)} %pad_add_fusion.where_ref) | copy-start | bytes 40
  19.8 23.5 %copy-start.2 = (s32[1,64]{1,0:T(1,128)S(1)}, s32[1,64]{1,0:T(1,128)}, u32[]{:S(2)}) copy-start(s32[1,64]{1,0:T(1,128)} %ok_ref.1) | copy-start | bytes 772
  19.8 23.5 %copy-start.3 = (s32[1,64]{1,0:T(1,128)S(1)}, s32[1,64]{1,0:T(1,128)}, u32[]{:S(2)}) copy-start(s32[1,64]{1,0:T(1,128)} %id_ref.1) | copy-start | bytes 772
  19.8 23.5 %copy-start.4 = (bf16[512,1024]{1,0:T(8,128)(2,1)S(1)}, bf16[512,1024]{1,0:T(8,128)(2,1)}, u32[]{:S(2)}) copy-start(bf16[512,1024]{1,0:T(8,128)(2,1)} %x_ref.1) | copy-start | bytes 3145732
  19.8 23.5 %copy-start.5 = (s32[64,64]{1,0:T(8,128)S(1)}, s32[64,64]{1,0:T(8,128)}, u32[]{:S(2)}) copy-start(s32[64,64]{1,0:T(8,128)} %plan_ref.3) | copy-start | bytes 49156
  25.7 3.5 %collective-permute-start = (bf16[512,128]{1,0:T(8,128)(2,1)}, bf16[512,128]{1,0:T(8,128)(2,1)S(1)}, u32[]{:S(2)}, u32[]{:S(2)}) collective-permute-start(bf16[512,128]{1,0:T(8,128)(2,1)} %get-tuple-element.13), channel_id=1, source_target_pairs={{0,1},{1,0},{2,3},{3,2},{4,5},{5,4},{6,7},{7,6},{8,9},{9,8},{10,11... | collective-permute-start | bytes 393224 | tf_op jit(solution)/shard_map/ppermute | solution.py:219
  44.8 1.0 copy-start.7
  45.8 0.8 copy-start.9
  52.1 1.2 %copy-start.8 = (bf16[512,1024]{1,0:T(8,128)(2,1)S(1)}, bf16[512,1024]{1,0:T(8,128)(2,1)}, u32[]{:S(2)}) copy-start(bf16[512,1024]{1,0:T(8,128)(2,1)} %copy-done.7) | copy-start | bytes 3145732
  53.3 1.1 copy-start.10
  57.8 23.5 %all-to-all-start.1 = ((bf16[4,1024,128]{2,1,0:T(8,128)(2,1)}), bf16[4,1024,128]{2,1,0:T(8,128)(2,1)S(1)}, u32[]{:S(2)}, u32[]{:S(2)}) async-start(bf16[4,1024,128]{2,1,0:T(8,128)(2,1)} %get-tuple-element.20), calls=%async_computation.1 | async-start | bytes 2097152 | tf_op jit(solution)/shard_map/all_to_all | solution.py:231
  61.3 20.0 %copy-start = (bf16[512,128]{1,0:T(8,128)(2,1)S(1)}, bf16[512,128]{1,0:T(8,128)(2,1)}, u32[]{:S(2)}) copy-start(bf16[512,128]{1,0:T(8,128)(2,1)} %get-tuple-element.21.pr_ref) | copy-start | bytes 393220
  61.3 3.9 %collective-permute-start.1 = (bf16[4,512,128]{2,1,0:T(8,128)(2,1)S(1)}, bf16[4,512,128]{2,1,0:T(8,128)(2,1)S(1)}, u32[]{:S(2)}, u32[]{:S(2)}) collective-permute-start(bf16[4,512,128]{2,1,0:T(8,128)(2,1)S(1)} %get-tuple-element.16.mine_ref), channel_id=1, source_target_pairs={{0,1},{1,0},{2,3},{3,2},{4,5},{5,4},{6,7},{7,6},{8,9},{9,8},{10,11... | collective-permute-start | bytes 1572872 | tf_op jit(solution)/shard_map/ppermute | solution.py:219
  65.8 11.6 %collective-permute-start.2 = (bf16[512,128]{1,0:T(8,128)(2,1)S(1)}, bf16[512,128]{1,0:T(8,128)(2,1)S(1)}, u32[]{:S(2)}, u32[]{:S(2)}) collective-permute-start(bf16[512,128]{1,0:T(8,128)(2,1)S(1)} %get-tuple-element.18), channel_id=1, source_target_pairs={{0,2},{1,7},{2,4},{3,1},{4,6},{5,3},{6,0},{7,5},{8,10},{9,15},{10,... | collective-permute-start | bytes 393224 | tf_op jit(solution)/shard_map/ppermute | solution.py:223
  69.2 8.2 %collective-permute-start.3 = (bf16[256,128]{1,0:T(8,128)(2,1)S(1)}, bf16[256,128]{1,0:T(8,128)(2,1)S(1)}, u32[]{:S(2)}, u32[]{:S(2)}) collective-permute-start(bf16[256,128]{1,0:T(8,128)(2,1)S(1)} %get-tuple-element.19), channel_id=1, source_target_pairs={{0,4},{1,5},{2,6},{3,7},{4,0},{5,1},{6,2},{7,3},{8,12},{9,13},{10,... | collective-permute-start | bytes 196616 | tf_op jit(solution)/shard_map/ppermute | solution.py:227
  78.0 3.2 %collective-permute-start.4 = (bf16[512,128]{1,0:T(8,128)(2,1)S(1)}, bf16[512,128]{1,0:T(8,128)(2,1)S(1)}, u32[]{:S(2)}, u32[]{:S(2)}) collective-permute-start(bf16[512,128]{1,0:T(8,128)(2,1)S(1)} %shard_map.109.r1_ref), channel_id=1, source_target_pairs={{0,1},{1,0},{2,3},{3,2},{4,5},{5,4},{6,7},{7,6},{8,9},{9,8},{10,11... | collective-permute-start | bytes 393224 | tf_op jit(solution)/shard_map/ppermute | solution.py:219
  81.3 27.4 %copy-start.6 = (s32[64,64]{1,0:T(8,128)S(1)}, s32[64,64]{1,0:T(8,128)}, u32[]{:S(2)}) copy-start(s32[64,64]{1,0:T(8,128)} %len_ref.3) | copy-start | bytes 49156

commit v3 on v2

--- a/solution.py
+++ b/solution.py
@@ -138,12 +138,15 @@
     return 1.0 - missed
 
 
-def multiply(where_ref, w_ref, xb_ref, dv_ref, part_ref, grad_ref):
+def project(where_ref, w_ref, xb_ref, out_ref):
     xpos = where_ref[1]
     for i in range(KEY_HEADS):
         m = lax.rem(xpos + i, KEY_HEADS)
         w = w_ref[:, pl.ds(pl.multiple_of(m * WROWS, WROWS), WROWS), :].reshape(FEATS, HEAD)
-        part_ref[i] = dot(xb_ref[...], w).astype(bf16)
+        out_ref[i] = dot(xb_ref[...], w).astype(bf16)
+
+
+def weight_gradient(w_ref, xb_ref, dv_ref, after_ref, out_ref):
     hits = jnp.sum(w_ref[:, BLOCK:, :].astype(f32), axis=0)[:1]
     good = (iota((1, 128), 1) // BINS).astype(f32)
     table = pass_rate(float(GROUP), hits) - pass_rate(float(GROUP - 1), hits - good)
@@ -152,7 +155,7 @@
     dv = (gain * dv_ref[:, : KEY_HEADS * HEAD].astype(f32)).astype(bf16)
     grad = dot(xb_ref[...].T, dv).astype(bf16)
     for m in range(KEY_HEADS):
-        grad_ref[m] = grad[:, m * HEAD : (m + 1) * HEAD]
+        out_ref[m] = grad[:, m * HEAD : (m + 1) * HEAD]
 
 
 def add_cores(where_ref, mine_ref, other_ref, own_ref, next_ref, far_ref):
@@ -178,23 +181,26 @@
     out_ref[:, WROWS + LMAX :, :] = pr_ref[...].reshape(BINS, LMAX, HEAD)
 
 
-def finish(where_ref, got_ref, len_ref, grad_ref, out_ref):
-    me = where_ref[0]
-    probs = got_ref[:, WROWS + LMAX :, :].reshape(ROWS, HEAD)
-    values = got_ref[:, WROWS : WROWS + LMAX, :].reshape(ROWS, HEAD)
-    own = jnp.where(iota((BINS, BINS), 0) == me, len_ref[...], 0).astype(f32)
+def place_rows(where_ref, len_ref, take_ref, same_ref):
+    own = jnp.where(iota((BINS, BINS), 0) == where_ref[0], len_ref[...], 0).astype(f32)
     own = jnp.broadcast_to(jnp.sum(own, axis=0, keepdims=True), (8, BINS)).astype(bf16)
     s, lane = iota((BINS, ROWS), 0), iota((BINS, ROWS), 1)
     start = dot(own, (s < lane // LMAX).astype(f32).astype(bf16))[:1].astype(jnp.int32)
     size = dot(own, (s == lane // LMAX).astype(f32).astype(bf16))[:1].astype(jnp.int32)
     i, lane = iota((PACKED, ROWS), 0), iota((PACKED, ROWS), 1)
     same = (i >= start) & (i < start + size)
-    take = same & (i == start + lane % LMAX)
-    packed = dot(take.astype(f32).astype(bf16), probs).astype(bf16)
+    same_ref[...] = same.astype(f32).astype(bf16)
+    take_ref[...] = (same & (i == start + lane % LMAX)).astype(f32).astype(bf16)
+
+
+def finish(got_ref, take_ref, same_ref, grad_ref, out_ref):
+    probs = got_ref[:, WROWS + LMAX :, :].reshape(ROWS, HEAD)
+    values = got_ref[:, WROWS : WROWS + LMAX, :].reshape(ROWS, HEAD)
+    packed = dot(take_ref[...], probs).astype(bf16)
     a, b = iota((HEAD, ROWS), 0), iota((HEAD, ROWS), 1)
     for h in range(HEADS_DEV):
         spread = dot(packed, (a == h * LMAX + b % LMAX).astype(f32).astype(bf16))
-        spread = jnp.where(same, spread, 0.0).astype(bf16)
+        spread = spread.astype(bf16) * same_ref[...]
         out_ref[:, h * HEAD : (h + 1) * HEAD] = dot(spread, values).astype(bf16)
     for m in range(KEY_HEADS):
         total = jnp.zeros((WROWS, HEAD), f32)
@@ -279,16 +285,23 @@
         6 * 10**8,
         4 * 10**6,
     )
-    part, grads = call(
-        multiply,
-        (struct((KEY_HEADS, ROWS, HEAD), bf16), struct((KEY_HEADS, FEATS, HEAD), bf16)),
-        (where, weights, x_bins, packed),
-        [SM] + [VM] * 3,
-        10**9,
-        6 * 10**6,
+    part = call(
+        project,
+        struct((KEY_HEADS, ROWS, HEAD), bf16),
+        (where, weights, x_bins),
+        [SM, VM, VM],
+        6 * 10**8,
+        3 * 10**6,
     )
     other_part = swap_cores(part)
-    near = all_to_all(grads, SQUARES)
+    grads = call(
+        weight_gradient,
+        struct((KEY_HEADS, FEATS, HEAD), bf16),
+        (weights, x_bins, packed, part),
+        [VM, VM, VM, HB],
+        6 * 10**8,
+        3 * 10**6,
+    )
     own, following, far = call(
         add_cores,
         (struct((ROWS, HEAD), f32), rows, struct((ROWS // 2, HEAD), bf16)),
@@ -297,6 +310,8 @@
         10**6,
         2 * 10**6,
     )
+    grads, following = lax.optimization_barrier((grads, following))
+    near = all_to_all(grads, SQUARES)
     arrived = call(
         add_arrived,
         rows,
@@ -313,11 +328,15 @@
         10**6,
         3 * 10**6,
     )
+    square = struct((PACKED, ROWS), bf16)
+    take, same = call(
+        place_rows, (square, square), (where, lengths), [SM, VM], 10**7, 10**6
+    )
     grad_weight, context = call(
         finish,
         (struct((WROWS, KEY_HEADS * HEAD), f32), struct((PACKED, HEADS_DEV * HEAD), bf16)),
-        (where, all_to_all(block), lengths),
-        [SM] + [VM] * 2,
+        (all_to_all(block), take, same),
+        [VM] * 3,
         6 * 10**8,
         10**6,
     )

time: 112 us -> 108 us (0.964)
  blocking collectives: 40.3 us -> 13.1 us
  waiting for transfers between devices: 13.7 us -> 30.7 us
  starting transfers between devices: 34 us -> 41.5 us
  local copies, waits for them, and re-layouts: 4.15 us -> 1.24 us
  Pallas kernels: 16.6 us -> 18.1 us
    all_to_all x1 -> x0, blocking collectives: 27.2 us -> none  [all_to_all(): lax.all_to_all(a, 'dp', split_axis=0, concat_axis=0, tiled=True, axis_ind...]
    all_to_all x2 -> x3, waiting for transfers between devices: 5.48 us -> 24.8 us  [all_to_all(): lax.all_to_all(a, 'dp', split_axis=0, concat_axis=0, tiled=True, axis_ind...]
    all_to_all x2 -> x3, starting transfers between devices: 20 us -> 27.4 us  [all_to_all(): lax.all_to_all(a, 'dp', split_axis=0, concat_axis=0, tiled=True, axis_ind...]
    unnamed x22 -> x14, local copies, waits for them, and re-layouts: 4.15 us -> 1.24 us
    ppermute x3, waiting for transfers between devices: 4.61 us -> 2.59 us  [swap_cores(): return lax.ppermute(a, 'mp', [(p, p ^ 1) for p in range(8)])]
    pallas_call x8 -> x10, Pallas kernels: 16.6 us -> 18.1 us  [call(): pl.pallas_call(body, out_shape=out_shape, in_specs=specs, out_specs=jax.t...]
  transfers between devices with their start and end apart: 7 -> 8, of which waited for: 5 -> 5; matrix products, arithmetic and copies ran while one was open for 1% -> 1% of each run, Pallas kernels for 8% -> 10%
where the time goes in v3:
time: 108 us; the launch traced here: 107 us
  starting transfers between devices  41.5 us (38%)
  waiting for transfers between devices  30.7 us (28%)
  Pallas kernels  18.1 us (17%)
  blocking collectives  13.1 us (12%)
  other arithmetic  1.6 us (1%)
  local copies, waits for them, and re-layouts  1.24 us (1%)
    all_to_all x3, starting transfers between devices, all_to_all(): lax.all_to_all(a, 'dp', split_axis=0, concat_axis=0, tiled=True, axis_ind...  27.4 us
    all_to_all x3, waiting for transfers between devices, all_to_all(): lax.all_to_all(a, 'dp', split_axis=0, concat_axis=0, tiled=True, axis_ind...  24.8 us
    pallas_call x10, Pallas kernels, call(): pl.pallas_call(body, out_shape=out_shape, in_specs=specs, out_specs=jax.t...  18.1 us
    all_gather x1, blocking collectives, per_device(): lax.all_gather(dv, 'mp', axis_index_groups=[[0, 2, 4, 6], [1, 3, 5, 7]])  13.1 us
    ppermute x3, starting transfers between devices, swap_cores(): return lax.ppermute(a, 'mp', [(p, p ^ 1) for p in range(8)])  6.01 us
    ppermute x1, starting transfers between devices, to_far_chip(): return lax.ppermute(a, 'mp', [(p, (p + 4) % 8) for p in range(8)])  4.64 us
    ppermute x1, starting transfers between devices, to_next_chips(): lax.ppermute(a, 'mp', [(p, (p + (2, -2)[p % 2]) % 8) for p in range(8)])  3.4 us
    ppermute x1, waiting for transfers between devices, to_far_chip(): return lax.ppermute(a, 'mp', [(p, (p + 4) % 8) for p in range(8)])  3.28 us
  transfers between devices with their start and end apart: 8, of which 5 were waited for; matrix products, arithmetic and copies ran while one was open for 1% of the time, Pallas kernels for 10%

profile of v3, /device:TPU:16, one launch (start us, length us, event | category | flops | bytes accessed | tf_op | source)
XLA Modules:
  0.0 107.0 jit_solution(13077902571452886736)
XLA Ops:
  0.6 2.0 %shard_map.104 = bf16[64,72,128]{2,1,0:T(8,128)(2,1)} custom-call(bf16[16,512]{1,0:T(8,128)(2,1)} %wm_hbm.1, s32[1,64]{1,0:T(1,128)} %ok_ref.1, s32[1,64]{1,0:T(1,128)} %id_ref.1), custom_call_target="tpu_custom_call" | custom-call | flops 1000000 | bytes 1000000 | tf_op jit(solution)/shard_map/pallas_call | solution.py:43
  2.6 16.5 %all-to-all-start = ((bf16[64,72,128]{2,1,0:T(8,128)(2,1)}), bf16[64,72,128]{2,1,0:T(8,128)(2,1)S(1)}, u32[]{:S(2)}, u32[]{:S(2)}) async-start(bf16[64,72,128]{2,1,0:T(8,128)(2,1)} %shard_map.104), calls=%async_computation | async-start | bytes 2359296 | tf_op jit(solution)/shard_map/all_to_all | solution.py:237
  19.1 0.7 pad_add_fusion.where_ref
  19.8 0.0 copy-start.1
  19.8 0.0 copy-start.2
  19.8 0.0 copy-start.3
  19.8 0.0 copy-start.5
  19.8 5.9 %shard_map.105 = (bf16[512,128]{1,0:T(8,128)(2,1)}, bf16[512,128]{1,0:T(8,128)(2,1)}) custom-call(s32[3]{0:T(128)} %pad_add_fusion.where_ref, bf16[512,512]{1,0:T(8,128)(2,1)} %q_hbm.1, bf16[512,512]{1,0:T(8,128)(2,1)} %k_hbm.1, bf16[512,512]{1,0:T(8,128)(2,1)} %g_hbm.1, s32[64,64]{1,0:T(8,128)} %len_ref.3, s32[64,64]{1,0:T(8,128)} %plan_ref.3), custom_call_target="tpu_custom_call" | custom-call | flops 2000000000 | bytes 2000000 | tf_op jit(solution)/shard_map/pallas_call | solution.py:43
  25.7 1.9 %collective-permute-start = (bf16[512,128]{1,0:T(8,128)(2,1)}, bf16[512,128]{1,0:T(8,128)(2,1)S(1)}, u32[]{:S(2)}, u32[]{:S(2)}) collective-permute-start(bf16[512,128]{1,0:T(8,128)(2,1)} %get-tuple-element.15), channel_id=1, source_target_pairs={{0,1},{1,0},{2,3},{3,2},{4,5},{5,4},{6,7},{7,6},{8,9},{9,8},{10,11... | collective-permute-start | bytes 393224 | tf_op jit(solution)/shard_map/ppermute | solution.py:225
  27.6 1.5 %collective-permute-done = bf16[512,128]{1,0:T(8,128)(2,1)S(1)} collective-permute-done((bf16[512,128]{1,0:T(8,128)(2,1)}, bf16[512,128]{1,0:T(8,128)(2,1)S(1)}, u32[]{:S(2)}, u32[]{:S(2)}) %collective-permute-start) | collective-permute-done | bytes 131104 | tf_op jit(solution)/shard_map/ppermute | solution.py:225
  29.1 0.9 add_convert_fusion
  30.1 13.1 %all-gather = bf16[2048,128]{1,0:T(8,128)(2,1)S(1)} all-gather(bf16[512,128]{1,0:T(8,128)(2,1)S(1)} %add_convert_fusion), channel_id=2, replica_groups={{0,2,4,6},{1,3,5,7},{8,10,12,14},{9,11,13,15},{16,18,20,22},{17,19,21,2..., dimensions={0}, use_global_device_ids=true | all-gather | bytes 655360 | tf_op jit(solution)/shard_map/all_gather | solution.py:279
  43.2 0.0 copy-done.1
  43.2 0.0 copy-done.2
  43.2 0.0 copy-done.3
  43.2 0.0 copy-done.5
  43.2 0.0 copy-start.4
  43.3 1.2 %copy-done.4 = bf16[512,1024]{1,0:T(8,128)(2,1)S(1)} copy-done((bf16[512,1024]{1,0:T(8,128)(2,1)S(1)}, bf16[512,1024]{1,0:T(8,128)(2,1)}, u32[]{:S(2)}) %copy-start.4) | copy-done | bytes 1048600
  44.5 1.5 %shard_map.106 = (bf16[512,1024]{1,0:T(8,128)(2,1)S(1)}, bf16[512,640]{1,0:T(8,128)(2,1)S(1)}) custom-call(s32[3]{0:T(128)S(1)} %copy-done.1, bf16[512,1024]{1,0:T(8,128)(2,1)S(1)} %copy-done.4, s32[64,64]{1,0:T(8,128)S(1)} %copy-done.5, s32[1,64]{1,0:T(1,128)S(1)} %copy-done.2, s32[1,64]{1,0:T(1,128)S(1)} %copy-done.3, bf16[4,512,128]{2,1,0:T(8,128)(2,1)S(1)} %bitcast.4), custom_call_target="tpu_custom_call" | custom-call | flops 600000000 | bytes 4000000 | tf_op jit(solution)/shard_map/pallas_call | solution.py:43
  46.0 6.1 %all-to-all-done.w_ref = bf16[64,72,128]{2,1,0:T(8,128)(2,1)S(1)} async-done(((bf16[64,72,128]{2,1,0:T(8,128)(2,1)}), bf16[64,72,128]{2,1,0:T(8,128)(2,1)S(1)}, u32[]{:S(2)}, u32[]{:S(2)}) %all-to-all-start) | async-done | bytes 1179680 | tf_op jit(solution)/shard_map/all_to_all | solution.py:237
  52.1 1.8 %shard_map.107.mine_ref.after_ref = bf16[4,512,128]{2,1,0:T(8,128)(2,1)S(1)} custom-call(s32[3]{0:T(128)S(1)} %copy-done.1, bf16[64,72,128]{2,1,0:T(8,128)(2,1)S(1)} %all-to-all-done.w_ref, bf16[512,1024]{1,0:T(8,128)(2,1)S(1)} %get-tuple-element.16.xb_ref), custom_call_target="tpu_custom_call" | custom-call | flops 600000000 | bytes 3000000 | tf_op jit(solution)/shard_map/pallas_call | solution.py:43
  53.9 1.9 %collective-permute-start.1 = (bf16[4,512,128]{2,1,0:T(8,128)(2,1)S(1)}, bf16[4,512,128]{2,1,0:T(8,128)(2,1)S(1)}, u32[]{:S(2)}, u32[]{:S(2)}) collective-permute-start(bf16[4,512,128]{2,1,0:T(8,128)(2,1)S(1)} %shard_map.107.mine_ref.after_ref), channel_id=1, source_target_pairs={{0,1},{1,0},{2,3},{3,2},{4,5},{5,4},{6,7},{7,6},{8,9},{9,8},{10,11... | collective-permute-start | bytes 1572872 | tf_op jit(solution)/shard_map/ppermute | solution.py:225
  55.8 1.9 %shard_map.109 = bf16[4,1024,128]{2,1,0:T(8,128)(2,1)} custom-call(bf16[64,72,128]{2,1,0:T(8,128)(2,1)S(1)} %all-to-all-done.w_ref, bf16[512,1024]{1,0:T(8,128)(2,1)S(1)} %get-tuple-element.16.xb_ref, bf16[512,640]{1,0:T(8,128)(2,1)S(1)} %get-tuple-element.18.dv_ref, bf16[4,512,128]{2,1,0:T(8,128)(2,1)S(1)} %shard_map.107.mine_ref.after_ref), custom_call_target="tpu_custom_call" | custom-call | flops 600000000 | bytes 3000000 | tf_op jit(solution)/shard_map/pallas_call | solution.py:43
  57.7 0.0 collective-permute-done.1.other_ref
  57.7 0.6 shard_map.108
  58.4 0.0 copy-start
  58.4 3.7 %all-to-all-start.1 = ((bf16[4,1024,128]{2,1,0:T(8,128)(2,1)}), bf16[4,1024,128]{2,1,0:T(8,128)(2,1)S(1)}, u32[]{:S(2)}, u32[]{:S(2)}) async-start(bf16[4,1024,128]{2,1,0:T(8,128)(2,1)} %shard_map.109), calls=%async_computation.1 | async-start | bytes 2097152 | tf_op jit(solution)/shard_map/all_to_all | solution.py:237
  62.0 3.4 %collective-permute-start.2 = (bf16[512,128]{1,0:T(8,128)(2,1)S(1)}, bf16[512,128]{1,0:T(8,128)(2,1)S(1)}, u32[]{:S(2)}, u32[]{:S(2)}) collective-permute-start(bf16[512,128]{1,0:T(8,128)(2,1)S(1)} %get-tuple-element.20), channel_id=1, source_target_pairs={{0,2},{1,7},{2,4},{3,1},{4,6},{5,3},{6,0},{7,5},{8,10},{9,15},{10,... | collective-permute-start | bytes 393224 | tf_op jit(solution)/shard_map/ppermute | solution.py:229
  65.4 4.6 %collective-permute-start.3 = (bf16[256,128]{1,0:T(8,128)(2,1)S(1)}, bf16[256,128]{1,0:T(8,128)(2,1)S(1)}, u32[]{:S(2)}, u32[]{:S(2)}) collective-permute-start(bf16[256,128]{1,0:T(8,128)(2,1)S(1)} %get-tuple-element.21), channel_id=1, source_target_pairs={{0,4},{1,5},{2,6},{3,7},{4,0},{5,1},{6,2},{7,3},{8,12},{9,13},{10,... | collective-permute-start | bytes 196616 | tf_op jit(solution)/shard_map/ppermute | solution.py:233
  70.1 3.3 %collective-permute-done.3.far_ref = bf16[256,128]{1,0:T(8,128)(2,1)S(1)} collective-permute-done((bf16[256,128]{1,0:T(8,128)(2,1)S(1)}, bf16[256,128]{1,0:T(8,128)(2,1)S(1)}, u32[]{:S(2)}, u32[]{:S(2)}) %collective-permute-start.3) | collective-permute-done | bytes 65568 | tf_op jit(solution)/shard_map/ppermute | solution.py:233
  73.4 0.0 collective-permute-done.2.next_ref
  73.4 0.6 shard_map.110.r1_ref
  74.0 2.2 %collective-permute-start.4 = (bf16[512,128]{1,0:T(8,128)(2,1)S(1)}, bf16[512,128]{1,0:T(8,128)(2,1)S(1)}, u32[]{:S(2)}, u32[]{:S(2)}) collective-permute-start(bf16[512,128]{1,0:T(8,128)(2,1)S(1)} %shard_map.110.r1_ref), channel_id=1, source_target_pairs={{0,1},{1,0},{2,3},{3,2},{4,5},{5,4},{6,7},{7,6},{8,9},{9,8},{10,11... | collective-permute-start | bytes 393224 | tf_op jit(solution)/shard_map/ppermute | solution.py:225
  76.1 1.1 collective-permute-done.4.r2_ref
  77.2 0.0 all-to-all-done.1.near_ref
  77.2 0.0 copy-done
  77.2 0.0 copy-start.6
  77.2 1.0 shard_map.111
  78.2 7.3 %all-to-all-start.2 = ((bf16[64,32,128]{2,1,0:T(8,128)(2,1)}), bf16[64,32,128]{2,1,0:T(8,128)(2,1)S(1)}, u32[]{:S(2)}, u32[]{:S(2)}) async-start(bf16[64,32,128]{2,1,0:T(8,128)(2,1)} %shard_map.111), calls=%async_computation.2 | async-start | bytes 1048576 | tf_op jit(solution)/shard_map/all_to_all | solution.py:237
  85.5 0.0 copy-done.6
  85.5 1.0 shard_map.112
  86.5 18.7 %all-to-all-done.2.got_ref = bf16[64,32,128]{2,1,0:T(8,128)(2,1)S(1)} async-done(((bf16[64,32,128]{2,1,0:T(8,128)(2,1)}), bf16[64,32,128]{2,1,0:T(8,128)(2,1)S(1)}, u32[]{:S(2)}, u32[]{:S(2)}) %all-to-all-start.2) | async-done | bytes 524320 | tf_op jit(solution)/shard_map/all_to_all | solution.py:237
  105.2 1.8 %shard_map.113 = (f32[16,512]{1,0:T(8,128)}, bf16[256,512]{1,0:T(8,128)(2,1)}) custom-call(bf16[64,32,128]{2,1,0:T(8,128)(2,1)S(1)} %all-to-all-done.2.got_ref, bf16[256,512]{1,0:T(8,128)(2,1)S(1)} %get-tuple-element.24.take_ref, bf16[256,512]{1,0:T(8,128)(2,1)S(1)} %get-tuple-element.25.same_ref), custom_call_target="tpu_custom_call" | custom-call | flops 600000000 | bytes 1000000 | tf_op jit(solution)/shard_map/pallas_call | solution.py:43
Async XLA Ops:
  2.6 49.5 %all-to-all-start = ((bf16[64,72,128]{2,1,0:T(8,128)(2,1)}), bf16[64,72,128]{2,1,0:T(8,128)(2,1)S(1)}, u32[]{:S(2)}, u32[]{:S(2)}) async-start(bf16[64,72,128]{2,1,0:T(8,128)(2,1)} %shard_map.104), calls=%async_computation | async-start | bytes 2359296 | tf_op jit(solution)/shard_map/all_to_all | solution.py:237
  19.8 23.5 %copy-start.1 = (s32[3]{0:T(128)S(1)}, s32[3]{0:T(128)}, u32[]{:S(2)}) copy-start(s32[3]{0:T(128)} %pad_add_fusion.where_ref) | copy-start | bytes 40
  19.8 23.5 %copy-start.2 = (s32[1,64]{1,0:T(1,128)S(1)}, s32[1,64]{1,0:T(1,128)}, u32[]{:S(2)}) copy-start(s32[1,64]{1,0:T(1,128)} %ok_ref.1) | copy-start | bytes 772
  19.8 23.5 %copy-start.3 = (s32[1,64]{1,0:T(1,128)S(1)}, s32[1,64]{1,0:T(1,128)}, u32[]{:S(2)}) copy-start(s32[1,64]{1,0:T(1,128)} %id_ref.1) | copy-start | bytes 772
  19.8 23.5 %copy-start.5 = (s32[64,64]{1,0:T(8,128)S(1)}, s32[64,64]{1,0:T(8,128)}, u32[]{:S(2)}) copy-start(s32[64,64]{1,0:T(8,128)} %plan_ref.3) | copy-start | bytes 49156
  25.7 3.5 %collective-permute-start = (bf16[512,128]{1,0:T(8,128)(2,1)}, bf16[512,128]{1,0:T(8,128)(2,1)S(1)}, u32[]{:S(2)}, u32[]{:S(2)}) collective-permute-start(bf16[512,128]{1,0:T(8,128)(2,1)} %get-tuple-element.15), channel_id=1, source_target_pairs={{0,1},{1,0},{2,3},{3,2},{4,5},{5,4},{6,7},{7,6},{8,9},{9,8},{10,11... | collective-permute-start | bytes 393224 | tf_op jit(solution)/shard_map/ppermute | solution.py:225
  43.2 1.2 %copy-start.4 = (bf16[512,1024]{1,0:T(8,128)(2,1)S(1)}, bf16[512,1024]{1,0:T(8,128)(2,1)}, u32[]{:S(2)}) copy-start(bf16[512,1024]{1,0:T(8,128)(2,1)} %x_ref.1) | copy-start | bytes 3145732
  53.9 3.8 %collective-permute-start.1 = (bf16[4,512,128]{2,1,0:T(8,128)(2,1)S(1)}, bf16[4,512,128]{2,1,0:T(8,128)(2,1)S(1)}, u32[]{:S(2)}, u32[]{:S(2)}) collective-permute-start(bf16[4,512,128]{2,1,0:T(8,128)(2,1)S(1)} %shard_map.107.mine_ref.after_ref), channel_id=1, source_target_pairs={{0,1},{1,0},{2,3},{3,2},{4,5},{5,4},{6,7},{7,6},{8,9},{9,8},{10,11... | collective-permute-start | bytes 1572872 | tf_op jit(solution)/shard_map/ppermute | solution.py:225
  58.4 18.8 %copy-start = (bf16[512,128]{1,0:T(8,128)(2,1)S(1)}, bf16[512,128]{1,0:T(8,128)(2,1)}, u32[]{:S(2)}) copy-start(bf16[512,128]{1,0:T(8,128)(2,1)} %get-tuple-element.23.pr_ref) | copy-start | bytes 393220
  58.4 18.8 %all-to-all-start.1 = ((bf16[4,1024,128]{2,1,0:T(8,128)(2,1)}), bf16[4,1024,128]{2,1,0:T(8,128)(2,1)S(1)}, u32[]{:S(2)}, u32[]{:S(2)}) async-start(bf16[4,1024,128]{2,1,0:T(8,128)(2,1)} %shard_map.109), calls=%async_computation.1 | async-start | bytes 2097152 | tf_op jit(solution)/shard_map/all_to_all | solution.py:237
  62.0 11.3 %collective-permute-start.2 = (bf16[512,128]{1,0:T(8,128)(2,1)S(1)}, bf16[512,128]{1,0:T(8,128)(2,1)S(1)}, u32[]{:S(2)}, u32[]{:S(2)}) collective-permute-start(bf16[512,128]{1,0:T(8,128)(2,1)S(1)} %get-tuple-element.20), channel_id=1, source_target_pairs={{0,2},{1,7},{2,4},{3,1},{4,6},{5,3},{6,0},{7,5},{8,10},{9,15},{10,... | collective-permute-start | bytes 393224 | tf_op jit(solution)/shard_map/ppermute | solution.py:229
  65.4 7.9 %collective-permute-start.3 = (bf16[256,128]{1,0:T(8,128)(2,1)S(1)}, bf16[256,128]{1,0:T(8,128)(2,1)S(1)}, u32[]{:S(2)}, u32[]{:S(2)}) collective-permute-start(bf16[256,128]{1,0:T(8,128)(2,1)S(1)} %get-tuple-element.21), channel_id=1, source_target_pairs={{0,4},{1,5},{2,6},{3,7},{4,0},{5,1},{6,2},{7,3},{8,12},{9,13},{10,... | collective-permute-start | bytes 196616 | tf_op jit(solution)/shard_map/ppermute | solution.py:233
  74.0 3.2 %collective-permute-start.4 = (bf16[512,128]{1,0:T(8,128)(2,1)S(1)}, bf16[512,128]{1,0:T(8,128)(2,1)S(1)}, u32[]{:S(2)}, u32[]{:S(2)}) collective-permute-start(bf16[512,128]{1,0:T(8,128)(2,1)S(1)} %shard_map.110.r1_ref), channel_id=1, source_target_pairs={{0,1},{1,0},{2,3},{3,2},{4,5},{5,4},{6,7},{7,6},{8,9},{9,8},{10,11... | collective-permute-start | bytes 393224 | tf_op jit(solution)/shard_map/ppermute | solution.py:225
  77.2 8.3 %copy-start.6 = (s32[64,64]{1,0:T(8,128)S(1)}, s32[64,64]{1,0:T(8,128)}, u32[]{:S(2)}) copy-start(s32[64,64]{1,0:T(8,128)} %len_ref.3) | copy-start | bytes 49156
  78.2 27.0 %all-to-all-start.2 = ((bf16[64,32,128]{2,1,0:T(8,128)(2,1)}), bf16[64,32,128]{2,1,0:T(8,128)(2,1)S(1)}, u32[]{:S(2)}, u32[]{:S(2)}) async-start(bf16[64,32,128]{2,1,0:T(8,128)(2,1)} %shard_map.111), calls=%async_computation.2 | async-start | bytes 1048576 | tf_op jit(solution)/shard_map/all_to_all | solution.py:237

commit v4 on v3

--- a/solution.py
+++ b/solution.py
@@ -167,7 +167,7 @@
     far_ref[...] = (mine_ref[2, half].astype(f32) + other_ref[2, half].astype(f32)).astype(bf16)
 
 
-def add_arrived(where_ref, next_ref, far_ref, out_ref):
+def add_arrived(where_ref, next_ref, far_ref, take_ref, same_ref, out_ref):
     half = pl.ds(pl.multiple_of(where_ref[2] * (ROWS // 2), ROWS // 2), ROWS // 2)
     out_ref[...] = next_ref[...]
     out_ref[half] = (next_ref[half].astype(f32) + far_ref[...].astype(f32)).astype(bf16)
@@ -312,11 +312,15 @@
     )
     grads, following = lax.optimization_barrier((grads, following))
     near = all_to_all(grads, SQUARES)
+    square = struct((PACKED, ROWS), bf16)
+    take, same = call(
+        place_rows, (square, square), (where, lengths), [SM, VM], 10**7, 10**6
+    )
     arrived = call(
         add_arrived,
         rows,
-        (where, to_next_chips(following), to_far_chip(far)),
-        [SM] + [VM] * 2,
+        (where, to_next_chips(following), to_far_chip(far), take, same),
+        [SM] + [VM] * 2 + [HB] * 2,
         10**6,
         10**6,
     )
@@ -327,10 +331,6 @@
         [VM] * 5,
         10**6,
         3 * 10**6,
-    )
-    square = struct((PACKED, ROWS), bf16)
-    take, same = call(
-        place_rows, (square, square), (where, lengths), [SM, VM], 10**7, 10**6
     )
     grad_weight, context = call(
         finish,

time: 108 us -> 107 us (level)
  blocking collectives: 13.1 us -> 40 us
  waiting for transfers between devices: 30.7 us -> 11 us
  starting transfers between devices: 41.5 us -> 34.2 us
    all_to_all x0 -> x1, blocking collectives: none -> 26.8 us  [all_to_all(): lax.all_to_all(a, 'dp', split_axis=0, concat_axis=0, tiled=True, axis_ind...]
    all_to_all x3 -> x2, waiting for transfers between devices: 24.8 us -> 6.13 us  [all_to_all(): lax.all_to_all(a, 'dp', split_axis=0, concat_axis=0, tiled=True, axis_ind...]
    all_to_all x3 -> x2, starting transfers between devices: 27.4 us -> 20.1 us  [all_to_all(): lax.all_to_all(a, 'dp', split_axis=0, concat_axis=0, tiled=True, axis_ind...]
  transfers between devices with their start and end apart: 8 -> 7, of which waited for: 5 -> 4; matrix products, arithmetic and copies ran while one was open for 1% -> 2% of each run, Pallas kernels for 10% -> 10%
where the time goes in v4:
time: 107 us; the launch traced here: 106 us
  blocking collectives  40 us (37%)
  starting transfers between devices  34.2 us (32%)
  Pallas kernels  17.2 us (16%)
  waiting for transfers between devices  11 us (10%)
  other arithmetic  1.61 us (2%)
  local copies, waits for them, and re-layouts  1.25 us (1%)
    all_to_all x1, blocking collectives, all_to_all(): lax.all_to_all(a, 'dp', split_axis=0, concat_axis=0, tiled=True, axis_ind...  26.8 us
    all_to_all x2, starting transfers between devices, all_to_all(): lax.all_to_all(a, 'dp', split_axis=0, concat_axis=0, tiled=True, axis_ind...  20.1 us
    pallas_call x10, Pallas kernels, call(): pl.pallas_call(body, out_shape=out_shape, in_specs=specs, out_specs=jax.t...  17.2 us
    all_gather x1, blocking collectives, per_device(): lax.all_gather(dv, 'mp', axis_index_groups=[[0, 2, 4, 6], [1, 3, 5, 7]])  13.1 us
    all_to_all x2, waiting for transfers between devices, all_to_all(): lax.all_to_all(a, 'dp', split_axis=0, concat_axis=0, tiled=True, axis_ind...  6.13 us
    ppermute x3, starting transfers between devices, swap_cores(): return lax.ppermute(a, 'mp', [(p, p ^ 1) for p in range(8)])  6.02 us
    ppermute x1, starting transfers between devices, to_far_chip(): return lax.ppermute(a, 'mp', [(p, (p + 4) % 8) for p in range(8)])  4.63 us
    ppermute x1, starting transfers between devices, to_next_chips(): lax.ppermute(a, 'mp', [(p, (p + (2, -2)[p % 2]) % 8) for p in range(8)])  3.4 us
  transfers between devices with their start and end apart: 7, of which 4 were waited for; matrix products, arithmetic and copies ran while one was open for 2% of the time, Pallas kernels for 10%

profile of v4, /device:TPU:16, one launch (start us, length us, event | category | flops | bytes accessed | tf_op | source)
XLA Modules:
  0.0 106.0 jit_solution(8913852397822180306)
XLA Ops:
  0.6 2.0 %shard_map.104 = bf16[64,72,128]{2,1,0:T(8,128)(2,1)} custom-call(bf16[16,512]{1,0:T(8,128)(2,1)} %wm_hbm.1, s32[1,64]{1,0:T(1,128)} %ok_ref.1, s32[1,64]{1,0:T(1,128)} %id_ref.1), custom_call_target="tpu_custom_call" | custom-call | flops 1000000 | bytes 1000000 | tf_op jit(solution)/shard_map/pallas_call | solution.py:43
  2.6 16.5 %all-to-all-start = ((bf16[64,72,128]{2,1,0:T(8,128)(2,1)}), bf16[64,72,128]{2,1,0:T(8,128)(2,1)S(1)}, u32[]{:S(2)}, u32[]{:S(2)}) async-start(bf16[64,72,128]{2,1,0:T(8,128)(2,1)} %shard_map.104), calls=%async_computation | async-start | bytes 2359296 | tf_op jit(solution)/shard_map/all_to_all | solution.py:237
  19.1 0.7 pad_add_fusion.where_ref
  19.8 0.0 copy-start.1
  19.8 0.0 copy-start.2
  19.8 0.0 copy-start.3
  19.8 0.0 copy-start.5
  19.8 5.9 %shard_map.105 = (bf16[512,128]{1,0:T(8,128)(2,1)}, bf16[512,128]{1,0:T(8,128)(2,1)}) custom-call(s32[3]{0:T(128)} %pad_add_fusion.where_ref, bf16[512,512]{1,0:T(8,128)(2,1)} %q_hbm.1, bf16[512,512]{1,0:T(8,128)(2,1)} %k_hbm.1, bf16[512,512]{1,0:T(8,128)(2,1)} %g_hbm.1, s32[64,64]{1,0:T(8,128)} %len_ref.3, s32[64,64]{1,0:T(8,128)} %plan_ref.3), custom_call_target="tpu_custom_call" | custom-call | flops 2000000000 | bytes 2000000 | tf_op jit(solution)/shard_map/pallas_call | solution.py:43
  25.7 1.9 %collective-permute-start = (bf16[512,128]{1,0:T(8,128)(2,1)}, bf16[512,128]{1,0:T(8,128)(2,1)S(1)}, u32[]{:S(2)}, u32[]{:S(2)}) collective-permute-start(bf16[512,128]{1,0:T(8,128)(2,1)} %get-tuple-element.15), channel_id=1, source_target_pairs={{0,1},{1,0},{2,3},{3,2},{4,5},{5,4},{6,7},{7,6},{8,9},{9,8},{10,11... | collective-permute-start | bytes 393224 | tf_op jit(solution)/shard_map/ppermute | solution.py:225
  27.6 1.5 %collective-permute-done = bf16[512,128]{1,0:T(8,128)(2,1)S(1)} collective-permute-done((bf16[512,128]{1,0:T(8,128)(2,1)}, bf16[512,128]{1,0:T(8,128)(2,1)S(1)}, u32[]{:S(2)}, u32[]{:S(2)}) %collective-permute-start) | collective-permute-done | bytes 131104 | tf_op jit(solution)/shard_map/ppermute | solution.py:225
  29.1 0.9 add_convert_fusion
  30.1 13.1 %all-gather = bf16[2048,128]{1,0:T(8,128)(2,1)S(1)} all-gather(bf16[512,128]{1,0:T(8,128)(2,1)S(1)} %add_convert_fusion), channel_id=2, replica_groups={{0,2,4,6},{1,3,5,7},{8,10,12,14},{9,11,13,15},{16,18,20,22},{17,19,21,2..., dimensions={0}, use_global_device_ids=true | all-gather | bytes 655360 | tf_op jit(solution)/shard_map/all_gather | solution.py:279
  43.2 0.0 copy-done.1
  43.2 0.0 copy-done.2
  43.2 0.0 copy-done.3
  43.2 0.0 copy-done.5
  43.2 0.0 copy-start.4
  43.3 1.2 %copy-done.4 = bf16[512,1024]{1,0:T(8,128)(2,1)S(1)} copy-done((bf16[512,1024]{1,0:T(8,128)(2,1)S(1)}, bf16[512,1024]{1,0:T(8,128)(2,1)}, u32[]{:S(2)}) %copy-start.4) | copy-done | bytes 1048600
  44.5 1.5 %shard_map.106 = (bf16[512,1024]{1,0:T(8,128)(2,1)S(1)}, bf16[512,640]{1,0:T(8,128)(2,1)S(1)}) custom-call(s32[3]{0:T(128)S(1)} %copy-done.1, bf16[512,1024]{1,0:T(8,128)(2,1)S(1)} %copy-done.4, s32[64,64]{1,0:T(8,128)S(1)} %copy-done.5, s32[1,64]{1,0:T(1,128)S(1)} %copy-done.2, s32[1,64]{1,0:T(1,128)S(1)} %copy-done.3, bf16[4,512,128]{2,1,0:T(8,128)(2,1)S(1)} %bitcast.4), custom_call_target="tpu_custom_call" | custom-call | flops 600000000 | bytes 4000000 | tf_op jit(solution)/shard_map/pallas_call | solution.py:43
  46.0 6.1 %all-to-all-done.w_ref = bf16[64,72,128]{2,1,0:T(8,128)(2,1)S(1)} async-done(((bf16[64,72,128]{2,1,0:T(8,128)(2,1)}), bf16[64,72,128]{2,1,0:T(8,128)(2,1)S(1)}, u32[]{:S(2)}, u32[]{:S(2)}) %all-to-all-start) | async-done | bytes 1179680 | tf_op jit(solution)/shard_map/all_to_all | solution.py:237
  52.1 1.8 %shard_map.107.mine_ref.after_ref = bf16[4,512,128]{2,1,0:T(8,128)(2,1)S(1)} custom-call(s32[3]{0:T(128)S(1)} %copy-done.1, bf16[64,72,128]{2,1,0:T(8,128)(2,1)S(1)} %all-to-all-done.w_ref, bf16[512,1024]{1,0:T(8,128)(2,1)S(1)} %get-tuple-element.16.xb_ref), custom_call_target="tpu_custom_call" | custom-call | flops 600000000 | bytes 3000000 | tf_op jit(solution)/shard_map/pallas_call | solution.py:43
  53.9 1.9 %collective-permute-start.1 = (bf16[4,512,128]{2,1,0:T(8,128)(2,1)S(1)}, bf16[4,512,128]{2,1,0:T(8,128)(2,1)S(1)}, u32[]{:S(2)}, u32[]{:S(2)}) collective-permute-start(bf16[4,512,128]{2,1,0:T(8,128)(2,1)S(1)} %shard_map.107.mine_ref.after_ref), channel_id=1, source_target_pairs={{0,1},{1,0},{2,3},{3,2},{4,5},{5,4},{6,7},{7,6},{8,9},{9,8},{10,11... | collective-permute-start | bytes 1572872 | tf_op jit(solution)/shard_map/ppermute | solution.py:225
  55.8 1.9 %shard_map.109 = bf16[4,1024,128]{2,1,0:T(8,128)(2,1)} custom-call(bf16[64,72,128]{2,1,0:T(8,128)(2,1)S(1)} %all-to-all-done.w_ref, bf16[512,1024]{1,0:T(8,128)(2,1)S(1)} %get-tuple-element.16.xb_ref, bf16[512,640]{1,0:T(8,128)(2,1)S(1)} %get-tuple-element.18.dv_ref, bf16[4,512,128]{2,1,0:T(8,128)(2,1)S(1)} %shard_map.107.mine_ref.after_ref), custom_call_target="tpu_custom_call" | custom-call | flops 600000000 | bytes 3000000 | tf_op jit(solution)/shard_map/pallas_call | solution.py:43
  57.7 0.0 collective-permute-done.1.other_ref
  57.7 0.6 shard_map.108
  58.4 0.0 copy-start.6
  58.4 0.0 copy-start
  58.4 3.7 %all-to-all-start.1 = ((bf16[4,1024,128]{2,1,0:T(8,128)(2,1)}), bf16[4,1024,128]{2,1,0:T(8,128)(2,1)S(1)}, u32[]{:S(2)}, u32[]{:S(2)}) async-start(bf16[4,1024,128]{2,1,0:T(8,128)(2,1)} %shard_map.109), calls=%async_computation.1 | async-start | bytes 2097152 | tf_op jit(solution)/shard_map/all_to_all | solution.py:237
  62.1 3.4 %collective-permute-start.2 = (bf16[512,128]{1,0:T(8,128)(2,1)S(1)}, bf16[512,128]{1,0:T(8,128)(2,1)S(1)}, u32[]{:S(2)}, u32[]{:S(2)}) collective-permute-start(bf16[512,128]{1,0:T(8,128)(2,1)S(1)} %get-tuple-element.20), channel_id=1, source_target_pairs={{0,2},{1,7},{2,4},{3,1},{4,6},{5,3},{6,0},{7,5},{8,10},{9,15},{10,... | collective-permute-start | bytes 393224 | tf_op jit(solution)/shard_map/ppermute | solution.py:229
  65.5 4.6 %collective-permute-start.3 = (bf16[256,128]{1,0:T(8,128)(2,1)S(1)}, bf16[256,128]{1,0:T(8,128)(2,1)S(1)}, u32[]{:S(2)}, u32[]{:S(2)}) collective-permute-start(bf16[256,128]{1,0:T(8,128)(2,1)S(1)} %get-tuple-element.21), channel_id=1, source_target_pairs={{0,4},{1,5},{2,6},{3,7},{4,0},{5,1},{6,2},{7,3},{8,12},{9,13},{10,... | collective-permute-start | bytes 196616 | tf_op jit(solution)/shard_map/ppermute | solution.py:233
  70.1 0.0 copy-done.6
  70.1 1.0 shard_map.110
  71.1 2.2 %collective-permute-done.3.far_ref = bf16[256,128]{1,0:T(8,128)(2,1)S(1)} collective-permute-done((bf16[256,128]{1,0:T(8,128)(2,1)S(1)}, bf16[256,128]{1,0:T(8,128)(2,1)S(1)}, u32[]{:S(2)}, u32[]{:S(2)}) %collective-permute-start.3) | collective-permute-done | bytes 65568 | tf_op jit(solution)/shard_map/ppermute | solution.py:233
  73.4 0.0 collective-permute-done.2.next_ref
  73.4 0.6 shard_map.111.r1_ref
  74.0 2.2 %collective-permute-start.4 = (bf16[512,128]{1,0:T(8,128)(2,1)S(1)}, bf16[512,128]{1,0:T(8,128)(2,1)S(1)}, u32[]{:S(2)}, u32[]{:S(2)}) collective-permute-start(bf16[512,128]{1,0:T(8,128)(2,1)S(1)} %shard_map.111.r1_ref), channel_id=1, source_target_pairs={{0,1},{1,0},{2,3},{3,2},{4,5},{5,4},{6,7},{7,6},{8,9},{9,8},{10,11... | collective-permute-start | bytes 393224 | tf_op jit(solution)/shard_map/ppermute | solution.py:225
  76.1 1.1 collective-permute-done.4.r2_ref
  77.2 0.0 all-to-all-done.1.near_ref
  77.2 0.0 copy-done
  77.2 0.2 shard_map.112
  77.4 26.8 %all_to_all.15.got_ref = bf16[64,32,128]{2,1,0:T(8,128)(2,1)S(1)} all-to-all(bf16[64,32,128]{2,1,0:T(8,128)(2,1)S(1)} %shard_map.112), channel_id=1, replica_groups=mesh['dp'=64,'mp'=8] {'dp'}, dimensions={0} | all-to-all | bytes 1048576 | tf_op jit(solution)/shard_map/all_to_all | solution.py:237
  104.2 1.8 %shard_map.113 = (f32[16,512]{1,0:T(8,128)}, bf16[256,512]{1,0:T(8,128)(2,1)}) custom-call(bf16[64,32,128]{2,1,0:T(8,128)(2,1)S(1)} %all_to_all.15.got_ref, bf16[256,512]{1,0:T(8,128)(2,1)S(1)} %get-tuple-element.22.take_ref, bf16[256,512]{1,0:T(8,128)(2,1)S(1)} %get-tuple-element.23.same_ref), custom_call_target="tpu_custom_call" | custom-call | flops 600000000 | bytes 1000000 | tf_op jit(solution)/shard_map/pallas_call | solution.py:43
Async XLA Ops:
  2.6 49.5 %all-to-all-start = ((bf16[64,72,128]{2,1,0:T(8,128)(2,1)}), bf16[64,72,128]{2,1,0:T(8,128)(2,1)S(1)}, u32[]{:S(2)}, u32[]{:S(2)}) async-start(bf16[64,72,128]{2,1,0:T(8,128)(2,1)} %shard_map.104), calls=%async_computation | async-start | bytes 2359296 | tf_op jit(solution)/shard_map/all_to_all | solution.py:237
  19.8 23.4 %copy-start.1 = (s32[3]{0:T(128)S(1)}, s32[3]{0:T(128)}, u32[]{:S(2)}) copy-start(s32[3]{0:T(128)} %pad_add_fusion.where_ref) | copy-start | bytes 40
  19.8 23.4 %copy-start.2 = (s32[1,64]{1,0:T(1,128)S(1)}, s32[1,64]{1,0:T(1,128)}, u32[]{:S(2)}) copy-start(s32[1,64]{1,0:T(1,128)} %ok_ref.1) | copy-start | bytes 772
  19.8 23.4 %copy-start.3 = (s32[1,64]{1,0:T(1,128)S(1)}, s32[1,64]{1,0:T(1,128)}, u32[]{:S(2)}) copy-start(s32[1,64]{1,0:T(1,128)} %id_ref.1) | copy-start | bytes 772
  19.8 23.4 %copy-start.5 = (s32[64,64]{1,0:T(8,128)S(1)}, s32[64,64]{1,0:T(8,128)}, u32[]{:S(2)}) copy-start(s32[64,64]{1,0:T(8,128)} %plan_ref.3) | copy-start | bytes 49156
  25.7 3.5 %collective-permute-start = (bf16[512,128]{1,0:T(8,128)(2,1)}, bf16[512,128]{1,0:T(8,128)(2,1)S(1)}, u32[]{:S(2)}, u32[]{:S(2)}) collective-permute-start(bf16[512,128]{1,0:T(8,128)(2,1)} %get-tuple-element.15), channel_id=1, source_target_pairs={{0,1},{1,0},{2,3},{3,2},{4,5},{5,4},{6,7},{7,6},{8,9},{9,8},{10,11... | collective-permute-start | bytes 393224 | tf_op jit(solution)/shard_map/ppermute | solution.py:225
  43.2 1.2 %copy-start.4 = (bf16[512,1024]{1,0:T(8,128)(2,1)S(1)}, bf16[512,1024]{1,0:T(8,128)(2,1)}, u32[]{:S(2)}) copy-start(bf16[512,1024]{1,0:T(8,128)(2,1)} %x_ref.1) | copy-start | bytes 3145732
  53.9 3.8 %collective-permute-start.1 = (bf16[4,512,128]{2,1,0:T(8,128)(2,1)S(1)}, bf16[4,512,128]{2,1,0:T(8,128)(2,1)S(1)}, u32[]{:S(2)}, u32[]{:S(2)}) collective-permute-start(bf16[4,512,128]{2,1,0:T(8,128)(2,1)S(1)} %shard_map.107.mine_ref.after_ref), channel_id=1, source_target_pairs={{0,1},{1,0},{2,3},{3,2},{4,5},{5,4},{6,7},{7,6},{8,9},{9,8},{10,11... | collective-permute-start | bytes 1572872 | tf_op jit(solution)/shard_map/ppermute | solution.py:225
  58.4 11.7 %copy-start.6 = (s32[64,64]{1,0:T(8,128)S(1)}, s32[64,64]{1,0:T(8,128)}, u32[]{:S(2)}) copy-start(s32[64,64]{1,0:T(8,128)} %len_ref.3) | copy-start | bytes 49156
  58.4 18.8 %copy-start = (bf16[512,128]{1,0:T(8,128)(2,1)S(1)}, bf16[512,128]{1,0:T(8,128)(2,1)}, u32[]{:S(2)}) copy-start(bf16[512,128]{1,0:T(8,128)(2,1)} %get-tuple-element.25.pr_ref) | copy-start | bytes 393220
  58.4 18.8 %all-to-all-start.1 = ((bf16[4,1024,128]{2,1,0:T(8,128)(2,1)}), bf16[4,1024,128]{2,1,0:T(8,128)(2,1)S(1)}, u32[]{:S(2)}, u32[]{:S(2)}) async-start(bf16[4,1024,128]{2,1,0:T(8,128)(2,1)} %shard_map.109), calls=%async_computation.1 | async-start | bytes 2097152 | tf_op jit(solution)/shard_map/all_to_all | solution.py:237
  62.1 11.3 %collective-permute-start.2 = (bf16[512,128]{1,0:T(8,128)(2,1)S(1)}, bf16[512,128]{1,0:T(8,128)(2,1)S(1)}, u32[]{:S(2)}, u32[]{:S(2)}) collective-permute-start(bf16[512,128]{1,0:T(8,128)(2,1)S(1)} %get-tuple-element.20), channel_id=1, source_target_pairs={{0,2},{1,7},{2,4},{3,1},{4,6},{5,3},{6,0},{7,5},{8,10},{9,15},{10,... | collective-permute-start | bytes 393224 | tf_op jit(solution)/shard_map/ppermute | solution.py:229
  65.5 7.9 %collective-permute-start.3 = (bf16[256,128]{1,0:T(8,128)(2,1)S(1)}, bf16[256,128]{1,0:T(8,128)(2,1)S(1)}, u32[]{:S(2)}, u32[]{:S(2)}) collective-permute-start(bf16[256,128]{1,0:T(8,128)(2,1)S(1)} %get-tuple-element.21), channel_id=1, source_target_pairs={{0,4},{1,5},{2,6},{3,7},{4,0},{5,1},{6,2},{7,3},{8,12},{9,13},{10,... | collective-permute-start | bytes 196616 | tf_op jit(solution)/shard_map/ppermute | solution.py:233
  74.0 3.2 %collective-permute-start.4 = (bf16[512,128]{1,0:T(8,128)(2,1)S(1)}, bf16[512,128]{1,0:T(8,128)(2,1)S(1)}, u32[]{:S(2)}, u32[]{:S(2)}) collective-permute-start(bf16[512,128]{1,0:T(8,128)(2,1)S(1)} %shard_map.111.r1_ref), channel_id=1, source_target_pairs={{0,1},{1,0},{2,3},{3,2},{4,5},{5,4},{6,7},{7,6},{8,9},{9,8},{10,11... | collective-permute-start | bytes 393224 | tf_op jit(solution)/shard_map/ppermute | solution.py:225

commit v5 on v4

--- a/solution.py
+++ b/solution.py
@@ -140,10 +140,14 @@
 
 def project(where_ref, w_ref, xb_ref, out_ref):
     xpos = where_ref[1]
+    blocks = []
     for i in range(KEY_HEADS):
         m = lax.rem(xpos + i, KEY_HEADS)
         w = w_ref[:, pl.ds(pl.multiple_of(m * WROWS, WROWS), WROWS), :].reshape(FEATS, HEAD)
-        out_ref[i] = dot(xb_ref[...], w).astype(bf16)
+        blocks.append(w)
+    part = dot(xb_ref[...], jnp.concatenate(blocks, axis=1)).astype(bf16)
+    for i in range(KEY_HEADS):
+        out_ref[i] = part[:, i * HEAD : (i + 1) * HEAD]
 
 
 def weight_gradient(w_ref, xb_ref, dv_ref, after_ref, out_ref):

time: 107 us -> 106 us (level)
  no operation moved by 1% of the time
where the time goes in v5:
time: 106 us; the launch traced here: 105 us
  blocking collectives  39.9 us (38%)
  starting transfers between devices  34.2 us (32%)
  Pallas kernels  16.7 us (16%)
  waiting for transfers between devices  11 us (10%)
  other arithmetic  1.61 us (2%)
  local copies, waits for them, and re-layouts  1.25 us (1%)
    all_to_all x1, blocking collectives, all_to_all(): lax.all_to_all(a, 'dp', split_axis=0, concat_axis=0, tiled=True, axis_ind...  26.8 us
    all_to_all x2, starting transfers between devices, all_to_all(): lax.all_to_all(a, 'dp', split_axis=0, concat_axis=0, tiled=True, axis_ind...  20.1 us
    pallas_call x10, Pallas kernels, call(): pl.pallas_call(body, out_shape=out_shape, in_specs=specs, out_specs=jax.t...  16.7 us
    all_gather x1, blocking collectives, per_device(): lax.all_gather(dv, 'mp', axis_index_groups=[[0, 2, 4, 6], [1, 3, 5, 7]])  13.1 us
    all_to_all x2, waiting for transfers between devices, all_to_all(): lax.all_to_all(a, 'dp', split_axis=0, concat_axis=0, tiled=True, axis_ind...  6.13 us
    ppermute x3, starting transfers between devices, swap_cores(): return lax.ppermute(a, 'mp', [(p, p ^ 1) for p in range(8)])  6.01 us
    ppermute x1, starting transfers between devices, to_far_chip(): return lax.ppermute(a, 'mp', [(p, (p + 4) % 8) for p in range(8)])  4.64 us
    ppermute x1, starting transfers between devices, to_next_chips(): lax.ppermute(a, 'mp', [(p, (p + (2, -2)[p % 2]) % 8) for p in range(8)])  3.4 us
  transfers between devices with their start and end apart: 7, of which 4 were waited for; matrix products, arithmetic and copies ran while one was open for 2% of the time, Pallas kernels for 10%

profile of v5, /device:TPU:16, one launch (start us, length us, event | category | flops | bytes accessed | tf_op | source)
XLA Modules:
  0.0 105.5 jit_solution(13342216797625118210)
XLA Ops:
  0.6 2.0 %shard_map.104 = bf16[64,72,128]{2,1,0:T(8,128)(2,1)} custom-call(bf16[16,512]{1,0:T(8,128)(2,1)} %wm_hbm.1, s32[1,64]{1,0:T(1,128)} %ok_ref.1, s32[1,64]{1,0:T(1,128)} %id_ref.1), custom_call_target="tpu_custom_call" | custom-call | flops 1000000 | bytes 1000000 | tf_op jit(solution)/shard_map/pallas_call | solution.py:43
  2.6 16.5 %all-to-all-start = ((bf16[64,72,128]{2,1,0:T(8,128)(2,1)}), bf16[64,72,128]{2,1,0:T(8,128)(2,1)S(1)}, u32[]{:S(2)}, u32[]{:S(2)}) async-start(bf16[64,72,128]{2,1,0:T(8,128)(2,1)} %shard_map.104), calls=%async_computation | async-start | bytes 2359296 | tf_op jit(solution)/shard_map/all_to_all | solution.py:241
  19.1 0.7 pad_add_fusion.where_ref
  19.8 0.0 copy-start.1
  19.8 0.0 copy-start.2
  19.8 0.0 copy-start.3
  19.8 0.0 copy-start.5
  19.8 5.9 %shard_map.105 = (bf16[512,128]{1,0:T(8,128)(2,1)}, bf16[512,128]{1,0:T(8,128)(2,1)}) custom-call(s32[3]{0:T(128)} %pad_add_fusion.where_ref, bf16[512,512]{1,0:T(8,128)(2,1)} %q_hbm.1, bf16[512,512]{1,0:T(8,128)(2,1)} %k_hbm.1, bf16[512,512]{1,0:T(8,128)(2,1)} %g_hbm.1, s32[64,64]{1,0:T(8,128)} %len_ref.3, s32[64,64]{1,0:T(8,128)} %plan_ref.3), custom_call_target="tpu_custom_call" | custom-call | flops 2000000000 | bytes 2000000 | tf_op jit(solution)/shard_map/pallas_call | solution.py:43
  25.7 1.9 %collective-permute-start = (bf16[512,128]{1,0:T(8,128)(2,1)}, bf16[512,128]{1,0:T(8,128)(2,1)S(1)}, u32[]{:S(2)}, u32[]{:S(2)}) collective-permute-start(bf16[512,128]{1,0:T(8,128)(2,1)} %get-tuple-element.15), channel_id=1, source_target_pairs={{0,1},{1,0},{2,3},{3,2},{4,5},{5,4},{6,7},{7,6},{8,9},{9,8},{10,11... | collective-permute-start | bytes 393224 | tf_op jit(solution)/shard_map/ppermute | solution.py:229
  27.6 1.5 %collective-permute-done = bf16[512,128]{1,0:T(8,128)(2,1)S(1)} collective-permute-done((bf16[512,128]{1,0:T(8,128)(2,1)}, bf16[512,128]{1,0:T(8,128)(2,1)S(1)}, u32[]{:S(2)}, u32[]{:S(2)}) %collective-permute-start) | collective-permute-done | bytes 131104 | tf_op jit(solution)/shard_map/ppermute | solution.py:229
  29.1 0.9 add_convert_fusion
  30.1 13.1 %all-gather = bf16[2048,128]{1,0:T(8,128)(2,1)S(1)} all-gather(bf16[512,128]{1,0:T(8,128)(2,1)S(1)} %add_convert_fusion), channel_id=2, replica_groups={{0,2,4,6},{1,3,5,7},{8,10,12,14},{9,11,13,15},{16,18,20,22},{17,19,21,2..., dimensions={0}, use_global_device_ids=true | all-gather | bytes 655360 | tf_op jit(solution)/shard_map/all_gather | solution.py:283
  43.2 0.0 copy-done.1
  43.2 0.0 copy-done.2
  43.2 0.0 copy-done.3
  43.2 0.0 copy-done.5
  43.2 0.0 copy-start.4
  43.3 1.2 %copy-done.4 = bf16[512,1024]{1,0:T(8,128)(2,1)S(1)} copy-done((bf16[512,1024]{1,0:T(8,128)(2,1)S(1)}, bf16[512,1024]{1,0:T(8,128)(2,1)}, u32[]{:S(2)}) %copy-start.4) | copy-done | bytes 1048600
  44.5 1.5 %shard_map.106 = (bf16[512,1024]{1,0:T(8,128)(2,1)S(1)}, bf16[512,640]{1,0:T(8,128)(2,1)S(1)}) custom-call(s32[3]{0:T(128)S(1)} %copy-done.1, bf16[512,1024]{1,0:T(8,128)(2,1)S(1)} %copy-done.4, s32[64,64]{1,0:T(8,128)S(1)} %copy-done.5, s32[1,64]{1,0:T(1,128)S(1)} %copy-done.2, s32[1,64]{1,0:T(1,128)S(1)} %copy-done.3, bf16[4,512,128]{2,1,0:T(8,128)(2,1)S(1)} %bitcast.4), custom_call_target="tpu_custom_call" | custom-call | flops 600000000 | bytes 4000000 | tf_op jit(solution)/shard_map/pallas_call | solution.py:43
  46.0 6.1 %all-to-all-done.w_ref = bf16[64,72,128]{2,1,0:T(8,128)(2,1)S(1)} async-done(((bf16[64,72,128]{2,1,0:T(8,128)(2,1)}), bf16[64,72,128]{2,1,0:T(8,128)(2,1)S(1)}, u32[]{:S(2)}, u32[]{:S(2)}) %all-to-all-start) | async-done | bytes 1179680 | tf_op jit(solution)/shard_map/all_to_all | solution.py:241
  52.1 1.3 %shard_map.107.mine_ref.after_ref = bf16[4,512,128]{2,1,0:T(8,128)(2,1)S(1)} custom-call(s32[3]{0:T(128)S(1)} %copy-done.1, bf16[64,72,128]{2,1,0:T(8,128)(2,1)S(1)} %all-to-all-done.w_ref, bf16[512,1024]{1,0:T(8,128)(2,1)S(1)} %get-tuple-element.16.xb_ref), custom_call_target="tpu_custom_call" | custom-call | flops 600000000 | bytes 3000000 | tf_op jit(solution)/shard_map/pallas_call | solution.py:43
  53.4 1.9 %collective-permute-start.1 = (bf16[4,512,128]{2,1,0:T(8,128)(2,1)S(1)}, bf16[4,512,128]{2,1,0:T(8,128)(2,1)S(1)}, u32[]{:S(2)}, u32[]{:S(2)}) collective-permute-start(bf16[4,512,128]{2,1,0:T(8,128)(2,1)S(1)} %shard_map.107.mine_ref.after_ref), channel_id=1, source_target_pairs={{0,1},{1,0},{2,3},{3,2},{4,5},{5,4},{6,7},{7,6},{8,9},{9,8},{10,11... | collective-permute-start | bytes 1572872 | tf_op jit(solution)/shard_map/ppermute | solution.py:229
  55.3 1.9 %shard_map.109 = bf16[4,1024,128]{2,1,0:T(8,128)(2,1)} custom-call(bf16[64,72,128]{2,1,0:T(8,128)(2,1)S(1)} %all-to-all-done.w_ref, bf16[512,1024]{1,0:T(8,128)(2,1)S(1)} %get-tuple-element.16.xb_ref, bf16[512,640]{1,0:T(8,128)(2,1)S(1)} %get-tuple-element.18.dv_ref, bf16[4,512,128]{2,1,0:T(8,128)(2,1)S(1)} %shard_map.107.mine_ref.after_ref), custom_call_target="tpu_custom_call" | custom-call | flops 600000000 | bytes 3000000 | tf_op jit(solution)/shard_map/pallas_call | solution.py:43
  57.2 0.0 collective-permute-done.1.other_ref
  57.2 0.6 shard_map.108
  57.8 0.0 copy-start.6
  57.8 0.0 copy-start
  57.9 3.7 %all-to-all-start.1 = ((bf16[4,1024,128]{2,1,0:T(8,128)(2,1)}), bf16[4,1024,128]{2,1,0:T(8,128)(2,1)S(1)}, u32[]{:S(2)}, u32[]{:S(2)}) async-start(bf16[4,1024,128]{2,1,0:T(8,128)(2,1)} %shard_map.109), calls=%async_computation.1 | async-start | bytes 2097152 | tf_op jit(solution)/shard_map/all_to_all | solution.py:241
  61.5 3.4 %collective-permute-start.2 = (bf16[512,128]{1,0:T(8,128)(2,1)S(1)}, bf16[512,128]{1,0:T(8,128)(2,1)S(1)}, u32[]{:S(2)}, u32[]{:S(2)}) collective-permute-start(bf16[512,128]{1,0:T(8,128)(2,1)S(1)} %get-tuple-element.20), channel_id=1, source_target_pairs={{0,2},{1,7},{2,4},{3,1},{4,6},{5,3},{6,0},{7,5},{8,10},{9,15},{10,... | collective-permute-start | bytes 393224 | tf_op jit(solution)/shard_map/ppermute | solution.py:233
  64.9 4.6 %collective-permute-start.3 = (bf16[256,128]{1,0:T(8,128)(2,1)S(1)}, bf16[256,128]{1,0:T(8,128)(2,1)S(1)}, u32[]{:S(2)}, u32[]{:S(2)}) collective-permute-start(bf16[256,128]{1,0:T(8,128)(2,1)S(1)} %get-tuple-element.21), channel_id=1, source_target_pairs={{0,4},{1,5},{2,6},{3,7},{4,0},{5,1},{6,2},{7,3},{8,12},{9,13},{10,... | collective-permute-start | bytes 196616 | tf_op jit(solution)/shard_map/ppermute | solution.py:237
  69.6 0.0 copy-done.6
  69.6 1.0 shard_map.110
  70.6 2.2 %collective-permute-done.3.far_ref = bf16[256,128]{1,0:T(8,128)(2,1)S(1)} collective-permute-done((bf16[256,128]{1,0:T(8,128)(2,1)S(1)}, bf16[256,128]{1,0:T(8,128)(2,1)S(1)}, u32[]{:S(2)}, u32[]{:S(2)}) %collective-permute-start.3) | collective-permute-done | bytes 65568 | tf_op jit(solution)/shard_map/ppermute | solution.py:237
  72.8 0.0 collective-permute-done.2.next_ref
  72.8 0.6 shard_map.111.r1_ref
  73.4 2.2 %collective-permute-start.4 = (bf16[512,128]{1,0:T(8,128)(2,1)S(1)}, bf16[512,128]{1,0:T(8,128)(2,1)S(1)}, u32[]{:S(2)}, u32[]{:S(2)}) collective-permute-start(bf16[512,128]{1,0:T(8,128)(2,1)S(1)} %shard_map.111.r1_ref), channel_id=1, source_target_pairs={{0,1},{1,0},{2,3},{3,2},{4,5},{5,4},{6,7},{7,6},{8,9},{9,8},{10,11... | collective-permute-start | bytes 393224 | tf_op jit(solution)/shard_map/ppermute | solution.py:229
  75.6 1.1 %collective-permute-done.4.r2_ref = bf16[512,128]{1,0:T(8,128)(2,1)S(1)} collective-permute-done((bf16[512,128]{1,0:T(8,128)(2,1)S(1)}, bf16[512,128]{1,0:T(8,128)(2,1)S(1)}, u32[]{:S(2)}, u32[]{:S(2)}) %collective-permute-start.4) | collective-permute-done | bytes 131104 | tf_op jit(solution)/shard_map/ppermute | solution.py:229
  76.7 0.0 all-to-all-done.1.near_ref
  76.7 0.0 copy-done
  76.7 0.2 shard_map.112
  76.9 26.8 %all_to_all.15.got_ref = bf16[64,32,128]{2,1,0:T(8,128)(2,1)S(1)} all-to-all(bf16[64,32,128]{2,1,0:T(8,128)(2,1)S(1)} %shard_map.112), channel_id=1, replica_groups=mesh['dp'=64,'mp'=8] {'dp'}, dimensions={0} | all-to-all | bytes 1048576 | tf_op jit(solution)/shard_map/all_to_all | solution.py:241
  103.7 1.8 %shard_map.113 = (f32[16,512]{1,0:T(8,128)}, bf16[256,512]{1,0:T(8,128)(2,1)}) custom-call(bf16[64,32,128]{2,1,0:T(8,128)(2,1)S(1)} %all_to_all.15.got_ref, bf16[256,512]{1,0:T(8,128)(2,1)S(1)} %get-tuple-element.22.take_ref, bf16[256,512]{1,0:T(8,128)(2,1)S(1)} %get-tuple-element.23.same_ref), custom_call_target="tpu_custom_call" | custom-call | flops 600000000 | bytes 1000000 | tf_op jit(solution)/shard_map/pallas_call | solution.py:43
Async XLA Ops:
  2.6 49.5 %all-to-all-start = ((bf16[64,72,128]{2,1,0:T(8,128)(2,1)}), bf16[64,72,128]{2,1,0:T(8,128)(2,1)S(1)}, u32[]{:S(2)}, u32[]{:S(2)}) async-start(bf16[64,72,128]{2,1,0:T(8,128)(2,1)} %shard_map.104), calls=%async_computation | async-start | bytes 2359296 | tf_op jit(solution)/shard_map/all_to_all | solution.py:241
  19.8 23.4 %copy-start.1 = (s32[3]{0:T(128)S(1)}, s32[3]{0:T(128)}, u32[]{:S(2)}) copy-start(s32[3]{0:T(128)} %pad_add_fusion.where_ref) | copy-start | bytes 40
  19.8 23.4 %copy-start.2 = (s32[1,64]{1,0:T(1,128)S(1)}, s32[1,64]{1,0:T(1,128)}, u32[]{:S(2)}) copy-start(s32[1,64]{1,0:T(1,128)} %ok_ref.1) | copy-start | bytes 772
  19.8 23.4 %copy-start.3 = (s32[1,64]{1,0:T(1,128)S(1)}, s32[1,64]{1,0:T(1,128)}, u32[]{:S(2)}) copy-start(s32[1,64]{1,0:T(1,128)} %id_ref.1) | copy-start | bytes 772
  19.8 23.4 %copy-start.5 = (s32[64,64]{1,0:T(8,128)S(1)}, s32[64,64]{1,0:T(8,128)}, u32[]{:S(2)}) copy-start(s32[64,64]{1,0:T(8,128)} %plan_ref.3) | copy-start | bytes 49156
  25.7 3.5 %collective-permute-start = (bf16[512,128]{1,0:T(8,128)(2,1)}, bf16[512,128]{1,0:T(8,128)(2,1)S(1)}, u32[]{:S(2)}, u32[]{:S(2)}) collective-permute-start(bf16[512,128]{1,0:T(8,128)(2,1)} %get-tuple-element.15), channel_id=1, source_target_pairs={{0,1},{1,0},{2,3},{3,2},{4,5},{5,4},{6,7},{7,6},{8,9},{9,8},{10,11... | collective-permute-start | bytes 393224 | tf_op jit(solution)/shard_map/ppermute | solution.py:229
  43.2 1.2 %copy-start.4 = (bf16[512,1024]{1,0:T(8,128)(2,1)S(1)}, bf16[512,1024]{1,0:T(8,128)(2,1)}, u32[]{:S(2)}) copy-start(bf16[512,1024]{1,0:T(8,128)(2,1)} %x_ref.1) | copy-start | bytes 3145732
  53.4 3.8 %collective-permute-start.1 = (bf16[4,512,128]{2,1,0:T(8,128)(2,1)S(1)}, bf16[4,512,128]{2,1,0:T(8,128)(2,1)S(1)}, u32[]{:S(2)}, u32[]{:S(2)}) collective-permute-start(bf16[4,512,128]{2,1,0:T(8,128)(2,1)S(1)} %shard_map.107.mine_ref.after_ref), channel_id=1, source_target_pairs={{0,1},{1,0},{2,3},{3,2},{4,5},{5,4},{6,7},{7,6},{8,9},{9,8},{10,11... | collective-permute-start | bytes 1572872 | tf_op jit(solution)/shard_map/ppermute | solution.py:229
  57.8 11.7 %copy-start.6 = (s32[64,64]{1,0:T(8,128)S(1)}, s32[64,64]{1,0:T(8,128)}, u32[]{:S(2)}) copy-start(s32[64,64]{1,0:T(8,128)} %len_ref.3) | copy-start | bytes 49156
  57.8 18.8 %copy-start = (bf16[512,128]{1,0:T(8,128)(2,1)S(1)}, bf16[512,128]{1,0:T(8,128)(2,1)}, u32[]{:S(2)}) copy-start(bf16[512,128]{1,0:T(8,128)(2,1)} %get-tuple-element.25.pr_ref) | copy-start | bytes 393220
  57.9 18.8 %all-to-all-start.1 = ((bf16[4,1024,128]{2,1,0:T(8,128)(2,1)}), bf16[4,1024,128]{2,1,0:T(8,128)(2,1)S(1)}, u32[]{:S(2)}, u32[]{:S(2)}) async-start(bf16[4,1024,128]{2,1,0:T(8,128)(2,1)} %shard_map.109), calls=%async_computation.1 | async-start | bytes 2097152 | tf_op jit(solution)/shard_map/all_to_all | solution.py:241
  61.5 11.3 %collective-permute-start.2 = (bf16[512,128]{1,0:T(8,128)(2,1)S(1)}, bf16[512,128]{1,0:T(8,128)(2,1)S(1)}, u32[]{:S(2)}, u32[]{:S(2)}) collective-permute-start(bf16[512,128]{1,0:T(8,128)(2,1)S(1)} %get-tuple-element.20), channel_id=1, source_target_pairs={{0,2},{1,7},{2,4},{3,1},{4,6},{5,3},{6,0},{7,5},{8,10},{9,15},{10,... | collective-permute-start | bytes 393224 | tf_op jit(solution)/shard_map/ppermute | solution.py:233
  64.9 7.9 %collective-permute-start.3 = (bf16[256,128]{1,0:T(8,128)(2,1)S(1)}, bf16[256,128]{1,0:T(8,128)(2,1)S(1)}, u32[]{:S(2)}, u32[]{:S(2)}) collective-permute-start(bf16[256,128]{1,0:T(8,128)(2,1)S(1)} %get-tuple-element.21), channel_id=1, source_target_pairs={{0,4},{1,5},{2,6},{3,7},{4,0},{5,1},{6,2},{7,3},{8,12},{9,13},{10,... | collective-permute-start | bytes 196616 | tf_op jit(solution)/shard_map/ppermute | solution.py:237
  73.4 3.2 %collective-permute-start.4 = (bf16[512,128]{1,0:T(8,128)(2,1)S(1)}, bf16[512,128]{1,0:T(8,128)(2,1)S(1)}, u32[]{:S(2)}, u32[]{:S(2)}) collective-permute-start(bf16[512,128]{1,0:T(8,128)(2,1)S(1)} %shard_map.111.r1_ref), channel_id=1, source_target_pairs={{0,1},{1,0},{2,3},{3,2},{4,5},{5,4},{6,7},{7,6},{8,9},{9,8},{10,11... | collective-permute-start | bytes 393224 | tf_op jit(solution)/shard_map/ppermute | solution.py:229

commit v6 on v5

--- a/solution.py
+++ b/solution.py
@@ -163,24 +163,18 @@
 
 
 def add_cores(where_ref, mine_ref, other_ref, own_ref, next_ref, far_ref):
-    core = where_ref[2]
-    half = pl.ds(pl.multiple_of(core * (ROWS // 2), ROWS // 2), ROWS // 2)
     own_ref[...] = mine_ref[0].astype(f32) + other_ref[0].astype(f32)
-    to = 1 + 2 * core
+    to = 1 + 2 * where_ref[2]
     next_ref[...] = (mine_ref[to].astype(f32) + other_ref[to].astype(f32)).astype(bf16)
-    far_ref[...] = (mine_ref[2, half].astype(f32) + other_ref[2, half].astype(f32)).astype(bf16)
-
-
-def add_arrived(where_ref, next_ref, far_ref, take_ref, same_ref, out_ref):
-    half = pl.ds(pl.multiple_of(where_ref[2] * (ROWS // 2), ROWS // 2), ROWS // 2)
-    out_ref[...] = next_ref[...]
-    out_ref[half] = (next_ref[half].astype(f32) + far_ref[...].astype(f32)).astype(bf16)
-
-
-def assemble(own_ref, r1_ref, r2_ref, near_ref, pr_ref, out_ref):
+    far_ref[...] = (mine_ref[2].astype(f32) + other_ref[2].astype(f32)).astype(bf16)
+
+
+def assemble(own_ref, r1_ref, r2_ref, r3_ref, near_ref, pr_ref, take_ref, same_ref, out_ref):
     grad = jnp.sum(near_ref[...].astype(f32), axis=0).astype(bf16)
     out_ref[:, :WROWS, :] = grad.reshape(BINS, WROWS, HEAD)
-    value = own_ref[...] + r1_ref[...].astype(f32) + r2_ref[...].astype(f32)
+    value = own_ref[...]
+    for ref in (r1_ref, r2_ref, r3_ref):
+        value = value + ref[...].astype(f32)
     out_ref[:, WROWS : WROWS + LMAX, :] = value.astype(bf16).reshape(BINS, LMAX, HEAD)
     out_ref[:, WROWS + LMAX :, :] = pr_ref[...].reshape(BINS, LMAX, HEAD)
 
@@ -308,7 +302,7 @@
     )
     own, following, far = call(
         add_cores,
-        (struct((ROWS, HEAD), f32), rows, struct((ROWS // 2, HEAD), bf16)),
+        (struct((ROWS, HEAD), f32), rows, rows),
         (where, part, other_part),
         [SM] + [VM] * 2,
         10**6,
@@ -320,19 +314,13 @@
     take, same = call(
         place_rows, (square, square), (where, lengths), [SM, VM], 10**7, 10**6
     )
-    arrived = call(
-        add_arrived,
-        rows,
-        (where, to_next_chips(following), to_far_chip(far), take, same),
-        [SM] + [VM] * 2 + [HB] * 2,
-        10**6,
-        10**6,
-    )
+    arrived = to_next_chips(following)
+    from_far = to_far_chip(far)
     block = call(
         assemble,
         struct((BINS, WROWS + 2 * LMAX, HEAD), bf16),
-        (own, arrived, swap_cores(arrived), near, probs),
-        [VM] * 5,
+        (own, arrived, swap_cores(arrived), from_far, near, probs, take, same),
+        [VM] * 6 + [HB] * 2,
         10**6,
         3 * 10**6,
     )

time: 106 us -> 105 us (level)
    all_to_all x2, waiting for transfers between devices: 6.13 us -> 7.94 us  [all_to_all(): lax.all_to_all(a, 'dp', split_axis=0, concat_axis=0, tiled=True, axis_ind...]
    pallas_call x10 -> x9, Pallas kernels: 16.7 us -> 16.2 us  [call(): pl.pallas_call(body, out_shape=out_shape, in_specs=specs, out_specs=jax.t...]
where the time goes in v6:
time: 105 us; the launch traced here: 104 us
  blocking collectives  39.1 us (37%)
  starting transfers between devices  33.9 us (32%)
  Pallas kernels  16.2 us (15%)
  waiting for transfers between devices  11.2 us (11%)
  other arithmetic  1.61 us (2%)
  local copies, waits for them, and re-layouts  1.25 us (1%)
    all_to_all x1, blocking collectives, all_to_all(): lax.all_to_all(a, 'dp', split_axis=0, concat_axis=0, tiled=True, axis_ind...  26 us
    all_to_all x2, starting transfers between devices, all_to_all(): lax.all_to_all(a, 'dp', split_axis=0, concat_axis=0, tiled=True, axis_ind...  20.1 us
    pallas_call x9, Pallas kernels, call(): pl.pallas_call(body, out_shape=out_shape, in_specs=specs, out_specs=jax.t...  16.2 us
    all_gather x1, blocking collectives, per_device(): lax.all_gather(dv, 'mp', axis_index_groups=[[0, 2, 4, 6], [1, 3, 5, 7]])  13.1 us
    all_to_all x2, waiting for transfers between devices, all_to_all(): lax.all_to_all(a, 'dp', split_axis=0, concat_axis=0, tiled=True, axis_ind...  7.94 us
    ppermute x3, starting transfers between devices, swap_cores(): return lax.ppermute(a, 'mp', [(p, p ^ 1) for p in range(8)])  5.75 us
    ppermute x1, starting transfers between devices, to_far_chip(): return lax.ppermute(a, 'mp', [(p, (p + 4) % 8) for p in range(8)])  4.64 us
    ppermute x1, starting transfers between devices, to_next_chips(): lax.ppermute(a, 'mp', [(p, (p + (2, -2)[p % 2]) % 8) for p in range(8)])  3.4 us
  transfers between devices with their start and end apart: 7, of which 4 were waited for; matrix products, arithmetic and copies ran while one was open for 2% of the time, Pallas kernels for 10%

profile of v6, /device:TPU:16, one launch (start us, length us, event | category | flops | bytes accessed | tf_op | source)
XLA Modules:
  0.0 104.1 jit_solution(8273179298679245553)
XLA Ops:
  0.6 2.0 %shard_map.104 = bf16[64,72,128]{2,1,0:T(8,128)(2,1)} custom-call(bf16[16,512]{1,0:T(8,128)(2,1)} %wm_hbm.1, s32[1,64]{1,0:T(1,128)} %ok_ref.1, s32[1,64]{1,0:T(1,128)} %id_ref.1), custom_call_target="tpu_custom_call" | custom-call | flops 1000000 | bytes 1000000 | tf_op jit(solution)/shard_map/pallas_call | solution.py:43
  2.6 16.5 %all-to-all-start = ((bf16[64,72,128]{2,1,0:T(8,128)(2,1)}), bf16[64,72,128]{2,1,0:T(8,128)(2,1)S(1)}, u32[]{:S(2)}, u32[]{:S(2)}) async-start(bf16[64,72,128]{2,1,0:T(8,128)(2,1)} %shard_map.104), calls=%async_computation | async-start | bytes 2359296 | tf_op jit(solution)/shard_map/all_to_all | solution.py:235
  19.1 0.7 pad_add_fusion.where_ref
  19.8 0.0 copy-start.1
  19.8 0.0 copy-start.2
  19.8 0.0 copy-start.3
  19.8 0.0 copy-start.5
  19.8 5.9 %shard_map.105 = (bf16[512,128]{1,0:T(8,128)(2,1)}, bf16[512,128]{1,0:T(8,128)(2,1)}) custom-call(s32[3]{0:T(128)} %pad_add_fusion.where_ref, bf16[512,512]{1,0:T(8,128)(2,1)} %q_hbm.1, bf16[512,512]{1,0:T(8,128)(2,1)} %k_hbm.1, bf16[512,512]{1,0:T(8,128)(2,1)} %g_hbm.1, s32[64,64]{1,0:T(8,128)} %len_ref.3, s32[64,64]{1,0:T(8,128)} %plan_ref.3), custom_call_target="tpu_custom_call" | custom-call | flops 2000000000 | bytes 2000000 | tf_op jit(solution)/shard_map/pallas_call | solution.py:43
  25.7 1.9 %collective-permute-start = (bf16[512,128]{1,0:T(8,128)(2,1)}, bf16[512,128]{1,0:T(8,128)(2,1)S(1)}, u32[]{:S(2)}, u32[]{:S(2)}) collective-permute-start(bf16[512,128]{1,0:T(8,128)(2,1)} %get-tuple-element.15), channel_id=1, source_target_pairs={{0,1},{1,0},{2,3},{3,2},{4,5},{5,4},{6,7},{7,6},{8,9},{9,8},{10,11... | collective-permute-start | bytes 393224 | tf_op jit(solution)/shard_map/ppermute | solution.py:223
  27.6 1.5 %collective-permute-done = bf16[512,128]{1,0:T(8,128)(2,1)S(1)} collective-permute-done((bf16[512,128]{1,0:T(8,128)(2,1)}, bf16[512,128]{1,0:T(8,128)(2,1)S(1)}, u32[]{:S(2)}, u32[]{:S(2)}) %collective-permute-start) | collective-permute-done | bytes 131104 | tf_op jit(solution)/shard_map/ppermute | solution.py:223
  29.1 0.9 add_convert_fusion
  30.1 13.1 %all-gather = bf16[2048,128]{1,0:T(8,128)(2,1)S(1)} all-gather(bf16[512,128]{1,0:T(8,128)(2,1)S(1)} %add_convert_fusion), channel_id=2, replica_groups={{0,2,4,6},{1,3,5,7},{8,10,12,14},{9,11,13,15},{16,18,20,22},{17,19,21,2..., dimensions={0}, use_global_device_ids=true | all-gather | bytes 655360 | tf_op jit(solution)/shard_map/all_gather | solution.py:277
  43.2 0.0 copy-done.1
  43.2 0.0 copy-done.2
  43.2 0.0 copy-done.3
  43.2 0.0 copy-done.5
  43.2 0.0 copy-start.4
  43.3 1.2 %copy-done.4 = bf16[512,1024]{1,0:T(8,128)(2,1)S(1)} copy-done((bf16[512,1024]{1,0:T(8,128)(2,1)S(1)}, bf16[512,1024]{1,0:T(8,128)(2,1)}, u32[]{:S(2)}) %copy-start.4) | copy-done | bytes 1048600
  44.5 1.5 %shard_map.106 = (bf16[512,1024]{1,0:T(8,128)(2,1)S(1)}, bf16[512,640]{1,0:T(8,128)(2,1)S(1)}) custom-call(s32[3]{0:T(128)S(1)} %copy-done.1, bf16[512,1024]{1,0:T(8,128)(2,1)S(1)} %copy-done.4, s32[64,64]{1,0:T(8,128)S(1)} %copy-done.5, s32[1,64]{1,0:T(1,128)S(1)} %copy-done.2, s32[1,64]{1,0:T(1,128)S(1)} %copy-done.3, bf16[4,512,128]{2,1,0:T(8,128)(2,1)S(1)} %bitcast.4), custom_call_target="tpu_custom_call" | custom-call | flops 600000000 | bytes 4000000 | tf_op jit(solution)/shard_map/pallas_call | solution.py:43
  46.0 6.1 %all-to-all-done.w_ref = bf16[64,72,128]{2,1,0:T(8,128)(2,1)S(1)} async-done(((bf16[64,72,128]{2,1,0:T(8,128)(2,1)}), bf16[64,72,128]{2,1,0:T(8,128)(2,1)S(1)}, u32[]{:S(2)}, u32[]{:S(2)}) %all-to-all-start) | async-done | bytes 1179680 | tf_op jit(solution)/shard_map/all_to_all | solution.py:235
  52.1 1.3 %shard_map.107.mine_ref.after_ref = bf16[4,512,128]{2,1,0:T(8,128)(2,1)S(1)} custom-call(s32[3]{0:T(128)S(1)} %copy-done.1, bf16[64,72,128]{2,1,0:T(8,128)(2,1)S(1)} %all-to-all-done.w_ref, bf16[512,1024]{1,0:T(8,128)(2,1)S(1)} %get-tuple-element.16.xb_ref), custom_call_target="tpu_custom_call" | custom-call | flops 600000000 | bytes 3000000 | tf_op jit(solution)/shard_map/pallas_call | solution.py:43
  53.4 1.9 %collective-permute-start.1 = (bf16[4,512,128]{2,1,0:T(8,128)(2,1)S(1)}, bf16[4,512,128]{2,1,0:T(8,128)(2,1)S(1)}, u32[]{:S(2)}, u32[]{:S(2)}) collective-permute-start(bf16[4,512,128]{2,1,0:T(8,128)(2,1)S(1)} %shard_map.107.mine_ref.after_ref), channel_id=1, source_target_pairs={{0,1},{1,0},{2,3},{3,2},{4,5},{5,4},{6,7},{7,6},{8,9},{9,8},{10,11... | collective-permute-start | bytes 1572872 | tf_op jit(solution)/shard_map/ppermute | solution.py:223
  55.3 1.9 %shard_map.109 = bf16[4,1024,128]{2,1,0:T(8,128)(2,1)} custom-call(bf16[64,72,128]{2,1,0:T(8,128)(2,1)S(1)} %all-to-all-done.w_ref, bf16[512,1024]{1,0:T(8,128)(2,1)S(1)} %get-tuple-element.16.xb_ref, bf16[512,640]{1,0:T(8,128)(2,1)S(1)} %get-tuple-element.18.dv_ref, bf16[4,512,128]{2,1,0:T(8,128)(2,1)S(1)} %shard_map.107.mine_ref.after_ref), custom_call_target="tpu_custom_call" | custom-call | flops 600000000 | bytes 3000000 | tf_op jit(solution)/shard_map/pallas_call | solution.py:43
  57.2 0.0 collective-permute-done.1.other_ref
  57.2 0.6 shard_map.108
  57.8 0.0 copy-start.6
  57.9 0.0 copy-start
  57.9 3.7 %all-to-all-start.1 = ((bf16[4,1024,128]{2,1,0:T(8,128)(2,1)}), bf16[4,1024,128]{2,1,0:T(8,128)(2,1)S(1)}, u32[]{:S(2)}, u32[]{:S(2)}) async-start(bf16[4,1024,128]{2,1,0:T(8,128)(2,1)} %shard_map.109), calls=%async_computation.1 | async-start | bytes 2097152 | tf_op jit(solution)/shard_map/all_to_all | solution.py:235
  61.5 3.4 %collective-permute-start.2 = (bf16[512,128]{1,0:T(8,128)(2,1)S(1)}, bf16[512,128]{1,0:T(8,128)(2,1)S(1)}, u32[]{:S(2)}, u32[]{:S(2)}) collective-permute-start(bf16[512,128]{1,0:T(8,128)(2,1)S(1)} %get-tuple-element.20), channel_id=1, source_target_pairs={{0,2},{1,7},{2,4},{3,1},{4,6},{5,3},{6,0},{7,5},{8,10},{9,15},{10,... | collective-permute-start | bytes 393224 | tf_op jit(solution)/shard_map/ppermute | solution.py:227
  64.9 4.6 %collective-permute-start.4 = (bf16[512,128]{1,0:T(8,128)(2,1)S(1)}, bf16[512,128]{1,0:T(8,128)(2,1)S(1)}, u32[]{:S(2)}, u32[]{:S(2)}) collective-permute-start(bf16[512,128]{1,0:T(8,128)(2,1)S(1)} %get-tuple-element.21), channel_id=1, source_target_pairs={{0,4},{1,5},{2,6},{3,7},{4,0},{5,1},{6,2},{7,3},{8,12},{9,13},{10,... | collective-permute-start | bytes 393224 | tf_op jit(solution)/shard_map/ppermute | solution.py:231
  69.6 0.0 collective-permute-done.2.r1_ref
  69.6 1.9 %collective-permute-start.3 = (bf16[512,128]{1,0:T(8,128)(2,1)S(1)}, bf16[512,128]{1,0:T(8,128)(2,1)S(1)}, u32[]{:S(2)}, u32[]{:S(2)}) collective-permute-start(bf16[512,128]{1,0:T(8,128)(2,1)S(1)} %collective-permute-done.2.r1_ref), channel_id=1, source_target_pairs={{0,1},{1,0},{2,3},{3,2},{4,5},{5,4},{6,7},{7,6},{8,9},{9,8},{10,11... | collective-permute-start | bytes 393224 | tf_op jit(solution)/shard_map/ppermute | solution.py:223
  71.5 0.0 copy-done.6
  71.5 1.0 shard_map.110
  72.5 1.7 %collective-permute-done.4.r3_ref = bf16[512,128]{1,0:T(8,128)(2,1)S(1)} collective-permute-done((bf16[512,128]{1,0:T(8,128)(2,1)S(1)}, bf16[512,128]{1,0:T(8,128)(2,1)S(1)}, u32[]{:S(2)}, u32[]{:S(2)}) %collective-permute-start.4) | collective-permute-done | bytes 131104 | tf_op jit(solution)/shard_map/ppermute | solution.py:231
  74.3 0.0 collective-permute-done.3.r2_ref
  74.3 1.8 %all-to-all-done.1.near_ref = bf16[4,1024,128]{2,1,0:T(8,128)(2,1)S(1)} async-done(((bf16[4,1024,128]{2,1,0:T(8,128)(2,1)}), bf16[4,1024,128]{2,1,0:T(8,128)(2,1)S(1)}, u32[]{:S(2)}, u32[]{:S(2)}) %all-to-all-start.1) | async-done | bytes 1048608 | tf_op jit(solution)/shard_map/all_to_all | solution.py:235
  76.1 0.0 copy-done
  76.1 0.2 shard_map.111
  76.3 26.0 %all_to_all.15.got_ref = bf16[64,32,128]{2,1,0:T(8,128)(2,1)S(1)} all-to-all(bf16[64,32,128]{2,1,0:T(8,128)(2,1)S(1)} %shard_map.111), channel_id=1, replica_groups=mesh['dp'=64,'mp'=8] {'dp'}, dimensions={0} | all-to-all | bytes 1048576 | tf_op jit(solution)/shard_map/all_to_all | solution.py:235
  102.3 1.8 %shard_map.112 = (f32[16,512]{1,0:T(8,128)}, bf16[256,512]{1,0:T(8,128)(2,1)}) custom-call(bf16[64,32,128]{2,1,0:T(8,128)(2,1)S(1)} %all_to_all.15.got_ref, bf16[256,512]{1,0:T(8,128)(2,1)S(1)} %get-tuple-element.24.take_ref, bf16[256,512]{1,0:T(8,128)(2,1)S(1)} %get-tuple-element.25.same_ref), custom_call_target="tpu_custom_call" | custom-call | flops 600000000 | bytes 1000000 | tf_op jit(solution)/shard_map/pallas_call | solution.py:43
Async XLA Ops:
  2.6 49.5 %all-to-all-start = ((bf16[64,72,128]{2,1,0:T(8,128)(2,1)}), bf16[64,72,128]{2,1,0:T(8,128)(2,1)S(1)}, u32[]{:S(2)}, u32[]{:S(2)}) async-start(bf16[64,72,128]{2,1,0:T(8,128)(2,1)} %shard_map.104), calls=%async_computation | async-start | bytes 2359296 | tf_op jit(solution)/shard_map/all_to_all | solution.py:235
  19.8 23.4 %copy-start.1 = (s32[3]{0:T(128)S(1)}, s32[3]{0:T(128)}, u32[]{:S(2)}) copy-start(s32[3]{0:T(128)} %pad_add_fusion.where_ref) | copy-start | bytes 40
  19.8 23.4 %copy-start.2 = (s32[1,64]{1,0:T(1,128)S(1)}, s32[1,64]{1,0:T(1,128)}, u32[]{:S(2)}) copy-start(s32[1,64]{1,0:T(1,128)} %ok_ref.1) | copy-start | bytes 772
  19.8 23.4 %copy-start.3 = (s32[1,64]{1,0:T(1,128)S(1)}, s32[1,64]{1,0:T(1,128)}, u32[]{:S(2)}) copy-start(s32[1,64]{1,0:T(1,128)} %id_ref.1) | copy-start | bytes 772
  19.8 23.4 %copy-start.5 = (s32[64,64]{1,0:T(8,128)S(1)}, s32[64,64]{1,0:T(8,128)}, u32[]{:S(2)}) copy-start(s32[64,64]{1,0:T(8,128)} %plan_ref.3) | copy-start | bytes 49156
  25.7 3.5 %collective-permute-start = (bf16[512,128]{1,0:T(8,128)(2,1)}, bf16[512,128]{1,0:T(8,128)(2,1)S(1)}, u32[]{:S(2)}, u32[]{:S(2)}) collective-permute-start(bf16[512,128]{1,0:T(8,128)(2,1)} %get-tuple-element.15), channel_id=1, source_target_pairs={{0,1},{1,0},{2,3},{3,2},{4,5},{5,4},{6,7},{7,6},{8,9},{9,8},{10,11... | collective-permute-start | bytes 393224 | tf_op jit(solution)/shard_map/ppermute | solution.py:223
  43.2 1.2 %copy-start.4 = (bf16[512,1024]{1,0:T(8,128)(2,1)S(1)}, bf16[512,1024]{1,0:T(8,128)(2,1)}, u32[]{:S(2)}) copy-start(bf16[512,1024]{1,0:T(8,128)(2,1)} %x_ref.1) | copy-start | bytes 3145732
  53.4 3.8 %collective-permute-start.1 = (bf16[4,512,128]{2,1,0:T(8,128)(2,1)S(1)}, bf16[4,512,128]{2,1,0:T(8,128)(2,1)S(1)}, u32[]{:S(2)}, u32[]{:S(2)}) collective-permute-start(bf16[4,512,128]{2,1,0:T(8,128)(2,1)S(1)} %shard_map.107.mine_ref.after_ref), channel_id=1, source_target_pairs={{0,1},{1,0},{2,3},{3,2},{4,5},{5,4},{6,7},{7,6},{8,9},{9,8},{10,11... | collective-permute-start | bytes 1572872 | tf_op jit(solution)/shard_map/ppermute | solution.py:223
  57.8 13.7 %copy-start.6 = (s32[64,64]{1,0:T(8,128)S(1)}, s32[64,64]{1,0:T(8,128)}, u32[]{:S(2)}) copy-start(s32[64,64]{1,0:T(8,128)} %len_ref.3) | copy-start | bytes 49156
  57.9 18.2 %copy-start = (bf16[512,128]{1,0:T(8,128)(2,1)S(1)}, bf16[512,128]{1,0:T(8,128)(2,1)}, u32[]{:S(2)}) copy-start(bf16[512,128]{1,0:T(8,128)(2,1)} %get-tuple-element.23.pr_ref) | copy-start | bytes 393220
  57.9 18.2 %all-to-all-start.1 = ((bf16[4,1024,128]{2,1,0:T(8,128)(2,1)}), bf16[4,1024,128]{2,1,0:T(8,128)(2,1)S(1)}, u32[]{:S(2)}, u32[]{:S(2)}) async-start(bf16[4,1024,128]{2,1,0:T(8,128)(2,1)} %shard_map.109), calls=%async_computation.1 | async-start | bytes 2097152 | tf_op jit(solution)/shard_map/all_to_all | solution.py:235
  61.5 8.1 %collective-permute-start.2 = (bf16[512,128]{1,0:T(8,128)(2,1)S(1)}, bf16[512,128]{1,0:T(8,128)(2,1)S(1)}, u32[]{:S(2)}, u32[]{:S(2)}) collective-permute-start(bf16[512,128]{1,0:T(8,128)(2,1)S(1)} %get-tuple-element.20), channel_id=1, source_target_pairs={{0,2},{1,7},{2,4},{3,1},{4,6},{5,3},{6,0},{7,5},{8,10},{9,15},{10,... | collective-permute-start | bytes 393224 | tf_op jit(solution)/shard_map/ppermute | solution.py:227
  64.9 9.3 %collective-permute-start.4 = (bf16[512,128]{1,0:T(8,128)(2,1)S(1)}, bf16[512,128]{1,0:T(8,128)(2,1)S(1)}, u32[]{:S(2)}, u32[]{:S(2)}) collective-permute-start(bf16[512,128]{1,0:T(8,128)(2,1)S(1)} %get-tuple-element.21), channel_id=1, source_target_pairs={{0,4},{1,5},{2,6},{3,7},{4,0},{5,1},{6,2},{7,3},{8,12},{9,13},{10,... | collective-permute-start | bytes 393224 | tf_op jit(solution)/shard_map/ppermute | solution.py:231
  69.6 4.7 %collective-permute-start.3 = (bf16[512,128]{1,0:T(8,128)(2,1)S(1)}, bf16[512,128]{1,0:T(8,128)(2,1)S(1)}, u32[]{:S(2)}, u32[]{:S(2)}) collective-permute-start(bf16[512,128]{1,0:T(8,128)(2,1)S(1)} %collective-permute-done.2.r1_ref), channel_id=1, source_target_pairs={{0,1},{1,0},{2,3},{3,2},{4,5},{5,4},{6,7},{7,6},{8,9},{9,8},{10,11... | collective-permute-start | bytes 393224 | tf_op jit(solution)/shard_map/ppermute | solution.py:223

commit v7 on v6

--- a/solution.py
+++ b/solution.py
@@ -308,7 +308,6 @@
         10**6,
         2 * 10**6,
     )
-    grads, following = lax.optimization_barrier((grads, following))
     near = all_to_all(grads, SQUARES)
     square = struct((PACKED, ROWS), bf16)
     take, same = call(

time: 105 us -> 106 us (level)
    ppermute x3, waiting for transfers between devices: 1.53 us -> 3.4 us  [swap_cores(): return lax.ppermute(a, 'mp', [(p, p ^ 1) for p in range(8)])]
    all_to_all x2, waiting for transfers between devices: 7.94 us -> 6.13 us  [all_to_all(): lax.all_to_all(a, 'dp', split_axis=0, concat_axis=0, tiled=True, axis_ind...]
  transfers between devices with their start and end apart: 7 -> 7, of which waited for: 4 -> 4; matrix products, arithmetic and copies ran while one was open for 2% -> 2% of each run, Pallas kernels for 10% -> 9%
where the time goes in v7:
time: 106 us; the launch traced here: 105 us
  blocking collectives  39.7 us (37%)
  starting transfers between devices  33.9 us (32%)
  Pallas kernels  16.2 us (15%)
  waiting for transfers between devices  11.6 us (11%)
  other arithmetic  1.61 us (2%)
  local copies, waits for them, and re-layouts  1.24 us (1%)
    all_to_all x1, blocking collectives, all_to_all(): lax.all_to_all(a, 'dp', split_axis=0, concat_axis=0, tiled=True, axis_ind...  26.6 us
    all_to_all x2, starting transfers between devices, all_to_all(): lax.all_to_all(a, 'dp', split_axis=0, concat_axis=0, tiled=True, axis_ind...  20.1 us
    pallas_call x9, Pallas kernels, call(): pl.pallas_call(body, out_shape=out_shape, in_specs=specs, out_specs=jax.t...  16.2 us
    all_gather x1, blocking collectives, per_device(): lax.all_gather(dv, 'mp', axis_index_groups=[[0, 2, 4, 6], [1, 3, 5, 7]])  13.1 us
    all_to_all x2, waiting for transfers between devices, all_to_all(): lax.all_to_all(a, 'dp', split_axis=0, concat_axis=0, tiled=True, axis_ind...  6.13 us
    ppermute x3, starting transfers between devices, swap_cores(): return lax.ppermute(a, 'mp', [(p, p ^ 1) for p in range(8)])  5.76 us
    ppermute x1, starting transfers between devices, to_far_chip(): return lax.ppermute(a, 'mp', [(p, (p + 4) % 8) for p in range(8)])  4.64 us
    ppermute x1, starting transfers between devices, to_next_chips(): lax.ppermute(a, 'mp', [(p, (p + (2, -2)[p % 2]) % 8) for p in range(8)])  3.41 us
  transfers between devices with their start and end apart: 7, of which 4 were waited for; matrix products, arithmetic and copies ran while one was open for 2% of the time, Pallas kernels for 9%

profile of v7, /device:TPU:16, one launch (start us, length us, event | category | flops | bytes accessed | tf_op | source)
XLA Modules:
  0.0 105.0 jit_solution(11656497195740727763)
XLA Ops:
  0.6 2.0 %shard_map.104 = bf16[64,72,128]{2,1,0:T(8,128)(2,1)} custom-call(bf16[16,512]{1,0:T(8,128)(2,1)} %wm_hbm.1, s32[1,64]{1,0:T(1,128)} %ok_ref.1, s32[1,64]{1,0:T(1,128)} %id_ref.1), custom_call_target="tpu_custom_call" | custom-call | flops 1000000 | bytes 1000000 | tf_op jit(solution)/shard_map/pallas_call | solution.py:43
  2.6 16.5 %all-to-all-start = ((bf16[64,72,128]{2,1,0:T(8,128)(2,1)}), bf16[64,72,128]{2,1,0:T(8,128)(2,1)S(1)}, u32[]{:S(2)}, u32[]{:S(2)}) async-start(bf16[64,72,128]{2,1,0:T(8,128)(2,1)} %shard_map.104), calls=%async_computation | async-start | bytes 2359296 | tf_op jit(solution)/shard_map/all_to_all | solution.py:235
  19.1 0.7 pad_add_fusion.where_ref
  19.8 0.0 copy-start.1
  19.8 0.0 copy-start.2
  19.8 0.0 copy-start.3
  19.8 0.0 copy-start.5
  19.8 5.9 %shard_map.105 = (bf16[512,128]{1,0:T(8,128)(2,1)}, bf16[512,128]{1,0:T(8,128)(2,1)}) custom-call(s32[3]{0:T(128)} %pad_add_fusion.where_ref, bf16[512,512]{1,0:T(8,128)(2,1)} %q_hbm.1, bf16[512,512]{1,0:T(8,128)(2,1)} %k_hbm.1, bf16[512,512]{1,0:T(8,128)(2,1)} %g_hbm.1, s32[64,64]{1,0:T(8,128)} %len_ref.3, s32[64,64]{1,0:T(8,128)} %plan_ref.3), custom_call_target="tpu_custom_call" | custom-call | flops 2000000000 | bytes 2000000 | tf_op jit(solution)/shard_map/pallas_call | solution.py:43
  25.7 1.9 %collective-permute-start = (bf16[512,128]{1,0:T(8,128)(2,1)}, bf16[512,128]{1,0:T(8,128)(2,1)S(1)}, u32[]{:S(2)}, u32[]{:S(2)}) collective-permute-start(bf16[512,128]{1,0:T(8,128)(2,1)} %get-tuple-element.13), channel_id=1, source_target_pairs={{0,1},{1,0},{2,3},{3,2},{4,5},{5,4},{6,7},{7,6},{8,9},{9,8},{10,11... | collective-permute-start | bytes 393224 | tf_op jit(solution)/shard_map/ppermute | solution.py:223
  27.6 1.5 %collective-permute-done = bf16[512,128]{1,0:T(8,128)(2,1)S(1)} collective-permute-done((bf16[512,128]{1,0:T(8,128)(2,1)}, bf16[512,128]{1,0:T(8,128)(2,1)S(1)}, u32[]{:S(2)}, u32[]{:S(2)}) %collective-permute-start) | collective-permute-done | bytes 131104 | tf_op jit(solution)/shard_map/ppermute | solution.py:223
  29.1 0.9 add_convert_fusion
  30.1 13.1 %all-gather = bf16[2048,128]{1,0:T(8,128)(2,1)S(1)} all-gather(bf16[512,128]{1,0:T(8,128)(2,1)S(1)} %add_convert_fusion), channel_id=2, replica_groups={{0,2,4,6},{1,3,5,7},{8,10,12,14},{9,11,13,15},{16,18,20,22},{17,19,21,2..., dimensions={0}, use_global_device_ids=true | all-gather | bytes 655360 | tf_op jit(solution)/shard_map/all_gather | solution.py:277
  43.2 0.0 copy-done.1
  43.2 0.0 copy-done.2
  43.2 0.0 copy-done.3
  43.2 0.0 copy-done.5
  43.2 0.0 copy-start.4
  43.3 1.2 %copy-done.4 = bf16[512,1024]{1,0:T(8,128)(2,1)S(1)} copy-done((bf16[512,1024]{1,0:T(8,128)(2,1)S(1)}, bf16[512,1024]{1,0:T(8,128)(2,1)}, u32[]{:S(2)}) %copy-start.4) | copy-done | bytes 1048600
  44.5 1.5 %shard_map.106 = (bf16[512,1024]{1,0:T(8,128)(2,1)S(1)}, bf16[512,640]{1,0:T(8,128)(2,1)S(1)}) custom-call(s32[3]{0:T(128)S(1)} %copy-done.1, bf16[512,1024]{1,0:T(8,128)(2,1)S(1)} %copy-done.4, s32[64,64]{1,0:T(8,128)S(1)} %copy-done.5, s32[1,64]{1,0:T(1,128)S(1)} %copy-done.2, s32[1,64]{1,0:T(1,128)S(1)} %copy-done.3, bf16[4,512,128]{2,1,0:T(8,128)(2,1)S(1)} %bitcast.4), custom_call_target="tpu_custom_call" | custom-call | flops 600000000 | bytes 4000000 | tf_op jit(solution)/shard_map/pallas_call | solution.py:43
  46.0 6.1 %all-to-all-done.w_ref = bf16[64,72,128]{2,1,0:T(8,128)(2,1)S(1)} async-done(((bf16[64,72,128]{2,1,0:T(8,128)(2,1)}), bf16[64,72,128]{2,1,0:T(8,128)(2,1)S(1)}, u32[]{:S(2)}, u32[]{:S(2)}) %all-to-all-start) | async-done | bytes 1179680 | tf_op jit(solution)/shard_map/all_to_all | solution.py:235
  52.1 1.3 %shard_map.107.mine_ref.after_ref = bf16[4,512,128]{2,1,0:T(8,128)(2,1)S(1)} custom-call(s32[3]{0:T(128)S(1)} %copy-done.1, bf16[64,72,128]{2,1,0:T(8,128)(2,1)S(1)} %all-to-all-done.w_ref, bf16[512,1024]{1,0:T(8,128)(2,1)S(1)} %get-tuple-element.14.xb_ref), custom_call_target="tpu_custom_call" | custom-call | flops 600000000 | bytes 3000000 | tf_op jit(solution)/shard_map/pallas_call | solution.py:43
  53.4 1.9 %shard_map.109 = bf16[4,1024,128]{2,1,0:T(8,128)(2,1)} custom-call(bf16[64,72,128]{2,1,0:T(8,128)(2,1)S(1)} %all-to-all-done.w_ref, bf16[512,1024]{1,0:T(8,128)(2,1)S(1)} %get-tuple-element.14.xb_ref, bf16[512,640]{1,0:T(8,128)(2,1)S(1)} %get-tuple-element.18.dv_ref, bf16[4,512,128]{2,1,0:T(8,128)(2,1)S(1)} %shard_map.107.mine_ref.after_ref), custom_call_target="tpu_custom_call" | custom-call | flops 600000000 | bytes 3000000 | tf_op jit(solution)/shard_map/pallas_call | solution.py:43
  55.3 0.0 copy-start.6
  55.3 0.0 copy-start
  55.3 3.6 %all-to-all-start.1 = ((bf16[4,1024,128]{2,1,0:T(8,128)(2,1)}), bf16[4,1024,128]{2,1,0:T(8,128)(2,1)S(1)}, u32[]{:S(2)}, u32[]{:S(2)}) async-start(bf16[4,1024,128]{2,1,0:T(8,128)(2,1)} %shard_map.109), calls=%async_computation.1 | async-start | bytes 2097152 | tf_op jit(solution)/shard_map/all_to_all | solution.py:235
  58.9 1.9 %collective-permute-start.1 = (bf16[4,512,128]{2,1,0:T(8,128)(2,1)S(1)}, bf16[4,512,128]{2,1,0:T(8,128)(2,1)S(1)}, u32[]{:S(2)}, u32[]{:S(2)}) collective-permute-start(bf16[4,512,128]{2,1,0:T(8,128)(2,1)S(1)} %shard_map.107.mine_ref.after_ref), channel_id=1, source_target_pairs={{0,1},{1,0},{2,3},{3,2},{4,5},{5,4},{6,7},{7,6},{8,9},{9,8},{10,11... | collective-permute-start | bytes 1572872 | tf_op jit(solution)/shard_map/ppermute | solution.py:223
  60.8 1.9 %collective-permute-done.1.other_ref = bf16[4,512,128]{2,1,0:T(8,128)(2,1)S(1)} collective-permute-done((bf16[4,512,128]{2,1,0:T(8,128)(2,1)S(1)}, bf16[4,512,128]{2,1,0:T(8,128)(2,1)S(1)}, u32[]{:S(2)}, u32[]{:S(2)}) %collective-permute-start.1) | collective-permute-done | bytes 524320 | tf_op jit(solution)/shard_map/ppermute | solution.py:223
  62.7 0.6 shard_map.108
  63.4 3.4 %collective-permute-start.2 = (bf16[512,128]{1,0:T(8,128)(2,1)S(1)}, bf16[512,128]{1,0:T(8,128)(2,1)S(1)}, u32[]{:S(2)}, u32[]{:S(2)}) collective-permute-start(bf16[512,128]{1,0:T(8,128)(2,1)S(1)} %get-tuple-element.16), channel_id=1, source_target_pairs={{0,2},{1,7},{2,4},{3,1},{4,6},{5,3},{6,0},{7,5},{8,10},{9,15},{10,... | collective-permute-start | bytes 393224 | tf_op jit(solution)/shard_map/ppermute | solution.py:227
  66.8 4.6 %collective-permute-start.4 = (bf16[512,128]{1,0:T(8,128)(2,1)S(1)}, bf16[512,128]{1,0:T(8,128)(2,1)S(1)}, u32[]{:S(2)}, u32[]{:S(2)}) collective-permute-start(bf16[512,128]{1,0:T(8,128)(2,1)S(1)} %get-tuple-element.17), channel_id=1, source_target_pairs={{0,4},{1,5},{2,6},{3,7},{4,0},{5,1},{6,2},{7,3},{8,12},{9,13},{10,... | collective-permute-start | bytes 393224 | tf_op jit(solution)/shard_map/ppermute | solution.py:231
  71.4 0.0 collective-permute-done.2.r1_ref
  71.4 1.9 %collective-permute-start.3 = (bf16[512,128]{1,0:T(8,128)(2,1)S(1)}, bf16[512,128]{1,0:T(8,128)(2,1)S(1)}, u32[]{:S(2)}, u32[]{:S(2)}) collective-permute-start(bf16[512,128]{1,0:T(8,128)(2,1)S(1)} %collective-permute-done.2.r1_ref), channel_id=1, source_target_pairs={{0,1},{1,0},{2,3},{3,2},{4,5},{5,4},{6,7},{7,6},{8,9},{9,8},{10,11... | collective-permute-start | bytes 393224 | tf_op jit(solution)/shard_map/ppermute | solution.py:223
  73.4 0.0 copy-done.6
  73.4 1.0 shard_map.110
  74.4 2.0 %collective-permute-done.4.r3_ref = bf16[512,128]{1,0:T(8,128)(2,1)S(1)} collective-permute-done((bf16[512,128]{1,0:T(8,128)(2,1)S(1)}, bf16[512,128]{1,0:T(8,128)(2,1)S(1)}, u32[]{:S(2)}, u32[]{:S(2)}) %collective-permute-start.4) | collective-permute-done | bytes 131104 | tf_op jit(solution)/shard_map/ppermute | solution.py:231
  76.4 0.0 collective-permute-done.3.r2_ref
  76.4 0.0 all-to-all-done.1.near_ref
  76.4 0.0 copy-done
  76.4 0.2 shard_map.111
  76.6 26.6 %all_to_all.15.got_ref = bf16[64,32,128]{2,1,0:T(8,128)(2,1)S(1)} all-to-all(bf16[64,32,128]{2,1,0:T(8,128)(2,1)S(1)} %shard_map.111), channel_id=1, replica_groups=mesh['dp'=64,'mp'=8] {'dp'}, dimensions={0} | all-to-all | bytes 1048576 | tf_op jit(solution)/shard_map/all_to_all | solution.py:235
  103.2 1.8 %shard_map.112 = (f32[16,512]{1,0:T(8,128)}, bf16[256,512]{1,0:T(8,128)(2,1)}) custom-call(bf16[64,32,128]{2,1,0:T(8,128)(2,1)S(1)} %all_to_all.15.got_ref, bf16[256,512]{1,0:T(8,128)(2,1)S(1)} %get-tuple-element.20.take_ref, bf16[256,512]{1,0:T(8,128)(2,1)S(1)} %get-tuple-element.21.same_ref), custom_call_target="tpu_custom_call" | custom-call | flops 600000000 | bytes 1000000 | tf_op jit(solution)/shard_map/pallas_call | solution.py:43
Async XLA Ops:
  2.6 49.5 %all-to-all-start = ((bf16[64,72,128]{2,1,0:T(8,128)(2,1)}), bf16[64,72,128]{2,1,0:T(8,128)(2,1)S(1)}, u32[]{:S(2)}, u32[]{:S(2)}) async-start(bf16[64,72,128]{2,1,0:T(8,128)(2,1)} %shard_map.104), calls=%async_computation | async-start | bytes 2359296 | tf_op jit(solution)/shard_map/all_to_all | solution.py:235
  19.8 23.4 %copy-start.1 = (s32[3]{0:T(128)S(1)}, s32[3]{0:T(128)}, u32[]{:S(2)}) copy-start(s32[3]{0:T(128)} %pad_add_fusion.where_ref) | copy-start | bytes 40
  19.8 23.4 %copy-start.2 = (s32[1,64]{1,0:T(1,128)S(1)}, s32[1,64]{1,0:T(1,128)}, u32[]{:S(2)}) copy-start(s32[1,64]{1,0:T(1,128)} %ok_ref.1) | copy-start | bytes 772
  19.8 23.4 %copy-start.3 = (s32[1,64]{1,0:T(1,128)S(1)}, s32[1,64]{1,0:T(1,128)}, u32[]{:S(2)}) copy-start(s32[1,64]{1,0:T(1,128)} %id_ref.1) | copy-start | bytes 772
  19.8 23.4 %copy-start.5 = (s32[64,64]{1,0:T(8,128)S(1)}, s32[64,64]{1,0:T(8,128)}, u32[]{:S(2)}) copy-start(s32[64,64]{1,0:T(8,128)} %plan_ref.3) | copy-start | bytes 49156
  25.7 3.5 %collective-permute-start = (bf16[512,128]{1,0:T(8,128)(2,1)}, bf16[512,128]{1,0:T(8,128)(2,1)S(1)}, u32[]{:S(2)}, u32[]{:S(2)}) collective-permute-start(bf16[512,128]{1,0:T(8,128)(2,1)} %get-tuple-element.13), channel_id=1, source_target_pairs={{0,1},{1,0},{2,3},{3,2},{4,5},{5,4},{6,7},{7,6},{8,9},{9,8},{10,11... | collective-permute-start | bytes 393224 | tf_op jit(solution)/shard_map/ppermute | solution.py:223
  43.2 1.2 %copy-start.4 = (bf16[512,1024]{1,0:T(8,128)(2,1)S(1)}, bf16[512,1024]{1,0:T(8,128)(2,1)}, u32[]{:S(2)}) copy-start(bf16[512,1024]{1,0:T(8,128)(2,1)} %x_ref.1) | copy-start | bytes 3145732
  55.3 18.1 %copy-start.6 = (s32[64,64]{1,0:T(8,128)S(1)}, s32[64,64]{1,0:T(8,128)}, u32[]{:S(2)}) copy-start(s32[64,64]{1,0:T(8,128)} %len_ref.3) | copy-start | bytes 49156
  55.3 21.1 %copy-start = (bf16[512,128]{1,0:T(8,128)(2,1)S(1)}, bf16[512,128]{1,0:T(8,128)(2,1)}, u32[]{:S(2)}) copy-start(bf16[512,128]{1,0:T(8,128)(2,1)} %get-tuple-element.19.pr_ref) | copy-start | bytes 393220
  55.3 21.1 %all-to-all-start.1 = ((bf16[4,1024,128]{2,1,0:T(8,128)(2,1)}), bf16[4,1024,128]{2,1,0:T(8,128)(2,1)S(1)}, u32[]{:S(2)}, u32[]{:S(2)}) async-start(bf16[4,1024,128]{2,1,0:T(8,128)(2,1)} %shard_map.109), calls=%async_computation.1 | async-start | bytes 2097152 | tf_op jit(solution)/shard_map/all_to_all | solution.py:235
  58.9 3.8 %collective-permute-start.1 = (bf16[4,512,128]{2,1,0:T(8,128)(2,1)S(1)}, bf16[4,512,128]{2,1,0:T(8,128)(2,1)S(1)}, u32[]{:S(2)}, u32[]{:S(2)}) collective-permute-start(bf16[4,512,128]{2,1,0:T(8,128)(2,1)S(1)} %shard_map.107.mine_ref.after_ref), channel_id=1, source_target_pairs={{0,1},{1,0},{2,3},{3,2},{4,5},{5,4},{6,7},{7,6},{8,9},{9,8},{10,11... | collective-permute-start | bytes 1572872 | tf_op jit(solution)/shard_map/ppermute | solution.py:223
  63.4 8.1 %collective-permute-start.2 = (bf16[512,128]{1,0:T(8,128)(2,1)S(1)}, bf16[512,128]{1,0:T(8,128)(2,1)S(1)}, u32[]{:S(2)}, u32[]{:S(2)}) collective-permute-start(bf16[512,128]{1,0:T(8,128)(2,1)S(1)} %get-tuple-element.16), channel_id=1, source_target_pairs={{0,2},{1,7},{2,4},{3,1},{4,6},{5,3},{6,0},{7,5},{8,10},{9,15},{10,... | collective-permute-start | bytes 393224 | tf_op jit(solution)/shard_map/ppermute | solution.py:227
  66.8 9.6 %collective-permute-start.4 = (bf16[512,128]{1,0:T(8,128)(2,1)S(1)}, bf16[512,128]{1,0:T(8,128)(2,1)S(1)}, u32[]{:S(2)}, u32[]{:S(2)}) collective-permute-start(bf16[512,128]{1,0:T(8,128)(2,1)S(1)} %get-tuple-element.17), channel_id=1, source_target_pairs={{0,4},{1,5},{2,6},{3,7},{4,0},{5,1},{6,2},{7,3},{8,12},{9,13},{10,... | collective-permute-start | bytes 393224 | tf_op jit(solution)/shard_map/ppermute | solution.py:231
  71.4 5.0 %collective-permute-start.3 = (bf16[512,128]{1,0:T(8,128)(2,1)S(1)}, bf16[512,128]{1,0:T(8,128)(2,1)S(1)}, u32[]{:S(2)}, u32[]{:S(2)}) collective-permute-start(bf16[512,128]{1,0:T(8,128)(2,1)S(1)} %collective-permute-done.2.r1_ref), channel_id=1, source_target_pairs={{0,1},{1,0},{2,3},{3,2},{4,5},{5,4},{6,7},{7,6},{8,9},{9,8},{10,11... | collective-permute-start | bytes 393224 | tf_op jit(solution)/shard_map/ppermute | solution.py:223
